TPU v7x, 32 devices: a whole 2x2x4 slice. The times are simulated.
32 devices in a mesh: section: 2 (over core), tp: 4 (over y, x), seq: 4 (over z).
Axes of the slice: x: 2, y: 2, z: 4, core: 2. Of those that a mesh axis runs over, the one named last changes fastest.
Arguments:
- layer_input: bfloat16 [4, 2, 2048, 768], P(None, None, 'seq'), may hold values from -6 to 6
- cotangent: bfloat16 [4, 2, 2048, 768], P(None, None, 'seq'), may hold values from -6 to 6
- doc_lengths: int32 [4, 2, 4], replicated, may hold values from 1 to 512, 1024 in all within a row
- ln1_gain: float32 [2, 768], P('section'), may hold values from 0.5 to 1.5
- w_qkv: bfloat16 [2, 768, 3, 768], P('section', None, None, 'tp'), may hold values from -0.21875 to 0.21875
- w_out: bfloat16 [2, 768, 768], P('section', 'tp'), may hold values from -0.625 to 0.625
- ln2_gain: float32 [2, 768], P('section'), may hold values from 0.5 to 1.5
- w_up: bfloat16 [2, 768, 3072], P('section', None, 'tp'), may hold values from -0.21875 to 0.21875
- b_up: float32 [2, 3072], P('section', 'tp'), may hold values from -3 to 3
- w_down: bfloat16 [2, 3072, 768], P('section', 'tp'), may hold values from -0.109375 to 0.109375
- b_down: float32 [2, 768], P('section'), may hold values from -2 to 2
Outputs:
- layer_out: bfloat16 [2, 4, 2, 2048, 768], P('section', None, None, 'seq')
- input_grad: bfloat16 [2, 4, 2, 2048, 768], P('section', None, None, 'seq')
- grad_ln1_gain: float32 [2, 768], P('section')
- grad_w_qkv: float32 [2, 768, 3, 768], P('section', None, None, 'tp')
- grad_w_out: float32 [2, 768, 768], P('section', 'tp')
- grad_ln2_gain: float32 [2, 768], P('section')
- grad_w_up: float32 [2, 768, 3072], P('section', None, 'tp')
- grad_b_up: float32 [2, 3072], P('section', 'tp')
- grad_w_down: float32 [2, 3072, 768], P('section', 'tp')
- grad_b_down: float32 [2, 768], P('section')
All inputs are finite; a program needn't handle non-finite values.
Results may differ from a plain program's by a relative error of at most 0.028.
Values may be sent and summed in bfloat16 or wider, within the bound.
A program may use at most 512 MiB of HBM per device.

v0:
```python
import jax
import jax.numpy as jnp
from jax import lax
from jax.experimental import pallas as pl
from jax.experimental.pallas import tpu as pltpu
from jax.sharding import PartitionSpec as P

HDIM = 64
BLOCK = 16
HALF = 1024


def from_behind(value, axis, by):
    size = lax.axis_size(axis)
    pairs = [(i, i + by) for i in range(size) if 0 <= i + by < size]
    return lax.ppermute(value, axis, pairs)


def layer_norm(values, gain):
    center = values - jnp.mean(values, axis=-1, keepdims=True)
    spread = jnp.mean(center * center, axis=-1, keepdims=True)
    return center * lax.rsqrt(spread + 1e-05) * gain


def rotate(values, cosine, sine_table):
    middle = values.shape[-1] // 2
    first_half = values[..., :middle]
    second_half = values[..., middle:]
    return jnp.concatenate(
        [
            first_half * cosine - second_half * sine_table,
            second_half * cosine + first_half * sine_table,
        ],
        axis=-1,
    )


def rotary_tables(positions):
    frequency = 10000.0 ** (-jnp.arange(HDIM // 2).astype(jnp.float32) * 2.0 / HDIM)
    angles = (positions % HALF).astype(jnp.float32)[:, None, None] * frequency[None, None, :]
    return (jnp.cos(angles), jnp.sin(angles))


def allowed(query_pos, query_doc, key_pos, key_doc):
    query_noisy = query_pos < HALF
    key_noisy = key_pos < HALF
    query_block = query_pos % HALF // BLOCK
    key_block = key_pos % HALF // BLOCK
    within = query_noisy & key_noisy & (query_block == key_block)
    earlier = query_noisy & ~key_noisy & (key_block < query_block)
    causal = ~query_noisy & ~key_noisy & (key_block <= query_block)
    return (within | earlier | causal) & (query_doc == key_doc)


def document_ids(doc_lengths):
    doc_ends = jnp.cumsum(doc_lengths, axis=-1)
    base_pos = jnp.arange(2 * HALF) % HALF
    return jnp.sum((base_pos[:, None] >= doc_ends[..., None, :]).astype(jnp.int32), axis=-1)


def gelu_tanh(values):
    return jax.nn.gelu(values, approximate=True)


def keep_slot(storage, value, slot_index, is_active):
    current = lax.dynamic_index_in_dim(storage, slot_index, 0, keepdims=False)
    return lax.dynamic_update_index_in_dim(
        storage, jnp.where(is_active, value, current), slot_index, 0
    )


def local_queries(inputs, ln_one, w_mix, tables):
    cosine, sine_table, query_pos = tables
    row_count, pos_count = (inputs.shape[0], inputs.shape[1])
    normed = layer_norm(inputs, ln_one).astype(jnp.bfloat16)
    mixed = jnp.einsum("rpd,dcf->rpcf", normed, w_mix, preferred_element_type=jnp.float32)
    shaped = mixed.reshape(row_count, pos_count, 3, -1, HDIM)
    queries = rotate(shaped[:, :, 0], cosine, sine_table).astype(jnp.bfloat16)
    keys_own = rotate(shaped[:, :, 1], cosine, sine_table).astype(jnp.bfloat16)
    values_own = shaped[:, :, 2].astype(jnp.bfloat16)
    return (normed, queries, keys_own, values_own)


def masked_scores(queries, keys_heads, query_pos, docs_all):
    pos_count = queries.shape[1]
    query_docs = lax.dynamic_slice_in_dim(docs_all, query_pos[0], pos_count, 1)
    key_pos = jnp.arange(keys_heads.shape[1])
    key_mask = allowed(
        query_pos[None, :, None],
        query_docs[:, :, None],
        key_pos[None, None, :],
        docs_all[:, None, :],
    )
    scores = (
        jnp.einsum("rqhd,rkhd->rhqk", queries, keys_heads, preferred_element_type=jnp.float32)
        * 0.125
    )
    return jnp.where(key_mask[:, None], scores, -1e30)


def forward_step(inputs, weights, tables, docs_all):
    ln_one, w_mix, w_proj, ln_two, w_first, b_first, w_second, b_second = weights
    row_count, pos_count = (inputs.shape[0], inputs.shape[1])
    normed, queries, keys_own, values_own = local_queries(inputs, ln_one, w_mix, tables)
    local_width = w_mix.shape[-1]
    keys_all, values_all = (
        lax.all_gather(
            keys_own.reshape(row_count, pos_count, local_width), "seq", axis=1, tiled=True
        ),
        lax.all_gather(
            values_own.reshape(row_count, pos_count, local_width), "seq", axis=1, tiled=True
        ),
    )
    keys_heads = keys_all.reshape(row_count, keys_all.shape[1], -1, HDIM)
    values_heads = values_all.reshape(row_count, values_all.shape[1], -1, HDIM)
    softmax_out = jax.nn.softmax(
        masked_scores(queries, keys_heads, tables[2], docs_all), axis=-1
    ).astype(jnp.bfloat16)
    attended = jnp.einsum(
        "rhqk,rkhd->rqhd", softmax_out, values_heads, preferred_element_type=jnp.float32
    )
    attended = attended.astype(jnp.bfloat16).reshape(row_count, pos_count, local_width)
    middle = inputs + lax.psum(
        jnp.einsum("rpe,ed->rpd", attended, w_proj, preferred_element_type=jnp.float32).astype(
            jnp.bfloat16
        ),
        "tp",
    ).astype(jnp.float32)
    normed_two = layer_norm(middle, ln_two).astype(jnp.bfloat16)
    hidden_pre = (
        jnp.einsum("rpd,df->rpf", normed_two, w_first, preferred_element_type=jnp.float32) + b_first
    )
    activated = gelu_tanh(hidden_pre).astype(jnp.bfloat16)
    second_terms = jnp.einsum(
        "rpf,fd->rpd", activated, w_second, preferred_element_type=jnp.float32
    )
    result = (
        middle + lax.psum(second_terms.astype(jnp.bfloat16), "tp").astype(jnp.float32) + b_second
    )
    return (result, middle, keys_all, values_all)


def backward_step(inputs, middle, grad_out, weights, tables, docs_all):
    ln_one, w_mix, w_proj, ln_two, w_first, b_first, w_second, b_second = weights
    cosine, sine_table, query_pos = tables
    row_count, pos_count = (inputs.shape[0], inputs.shape[1])
    local_width = w_mix.shape[-1]
    head_count = local_width // HDIM
    normed, queries, keys_own, values_own = local_queries(inputs, ln_one, w_mix, tables)
    keys_all, values_all = (
        lax.all_gather(
            keys_own.reshape(row_count, pos_count, local_width), "seq", axis=1, tiled=True
        ),
        lax.all_gather(
            values_own.reshape(row_count, pos_count, local_width), "seq", axis=1, tiled=True
        ),
    )
    keys_heads = keys_all.reshape(row_count, keys_all.shape[1], head_count, HDIM)
    values_heads = values_all.reshape(row_count, values_all.shape[1], head_count, HDIM)
    scores = masked_scores(queries, keys_heads, query_pos, docs_all)
    softmax_out = jax.nn.softmax(scores, axis=-1)
    probs_low = softmax_out.astype(jnp.bfloat16)
    attended = jnp.einsum(
        "rhqk,rkhd->rqhd", probs_low, values_heads, preferred_element_type=jnp.float32
    )
    attended = attended.astype(jnp.bfloat16).reshape(row_count, pos_count, local_width)
    normed_two = layer_norm(middle, ln_two).astype(jnp.bfloat16)
    hidden_pre = (
        jnp.einsum("rpd,df->rpf", normed_two, w_first, preferred_element_type=jnp.float32) + b_first
    )
    activated = gelu_tanh(hidden_pre).astype(jnp.bfloat16)
    grad_low = grad_out.astype(jnp.bfloat16)
    grad_b_second = jnp.sum(grad_out, axis=(0, 1))
    grad_w_second = jnp.einsum(
        "rpf,rpd->fd", activated, grad_low, preferred_element_type=jnp.float32
    )
    grad_act = jnp.einsum("rpd,fd->rpf", grad_low, w_second, preferred_element_type=jnp.float32)
    unused_value, gelu_back = jax.vjp(gelu_tanh, hidden_pre)
    grad_pre = gelu_back(grad_act)[0].astype(jnp.bfloat16)
    grad_b_first = jnp.sum(grad_pre, axis=(0, 1), dtype=jnp.float32)
    grad_w_first = jnp.einsum(
        "rpd,rpf->df", normed_two, grad_pre, preferred_element_type=jnp.float32
    )
    grad_normed_two = lax.psum(
        jnp.einsum("rpf,df->rpd", grad_pre, w_first, preferred_element_type=jnp.float32).astype(
            jnp.bfloat16
        ),
        "tp",
    ).astype(jnp.float32)
    unused_norm, second_back = jax.vjp(layer_norm, middle, ln_two)
    grad_middle_norm, grad_ln_two = second_back(grad_normed_two)
    grad_middle = grad_out + grad_middle_norm
    middle_low = grad_middle.astype(jnp.bfloat16)
    grad_w_proj = jnp.einsum(
        "rpe,rpd->ed", attended, middle_low, preferred_element_type=jnp.float32
    )
    grad_att = jnp.einsum("rpd,ed->rpe", middle_low, w_proj, preferred_element_type=jnp.float32)
    grad_att = grad_att.astype(jnp.bfloat16).reshape(row_count, pos_count, head_count, HDIM)
    grad_probs = jnp.einsum(
        "rqhd,rkhd->rhqk", grad_att, values_heads, preferred_element_type=jnp.float32
    )
    row_delta = jnp.sum(grad_probs * softmax_out, axis=-1, keepdims=True)
    grad_scores = (softmax_out * (grad_probs - row_delta)).astype(jnp.bfloat16)
    grad_queries = (
        jnp.einsum("rhqk,rkhd->rqhd", grad_scores, keys_heads, preferred_element_type=jnp.float32)
        * 0.125
    )
    full_len = keys_all.shape[1]
    part_keys = (
        jnp.einsum("rhqk,rqhd->rkhd", grad_scores, queries, preferred_element_type=jnp.float32)
        * 0.125
    )
    part_values = jnp.einsum(
        "rhqk,rqhd->rkhd", probs_low, grad_att, preferred_element_type=jnp.float32
    )
    grad_keys, grad_values = (
        lax.psum_scatter(
            part_keys.reshape(row_count, full_len, local_width).astype(jnp.bfloat16),
            "seq",
            scatter_dimension=1,
            tiled=True,
        ).astype(jnp.float32),
        lax.psum_scatter(
            part_values.reshape(row_count, full_len, local_width).astype(jnp.bfloat16),
            "seq",
            scatter_dimension=1,
            tiled=True,
        ).astype(jnp.float32),
    )
    grad_query_raw = rotate(grad_queries.astype(jnp.bfloat16), cosine, -sine_table)
    grad_key_raw = rotate(
        grad_keys.astype(jnp.bfloat16).reshape(row_count, pos_count, head_count, HDIM),
        cosine,
        -sine_table,
    )
    grad_mixed = jnp.stack(
        [
            grad_query_raw.reshape(row_count, pos_count, local_width).astype(jnp.bfloat16),
            grad_key_raw.reshape(row_count, pos_count, local_width).astype(jnp.bfloat16),
            grad_values.astype(jnp.bfloat16),
        ],
        axis=2,
    )
    grad_w_mix = jnp.einsum("rpd,rpcf->dcf", normed, grad_mixed, preferred_element_type=jnp.float32)
    grad_normed = lax.psum(
        jnp.einsum("rpcf,dcf->rpd", grad_mixed, w_mix, preferred_element_type=jnp.float32).astype(
            jnp.bfloat16
        ),
        "tp",
    ).astype(jnp.float32)
    unused_first, first_back = jax.vjp(layer_norm, inputs, ln_one)
    grad_in_norm, grad_ln_one = first_back(grad_normed)
    grad_inputs = grad_middle + grad_in_norm
    return (
        grad_inputs,
        (
            grad_ln_one,
            grad_w_mix,
            grad_w_proj,
            grad_ln_two,
            grad_w_first,
            grad_b_first,
            grad_w_second,
            grad_b_second,
        ),
    )


def pipelined(
    layer_input,
    cotangent,
    doc_lengths,
    ln1_gain,
    w_qkv,
    w_out,
    ln2_gain,
    w_up,
    b_up,
    w_down,
    b_down,
):
    weights = tuple(
        (weight[0] for weight in (ln1_gain, w_qkv, w_out, ln2_gain, w_up, b_up, w_down, b_down))
    )
    micros, row_count, pos_count, width_model = layer_input.shape
    sections = lax.axis_size("section")
    section_index = lax.axis_index("section")
    first_pos = lax.axis_index("seq") * pos_count
    query_pos = first_pos + jnp.arange(pos_count)
    cosine, sine_table = rotary_tables(query_pos)
    tables = (cosine, sine_table, query_pos)
    docs_every = document_ids(doc_lengths)
    kept_inputs = jnp.zeros((micros, row_count, pos_count, width_model), jnp.float32)
    kept_middle = jnp.zeros((micros, row_count, pos_count, width_model), jnp.float32)
    layer_out = jnp.zeros(layer_input.shape, jnp.bfloat16)
    arrived = jnp.zeros((row_count, pos_count, width_model), jnp.bfloat16)
    moments = micros + sections - 1
    for moment in range(moments):
        offset = moment - section_index
        micro_index = jnp.clip(offset, 0, micros - 1)
        is_active = (offset >= 0) & (offset < micros)
        own_input = layer_input[min(moment, micros - 1)]
        inputs = jnp.where(section_index == 0, own_input, arrived).astype(jnp.float32)
        result, middle, keys_all, values_all = forward_step(
            inputs, weights, tables, docs_every[micro_index]
        )
        kept_inputs = keep_slot(kept_inputs, inputs, micro_index, is_active)
        kept_middle = keep_slot(kept_middle, middle, micro_index, is_active)
        result_low = result.astype(jnp.bfloat16)
        layer_out = keep_slot(layer_out, result_low, micro_index, is_active)
        if moment < moments - 1:
            arrived = from_behind(result_low, "section", 1)
    grad_totals = tuple((jnp.zeros(weight.shape, jnp.float32) for weight in weights))
    input_grad = jnp.zeros(layer_input.shape, jnp.bfloat16)
    returned = jnp.zeros((row_count, pos_count, width_model), jnp.bfloat16)
    for moment in range(moments):
        offset = moment - (sections - 1 - section_index)
        micro_index = jnp.clip(offset, 0, micros - 1)
        is_active = (offset >= 0) & (offset < micros)
        incoming = jnp.where(
            section_index == sections - 1, cotangent[min(moment, micros - 1)], returned
        ).astype(jnp.float32)
        incoming = jnp.where(is_active, incoming, 0.0)
        grad_inputs, grad_parts = backward_step(
            kept_inputs[micro_index],
            kept_middle[micro_index],
            incoming,
            weights,
            tables,
            docs_every[micro_index],
        )
        grad_totals = tuple((total + piece for total, piece in zip(grad_totals, grad_parts)))
        grad_sent = grad_inputs.astype(jnp.bfloat16)
        input_grad = keep_slot(input_grad, grad_sent, micro_index, is_active)
        if moment < moments - 1:
            returned = from_behind(grad_sent, "section", -1)
    (
        grad_ln_one,
        grad_w_mix,
        grad_w_proj,
        grad_ln_two,
        grad_w_first,
        grad_b_first,
        grad_w_second,
        grad_b_second,
    ) = grad_totals
    summed = (
        lax.psum(grad_ln_one.astype(jnp.bfloat16), "seq").astype(jnp.float32),
        lax.psum(grad_w_mix.astype(jnp.bfloat16), "seq").astype(jnp.float32),
        lax.psum(grad_w_proj.astype(jnp.bfloat16), "seq").astype(jnp.float32),
        lax.psum(grad_ln_two.astype(jnp.bfloat16), "seq").astype(jnp.float32),
        lax.psum(grad_w_first.astype(jnp.bfloat16), "seq").astype(jnp.float32),
        lax.psum(grad_b_first.astype(jnp.bfloat16), "seq").astype(jnp.float32),
        lax.psum(grad_w_second.astype(jnp.bfloat16), "seq").astype(jnp.float32),
        lax.psum(grad_b_second.astype(jnp.bfloat16), "seq").astype(jnp.float32),
    )
    return (
        layer_out[None],
        input_grad[None],
        summed[0][None],
        summed[1][None],
        summed[2][None],
        summed[3][None],
        summed[4][None],
        summed[5][None],
        summed[6][None],
        summed[7][None],
    )


PIECE = 256
LANES = 256
MESH = pl.DeviceIdType.MESH
HBM = pl.BlockSpec(memory_space=pl.ANY)
VMEM = pl.BlockSpec(memory_space=pltpu.VMEM)


def dot_nn(left, right):
    return lax.dot_general(left, right, (((1,), (0,)), ((), ())), preferred_element_type=jnp.float32)


def dot_nt(left, right):
    return lax.dot_general(left, right, (((1,), (1,)), ((), ())), preferred_element_type=jnp.float32)


def dot_tn(left, right):
    return lax.dot_general(left, right, (((0,), (0,)), ((), ())), preferred_element_type=jnp.float32)


class Place:
    def __init__(self):
        self.s, self.t, self.z = (lax.axis_index(name) for name in ("section", "tp", "seq"))
        self.core = 1 - self.s
        self.half, self.group = self.z % 2, self.z // 2
        beside_x = self.t + 1 - 2 * (self.t % 2)
        beside_y = (self.t + 2) % 4
        self.beside_x, self.beside_y = beside_x, beside_y
        self.hop_one = beside_x * (1 - self.s) + beside_y * self.s
        self.hop_two = beside_y * (1 - self.s) + beside_x * self.s
        self.rel_one, self.rel_two = 1 + self.s, 2 - self.s
        self.far = (self.z + 2) % 4
        self.twin = self.z + 1 - 2 * self.half

    def on(self, section=None, tp=None, seq=None):
        return (
            self.s if section is None else section,
            self.t if tp is None else tp,
            self.z if seq is None else seq,
        )

    def partners(self):
        return [
            self.on(section=self.core),
            self.on(tp=self.beside_x),
            self.on(tp=self.beside_y),
            self.on(seq=self.far),
            self.on(seq=self.twin),
            self.on(seq=3 - self.z),
            self.on(section=self.core, seq=self.twin),
        ]

    def meet(self, partners):
        barrier = pltpu.get_barrier_semaphore()
        for partner in partners:
            pl.semaphore_signal(barrier, inc=1, device_id=partner, device_id_type=MESH)
        pl.semaphore_wait(barrier, len(partners))


def remote(source, target, send, receive, device):
    return pltpu.make_async_remote_copy(
        src_ref=source,
        dst_ref=target,
        send_sem=send,
        recv_sem=receive,
        device_id=device,
        device_id_type=MESH,
    )


def normalize(values):
    center = values - jnp.mean(values, axis=-1, keepdims=True)
    spread = jnp.mean(center * center, axis=-1, keepdims=True)
    scale = lax.rsqrt(spread + 1e-05)
    return center * scale, scale


def turn(values, cosine, sine_table):
    width = values.shape[-1]
    times = width // cosine.shape[-1]
    lane = lax.broadcasted_iota(jnp.int32, values.shape, 1) % HDIM
    ahead = pltpu.roll(values, width - HDIM // 2, 1)
    behind = pltpu.roll(values, HDIM // 2, 1)
    swapped = jnp.where(lane < HDIM // 2, ahead, behind)
    return values * jnp.tile(cosine, (1, times)) + swapped * jnp.tile(sine_table, (1, times))


def gelu(values):
    inner = 0.7978845608028654 * (values + 0.044715 * values * values * values)
    return 0.5 * values * (1.0 + jnp.tanh(inner))


def head_mask(head, scale):
    lane = lax.broadcasted_iota(jnp.int32, (1, LANES), 1)
    inside = (lane >= head * HDIM) & (lane < (head + 1) * HDIM)
    return jnp.where(inside, jnp.float32(scale), jnp.float32(0.0))


def attention_block(q_ref, keys, values_turned, bias, lse, turned):
    def one(head, _):
        rows = pl.ds(pl.multiple_of(head * HDIM, HDIM), HDIM)
        query = q_ref[...] * head_mask(head, 0.125).astype(jnp.bfloat16)
        scores = dot_nt(keys[...], query) + bias[...].astype(jnp.float32)
        top = jnp.max(scores, axis=0, keepdims=True)
        raised = jnp.exp(scores - top)
        total = jnp.sum(raised, axis=0, keepdims=True)
        lse[pl.ds(head, 1), :] = top + jnp.log(total)
        turned[rows, :] = dot_nn(values_turned[rows, :], raised.astype(jnp.bfloat16)) * (1.0 / total)
        return 0

    lax.fori_loop(0, LANES // HDIM, one, 0)
    return turned[...].T.astype(jnp.bfloat16)


class Weights:
    def __init__(self, place, own, full, sems):
        self.place, self.own, self.full = place, own, full
        (
            self.local,
            self.own_send,
            self.own_recv,
            self.hop_send,
            self.hop_recv,
            self.chip_send,
            self.chip_recv,
        ) = sems

    def source(self, chunk, pack):
        if chunk == 0:
            return self.own[0].at[pack]
        if chunk == 3:
            return self.own[2].at[pack]
        return self.own[1].at[pack, chunk - 1]

    def piece(self, layer, chunk, pack, rel):
        if chunk == 0:
            return self.full[0].at[layer, pack, :, pl.ds(pl.multiple_of(rel * 192, 64), 192)]
        if chunk == 3:
            return self.full[2].at[layer, pack, rel]
        return self.full[1].at[layer, pack, rel * 2 + chunk - 1]

    def own_copies(self, chunk, pack):
        s = self.place.s
        here = pltpu.make_async_copy(
            self.source(chunk, pack), self.piece(s, chunk, pack, 0), self.local.at[chunk, pack]
        )
        there = remote(
            self.source(chunk, pack),
            self.piece(s, chunk, pack, 0),
            self.own_send.at[chunk, pack],
            self.own_recv.at[chunk, pack],
            self.place.on(section=self.place.core),
        )
        return here, there

    def start_own(self, chunk):
        for pack in range(2):
            for copy in self.own_copies(chunk, pack):
                copy.start()

    def wait_own(self, layer, chunk):
        for pack in range(2):
            here, there = self.own_copies(chunk, pack)

            @pl.when(self.place.s == layer)
            def _():
                here.wait()

            @pl.when(self.place.s != layer)
            def _():
                there.wait_recv()

    def hops(self, layer, chunk):
        place = self.place
        own = self.piece(layer, chunk, place.s, 0)
        first = self.piece(layer, chunk, place.s, place.rel_one)
        second = self.piece(layer, chunk, place.s, place.rel_two)
        third = self.piece(layer, chunk, place.s, 3)
        moves = ((own, first, place.hop_one), (own, second, place.hop_two), (first, third, place.hop_two))
        return [
            remote(
                source,
                target,
                self.hop_send.at[layer, chunk, i],
                self.hop_recv.at[layer, chunk, i],
                place.on(tp=column),
            )
            for i, (source, target, column) in enumerate(moves)
        ]

    def chips(self, layer, chunk):
        place = self.place
        return [
            remote(
                self.piece(layer, chunk, place.s, rel),
                self.piece(layer, chunk, place.s, rel),
                self.chip_send.at[layer, chunk, i],
                self.chip_recv.at[layer, chunk, i],
                place.on(section=place.core),
            )
            for i, rel in enumerate((place.rel_one, place.rel_two, 3))
        ]

    def begin(self, layer, chunk):
        self.wait_own(layer, chunk)
        first, second, _ = self.hops(layer, chunk)
        first.start()
        second.start()

    def forward(self, layer, chunk):
        first, second, third = self.hops(layer, chunk)
        chips = self.chips(layer, chunk)
        first.wait_recv()
        third.start()
        chips[0].start()
        second.wait_recv()
        chips[1].start()

    def finish(self, layer, chunk):
        self.hops(layer, chunk)[2].wait_recv()
        self.chips(layer, chunk)[2].start()

    def need(self, layer, chunk):
        for copy in self.chips(layer, chunk):
            copy.wait_recv()

    def drain(self):
        for chunk in range(4):
            for pack in range(2):
                self.own_copies(chunk, pack)[1].wait_send()
            for layer in range(2):
                for copy in self.hops(layer, chunk) + self.chips(layer, chunk):
                    copy.wait_send()


class KeyShare:
    def __init__(self, place, kv, layer, sems):
        self.place, self.kv, self.layer = place, kv, layer
        self.near_send, self.near_recv, self.far_send, self.far_recv = sems
        s, odd = place.s, place.half == 1
        self.sends_near = (s == 0) | ~odd
        self.sends_far = (s == 0) & ~odd
        self.passes = (s == 0) & odd
        self.gets_near = (s == 1) | odd
        self.gets_far = odd

    def rows(self, start, part):
        lanes = pl.ds(part * LANES, LANES)
        return self.kv.at[self.layer, :, pl.ds(start, PIECE), lanes]

    def near(self, part):
        place = self.place
        return remote(
            self.rows(2 * PIECE, part),
            self.rows(PIECE, part),
            self.near_send.at[self.layer, part],
            self.near_recv.at[self.layer, part],
            place.on(section=place.core, seq=place.z + place.s * (1 - place.half)),
        )

    def far(self, part):
        place = self.place
        return remote(
            self.rows(2 * PIECE, part),
            self.rows(0, part),
            self.far_send.at[self.layer, part],
            self.far_recv.at[self.layer, part],
            place.on(seq=place.twin),
        )

    def last(self, part):
        place = self.place
        return remote(
            self.rows(PIECE, part),
            self.rows(0, part),
            self.far_send.at[self.layer, part],
            self.far_recv.at[self.layer, part],
            place.on(section=place.core),
        )

    def start(self, part):
        @pl.when(self.sends_near)
        def _():
            self.near(part).start()

        @pl.when(self.sends_far)
        def _():
            self.far(part).start()

    def arrive(self, part):
        @pl.when(self.gets_near)
        def _():
            self.near(part).wait_recv()

        @pl.when(self.passes)
        def _():
            self.last(part).start()

        @pl.when(self.gets_far)
        def _():
            self.far(part).wait_recv()

    def drain(self):
        for part in range(3):

            @pl.when(self.sends_near)
            def _():
                self.near(part).wait_send()

            @pl.when(self.sends_far)
            def _():
                self.far(part).wait_send()

            @pl.when(self.passes)
            def _():
                self.last(part).wait_send()


def forward_kernel(
    tokens,
    cotangent,
    own_a,
    own_b,
    own_c,
    bias,
    cosine,
    sine_table,
    full_a_out,
    full_b_out,
    gains_out,
    seeded_out,
    x_out,
    low_out,
    q_out,
    kv_out,
    att_out,
    mid_out,
    hid_out,
    lse_out,
    full_a,
    full_b,
    full_c,
    low,
    x,
    normed,
    q,
    kv,
    att,
    mid,
    hid,
    lse,
    values_turned,
    turned_att,
    *sems,
):
    weight_sems, key_sems = sems[:7], sems[7:11]
    token_sem, swap_send, swap_recv, seed_sem, seed_send, seed_recv, save_sem = sems[11:]
    place = Place()
    weights = Weights(place, (own_a, own_b, own_c), (full_a, full_b, full_c), weight_sems)
    lse[...] = jnp.zeros_like(lse)
    kv[:, :, : 2 * PIECE, :] = jnp.zeros((2, 2, 2 * PIECE, kv.shape[-1]), jnp.bfloat16)
    place.meet(place.partners())
    group_rows = pl.ds(pl.multiple_of(place.group * PIECE, PIECE), PIECE)
    columns = pl.ds(pl.multiple_of(place.s * PIECE, PIECE), PIECE)

    def bring(whole, target, here, send, receive):
        kept = whole.at[4 * place.group + place.t, columns]
        sent = whole.at[4 * (1 - place.group) + place.t, columns]
        target = target.at[group_rows]
        return (
            pltpu.make_async_copy(kept, target, here),
            remote(sent, target, send, receive, place.on(seq=place.far)),
        )

    own_tokens, swap = bring(tokens, low, token_sem, swap_send, swap_recv)
    own_seed, seed_swap = bring(cotangent, seeded_out, seed_sem, seed_send, seed_recv)
    own_tokens.start()
    swap.start()
    for chunk in (3, 0, 1, 2):
        weights.start_own(chunk)
    weights.begin(0, 0)
    weights.begin(0, 1)
    weights.begin(0, 3)
    weights.begin(1, 3)
    gains = full_c.at[:, 0, 0]
    gains_out[...] = full_c[:, 0, 0]
    own_tokens.wait()
    swap.wait()
    x_save = pltpu.make_async_copy(low, x_out, save_sem.at[16])
    x_save.start()
    x[...] = low[...].astype(jnp.float32)

    def saves(layer):
        pairs = [
            (low, low_out.at[layer]),
            (q, q_out.at[layer]),
            (kv.at[layer], kv_out.at[layer]),
            (att, att_out.at[layer]),
            (mid, mid_out.at[layer]),
            (hid, hid_out.at[layer]),
            (lse, lse_out.at[layer]),
        ]
        return [pltpu.make_async_copy(a, b, save_sem.at[i]) for i, (a, b) in enumerate(pairs)]

    def weight_saves(layer):
        copies = []
        for i, (a, b) in enumerate(((full_a, full_a_out), (full_b, full_b_out))):
            for pack in range(2):
                sem = save_sem.at[8 + 4 * layer + 2 * i + pack]
                copies.append(pltpu.make_async_copy(a.at[layer, pack], b.at[layer, pack], sem))
        return copies

    for layer in range(2):
        share = KeyShare(place, kv, layer, key_sems)
        unit, _ = normalize(x[...])
        normed[...] = (unit * gains[layer, 0:1]).astype(jnp.bfloat16)
        if layer == 0:
            weights.forward(0, 0)
            weights.begin(0, 2)
            weights.finish(0, 0)
        else:
            weights.forward(1, 0)
            weights.begin(1, 2)
            weights.finish(1, 0)
            for copy in saves(0)[1:]:
                copy.wait()
        weights.need(layer, 0)
        for copy in weight_saves(layer)[:2]:
            copy.start()
        for part in range(3):
            lanes = pl.ds(part * LANES, LANES)
            keep = normed[...]
            mixed = dot_nt(keep, full_a[layer, 0, 0, lanes, :])
            q[:, lanes] = turn(mixed, cosine[...], sine_table[...]).astype(jnp.bfloat16)
            mixed = dot_nt(keep, full_a[layer, 0, 1, lanes, :])
            mixed = turn(mixed, cosine[...], sine_table[...]).astype(jnp.bfloat16)
            kv[layer, 0, 2 * PIECE : 3 * PIECE, lanes] = mixed[PIECE:]
            kv[layer, 0, 3 * PIECE :, lanes] = mixed[:PIECE]
            mixed = dot_nt(keep, full_a[layer, 1, 0, lanes, :]).astype(jnp.bfloat16)
            kv[layer, 1, 2 * PIECE : 3 * PIECE, lanes] = mixed[PIECE:]
            kv[layer, 1, 3 * PIECE :, lanes] = mixed[:PIECE]
            share.start(part)
        if layer == 0:
            weights.forward(0, 3)
            weights.forward(1, 3)
            weights.finish(0, 3)
            weights.finish(1, 3)
            own_seed.start()
            weights.forward(0, 1)
            weights.begin(1, 0)
        else:
            weights.forward(1, 1)
        for part in range(3):
            lanes = pl.ds(part * LANES, LANES)
            share.arrive(part)
            values_turned[...] = kv[layer, 1, :, lanes].astype(jnp.float32).T.astype(jnp.bfloat16)
            for start, count in ((0, 4 * PIECE), (PIECE, 3 * PIECE)):
                queries = pl.ds(start, PIECE)
                att[queries, lanes] = attention_block(
                    q.at[queries, lanes],
                    kv.at[layer, 0, :count, lanes],
                    values_turned.at[:, :count],
                    bias.at[:count, queries],
                    lse.at[pl.ds(8 * part, 8), queries],
                    turned_att,
                )
            if part == 2 and layer == 0:
                seed_swap.start()
            if part == 0:
                weights.finish(layer, 1)
            elif part == 1:
                weights.forward(layer, 2)
                if layer == 0:
                    weights.begin(1, 1)
            else:
                weights.finish(layer, 2)
        for copy in saves(layer)[1:4] + saves(layer)[6:]:
            copy.start()

        def project(part, _):
            lanes = pl.ds(pl.multiple_of(part * LANES, LANES), LANES)
            mid[:, lanes] = x[:, lanes] + dot_nn(att[...], full_a[layer, 1, 1, :, lanes])
            return 0

        lax.fori_loop(0, 3, project, 0)
        unit, _ = normalize(mid[...])
        normed[...] = (unit * gains[layer, 1:2]).astype(jnp.bfloat16)
        x[...] = mid[...] + gains[layer, 2:3]
        saves(layer)[4].start()
        weights.need(layer, 3)
        for part in range(2):
            weights.need(layer, part + 1)
            if part == 1:
                for copy in weight_saves(layer)[2:]:
                    copy.start()

            def feed(rel, _):
                start = pl.multiple_of(rel * 768 + part * 384, 128)
                units = pl.ds(start, 384)
                shift = full_c[layer, 1, rel, 0:1, pl.ds(part * 384, 384)]
                tile = rel * 2 + part
                pre = dot_nn(normed[...], full_b[layer, 0, tile]) + shift
                hid[:, units] = pre.astype(jnp.bfloat16)
                active = gelu(pre).astype(jnp.bfloat16)
                x[...] += dot_nt(active, full_b[layer, 1, tile])
                return 0

            lax.fori_loop(0, 4, feed, 0)
        saves(layer)[5].start()
        if layer == 0:
            x_save.wait()
        else:
            saves(0)[0].wait()
        low[...] = x[...].astype(jnp.bfloat16)
        saves(layer)[0].start()
        x[...] = low[...].astype(jnp.float32)
    for copy in saves(1):
        copy.wait()
    for layer in range(2):
        for copy in weight_saves(layer):
            copy.wait()
        KeyShare(place, kv, layer, key_sems).drain()
    weights.drain()
    own_seed.wait()
    seed_swap.wait()


def run_forward(tokens, cotangent, own_a, own_b, own_c, bias, cosine, sine_table):
    shape = jax.ShapeDtypeStruct
    low_type, full_type = jnp.bfloat16, jnp.float32
    count = 2 * PIECE
    width = tokens.shape[-1]
    units = 8 * own_b.shape[-1]
    dma = pltpu.SemaphoreType.DMA
    return pl.pallas_call(
        forward_kernel,
        name="forward_layers",
        out_shape=[
            shape((2, 2, 2, width, width), low_type),
            shape((2, 2, 8, width, units // 8), low_type),
            shape((2, 8, width), full_type),
            shape((count, width), low_type),
            shape((count, width), low_type),
            shape((2, count, width), low_type),
            shape((2, count, width), low_type),
            shape((2, 2, 4 * PIECE, width), low_type),
            shape((2, count, width), low_type),
            shape((2, count, width), full_type),
            shape((2, count, units), low_type),
            shape((2, 24, count), full_type),
        ],
        in_specs=[HBM] * 5 + [VMEM] * 3,
        out_specs=[HBM] * 2 + [VMEM] + [HBM] * 9,
        scratch_shapes=[
            pltpu.VMEM((2, 2, 2, width, width), low_type),
            pltpu.VMEM((2, 2, 8, width, units // 8), low_type),
            pltpu.VMEM((2, 2, 4, 8, width), full_type),
            pltpu.VMEM((count, width), low_type),
            pltpu.VMEM((count, width), full_type),
            pltpu.VMEM((count, width), low_type),
            pltpu.VMEM((count, width), low_type),
            pltpu.VMEM((2, 2, 4 * PIECE, width), low_type),
            pltpu.VMEM((count, width), low_type),
            pltpu.VMEM((count, width), full_type),
            pltpu.VMEM((count, units), low_type),
            pltpu.VMEM((24, count), full_type),
            pltpu.VMEM((LANES, 4 * PIECE), low_type),
            pltpu.VMEM((LANES, PIECE), full_type),
            dma((4, 2)),
            dma((4, 2)),
            dma((4, 2)),
            dma((2, 4, 3)),
            dma((2, 4, 3)),
            dma((2, 4, 3)),
            dma((2, 4, 3)),
            dma((2, 3)),
            dma((2, 3)),
            dma((2, 3)),
            dma((2, 3)),
            dma,
            dma,
            dma,
            dma,
            dma,
            dma,
            dma((17,)),
        ],
        compiler_params=pltpu.CompilerParams(
            collective_id=1, has_side_effects=True, vmem_limit_bytes=62 * 1024 * 1024
        ),
        cost_estimate=pl.CostEstimate(
            flops=30_000_000_000, bytes_accessed=80_000_000, transcendentals=20_000_000
        ),
    )(tokens, cotangent, own_a, own_b, own_c, bias, cosine, sine_table)


def low_sum(*parts):
    total = parts[0].astype(jnp.float32)
    for part in parts[1:]:
        total = total + part.astype(jnp.float32)
    return total.astype(jnp.bfloat16)


class Spread:
    def __init__(self, place, source, stage, layer, out, sems):
        self.place, self.source, self.stage = place, source, stage
        self.layer, self.out = layer, out
        self.local, self.swap_send, self.swap_recv, self.hop_send, self.hop_recv = sems[:5]
        self.end_local, self.end_send, self.end_recv = sems[5:]
        self.groups = (place.group, 1 - place.group)

    def entry(self):
        place = self.place
        kept = self.source.at[pl.ds(pl.multiple_of(place.group * PIECE, PIECE), PIECE)]
        sent = self.source.at[pl.ds(pl.multiple_of((1 - place.group) * PIECE, PIECE), PIECE)]
        target = self.stage.at[0, place.group]
        here = pltpu.make_async_copy(kept, target, self.local)
        there = remote(sent, target, self.swap_send, self.swap_recv, place.on(seq=place.far))
        return here, there

    def take(self):
        self.entry()[0].start()

    def swap(self):
        self.entry()[1].start()

    def moves(self, half):
        place, group = self.place, self.groups[half]
        own = self.stage.at[0, group]
        first = self.stage.at[place.rel_one, group]
        second = self.stage.at[place.rel_two, group]
        third = self.stage.at[3, group]
        listed = (
            (own, first, place.hop_one),
            (own, second, place.hop_two),
            (first, third, place.hop_two),
        )
        return [
            remote(
                source,
                target,
                self.hop_send.at[half, i],
                self.hop_recv.at[half, i],
                place.on(tp=column),
            )
            for i, (source, target, column) in enumerate(listed)
        ]

    def hops(self, half):
        here, there = self.entry()
        if half == 0:
            here.wait()
        else:
            there.wait_recv()
        first, second, _ = self.moves(half)
        first.start()
        second.start()
        self.put(half, 0)

    def forward(self, half):
        first, _, third = self.moves(half)
        first.wait_recv()
        third.start()
        self.put(half, 1)

    def finish(self, half):
        _, second, third = self.moves(half)
        second.wait_recv()
        self.put(half, 2)
        third.wait_recv()
        self.put(half, 3)

    def ends(self, half, step):
        place, group = self.place, self.groups[half]
        rows = pl.ds(pl.multiple_of(place.s * PIECE, PIECE), PIECE)
        rel = (0, place.rel_one, place.rel_two, 3)[step]
        column = (place.t, place.hop_one, place.hop_two, 3 - place.t)[step]
        source, target = self.stage.at[rel, group], self.out.at[group, column, rows]
        here = pltpu.make_async_copy(source, target, self.end_local.at[half, step])
        there = remote(
            source,
            target,
            self.end_send.at[half, step],
            self.end_recv.at[half, step],
            place.on(section=place.core),
        )
        return here, there

    def put(self, half, step):
        @pl.when(self.place.s == self.layer)
        def _():
            self.ends(half, step)[0].start()

        @pl.when(self.place.s != self.layer)
        def _():
            self.ends(half, step)[1].start()

    def drain(self):
        self.entry()[1].wait_send()
        for half in range(2):
            for copy in self.moves(half):
                copy.wait_send()

        @pl.when(self.place.s == self.layer)
        def _():
            for half in range(2):
                for step in range(4):
                    here, there = self.ends(half, step)
                    here.wait()
                    there.wait_recv()

        @pl.when(self.place.s != self.layer)
        def _():
            for half in range(2):
                for step in range(4):
                    self.ends(half, step)[1].wait_send()


def spread_sems():
    dma = pltpu.SemaphoreType.DMA
    return [dma, dma, dma, dma((2, 3)), dma((2, 3)), dma((2, 4)), dma((2, 4)), dma((2, 4))]


class Sum:
    def __init__(self, place, source, total, buffers, sems, loaded=False, opens=None, waits=None):
        self.place, self.source, self.total = place, source, total
        self.inbox, self.hop_in, self.line_in = buffers
        self.loaded, self.opens, self.waits = loaded, opens, waits
        (
            self.mine_sem,
            self.chip_send,
            self.chip_recv,
            self.hop_send,
            self.hop_recv,
            self.line_send,
            self.line_recv,
            self.end_local,
            self.end_send,
            self.end_recv,
        ) = sems
        z = place.z
        self.outer = (z == 0) | (z == 3)
        self.inner = (z == 1) | (z == 2)
        self.order = (3, 1, 2, 0)

    def mine(self, rel):
        return pltpu.make_async_copy(
            self.source(self.place.s, rel), self.total(rel), self.mine_sem.at[rel]
        )

    def other(self, rel):
        return remote(
            self.source(self.place.core, rel),
            self.inbox.at[rel],
            self.chip_send.at[rel],
            self.chip_recv.at[rel],
            self.place.on(section=self.place.core),
        )

    def start(self):
        if self.waits is not None:
            pl.semaphore_wait(self.waits, 1)
        for rel in self.order:
            if self.inbox is not None:
                self.other(rel).start()
            if self.loaded:
                self.mine(rel).start()

    def load(self, travels=True):
        for rel in self.order:
            if self.loaded:
                self.mine(rel).wait()
            if self.inbox is not None:
                self.other(rel).wait_recv()
                total = self.total(rel)
                total[...] = low_sum(total[...], self.inbox[rel])
            if travels and rel == 3:
                self.moves()[0].start()
            elif travels and rel == 2:
                self.moves()[1].start()
        if self.opens is not None:
            pl.semaphore_signal(
                self.opens,
                inc=1,
                device_id=self.place.on(section=self.place.core),
                device_id_type=MESH,
            )

    def moves(self):
        place = self.place
        listed = (
            (3, 0, place.hop_two),
            (place.rel_two, 1, place.hop_two),
            (place.rel_one, 2, place.hop_one),
        )
        return [
            remote(
                self.total(rel),
                self.hop_in.at[slot],
                self.hop_send.at[slot],
                self.hop_recv.at[slot],
                place.on(tp=column),
            )
            for rel, slot, column in listed
        ]

    def middle(self):
        first, _, third = self.moves()
        first.wait_recv()
        total = self.total(self.place.rel_one)
        total[...] = low_sum(total[...], self.hop_in[0])
        third.start()

    def lines(self):
        place = self.place
        own, line_sum = self.total(0), self.total(1)
        listed = (
            (own, self.line_in.at[0], place.twin),
            (own, self.line_in.at[1], 3 - place.z),
            (line_sum, line_sum, place.twin),
        )
        return [
            remote(
                source,
                target,
                self.line_send.at[i],
                self.line_recv.at[i],
                place.on(seq=plane),
            )
            for i, (source, target, plane) in enumerate(listed)
        ]

    def gather(self):
        _, second, third = self.moves()
        second.wait_recv()
        third.wait_recv()
        total = self.total(0)
        total[...] = low_sum(total[...], self.hop_in[1], self.hop_in[2])
        second.wait_send()
        third.wait_send()

        @pl.when(self.outer)
        def _():
            self.lines()[0].start()

    def line_one(self):
        @pl.when(self.inner)
        def _():
            self.lines()[0].wait_recv()
            total = self.total(0)
            total[...] = low_sum(total[...], self.line_in[0])
            self.lines()[1].start()

    def line_two(self):
        @pl.when(self.inner)
        def _():
            self.lines()[1].wait_recv()
            self.total(1)[...] = low_sum(self.total(0)[...], self.line_in[1])
            self.lines()[2].start()

    def line_three(self):
        @pl.when(self.outer)
        def _():
            self.lines()[2].wait_recv()

    def ends(self, target):
        here = pltpu.make_async_copy(self.total(1), target, self.end_local)
        there = remote(
            self.total(1),
            target,
            self.end_send,
            self.end_recv,
            self.place.on(section=self.place.core),
        )
        return here, there

    def finish(self, layer, target):
        self.line_three()
        here, there = self.ends(target)

        @pl.when(self.place.s == layer)
        def _():
            here.start()

        @pl.when(self.place.s != layer)
        def _():
            there.start()

    def drain_exchange(self):
        if self.inbox is not None:
            for rel in range(4):
                self.other(rel).wait_send()

    def drain(self, layer, target):
        here, there = self.ends(target)

        @pl.when(self.place.s == layer)
        def _():
            here.wait()
            there.wait_recv()

        @pl.when(self.place.s != layer)
        def _():
            there.wait_send()

        self.drain_exchange()
        self.moves()[0].wait_send()

        @pl.when(self.outer)
        def _():
            self.lines()[0].wait_send()

        @pl.when(self.inner)
        def _():
            self.lines()[1].wait_send()
            self.lines()[2].wait_send()


def sum_sems():
    dma = pltpu.SemaphoreType.DMA
    return [dma((4,))] * 3 + [dma((3,))] * 4 + [dma] * 3


SUM_SEMS = 10


def sum_buffers(piece, counts):
    return [pltpu.VMEM((count,) + piece, jnp.bfloat16) for count in counts]


def attention_sums(place, grads, buffers, sems):
    sums = []
    for i in range(2):
        total, inbox, hop_in, line_in = buffers[4 * i : 4 * i + 4]

        def source(pack, rel, i=i):
            return grads.at[pack, i, rel]

        def kept(rel, total=total):
            return total.at[rel]

        own_sems = sems[SUM_SEMS * i : SUM_SEMS * (i + 1)]
        sums.append(Sum(place, source, kept, (inbox, hop_in, line_in), own_sems, loaded=True))
    return sums


def feed_sums(place, wb, buffers, sems, gate):
    inbox, sums = buffers[0], []
    for i in range(2):

        def source(pack, rel, i=i):
            return wb.at[pack, rel * 2 + i]

        def kept(rel, i=i):
            return wb.at[place.s, rel * 2 + i]

        own_sems = sems[SUM_SEMS * i : SUM_SEMS * (i + 1)]
        gates = {"opens": gate} if i == 0 else {"waits": gate}
        at = min(i, buffers[1].shape[0] - 1)
        parts = (inbox, buffers[1].at[at], buffers[2].at[at])
        sums.append(Sum(place, source, kept, parts, own_sems, **gates))
    return sums


def feed_buffers(piece, count):
    kind = jnp.bfloat16
    return [
        pltpu.VMEM((4,) + piece, kind),
        pltpu.VMEM((count, 3) + piece, kind),
        pltpu.VMEM((count, 2) + piece, kind),
    ]


class KeyReturn:
    def __init__(self, place, kv, near_in, far_in, sems):
        self.place, self.kv = place, kv
        self.near_in, self.far_in, self.pass_in = near_in, far_in, far_in
        (
            self.near_send,
            self.near_recv,
            self.far_send,
            self.far_recv,
            self.pass_send,
            self.pass_recv,
        ) = sems
        s, odd = place.s, place.half == 1
        self.is_third = (s == 0) & odd
        self.is_fourth = (s == 1) & odd
        self.is_second = (s == 1) & ~odd
        self.is_first = (s == 0) & ~odd

    def sources(self, start, part):
        return self.kv.at[:, pl.ds(start, PIECE), pl.ds(part * LANES, LANES)]

    def copies(self, part):
        place = self.place
        lanes = pl.ds(part * LANES, LANES)
        near = remote(
            self.sources(PIECE, part),
            self.near_in.at[:, :, lanes],
            self.near_send.at[part],
            self.near_recv.at[part],
            place.on(section=place.core, seq=place.z - (1 - place.s) * place.half),
        )
        far = remote(
            self.sources(0, part),
            self.far_in.at[:, :, lanes],
            self.far_send.at[part],
            self.far_recv.at[part],
            place.on(seq=place.twin),
        )
        passed = remote(
            self.sources(0, part),
            self.pass_in.at[:, :, lanes],
            self.pass_send.at[part],
            self.pass_recv.at[part],
            place.on(section=place.core),
        )
        return near, far, passed

    def start(self, part):
        near, far, passed = self.copies(part)

        @pl.when(self.is_fourth)
        def _():
            passed.start()
            near.start()

        @pl.when(self.is_second)
        def _():
            near.start()

        @pl.when(self.is_third)
        def _():
            far.start()

    def relay(self, part):
        near, _, passed = self.copies(part)
        lanes = pl.ds(part * LANES, LANES)

        @pl.when(self.is_third)
        def _():
            passed.wait_recv()
            self.kv[:, PIECE : 2 * PIECE, lanes] = low_sum(
                self.kv[:, PIECE : 2 * PIECE, lanes], self.pass_in[:, :, lanes]
            )
            near.start()

    def collect(self, part):
        near, far, _ = self.copies(part)
        lanes = pl.ds(part * LANES, LANES)
        clean = pl.ds(2 * PIECE, PIECE)

        @pl.when(~self.is_fourth)
        def _():
            near.wait_recv()
            self.kv[:, clean, lanes] = low_sum(self.kv[:, clean, lanes], self.near_in[:, :, lanes])

        @pl.when(self.is_first)
        def _():
            far.wait_recv()
            self.kv[:, clean, lanes] = low_sum(self.kv[:, clean, lanes], self.far_in[:, :, lanes])

    def drain(self):
        for part in range(3):
            near, far, passed = self.copies(part)

            @pl.when(self.is_fourth)
            def _():
                passed.wait_send()
                near.wait_send()

            @pl.when(self.is_second)
            def _():
                near.wait_send()

            @pl.when(self.is_third)
            def _():
                far.wait_send()
                near.wait_send()


def normalize_back(grads, unit, scale, gain):
    lifted = grads * gain
    mean = jnp.mean(lifted, axis=-1, keepdims=True)
    along = jnp.mean(lifted * unit, axis=-1, keepdims=True)
    return scale * (lifted - mean - unit * along)


def attention_back(q_ref, grad_ref, att_ref, keys, values, keys_turned, bias, lse, sums, turned, count):
    turned[...] = (grad_ref[...].astype(jnp.float32) * att_ref[...].astype(jnp.float32)).T

    def one(head, _):
        rows = pl.ds(pl.multiple_of(head * HDIM, HDIM), HDIM)
        query = q_ref[...] * head_mask(head, 0.125).astype(jnp.bfloat16)
        grad = grad_ref[...] * head_mask(head, 1.0).astype(jnp.bfloat16)
        delta = jnp.sum(turned[rows, :], axis=0, keepdims=True)
        scores = dot_nt(keys[...], query) + bias[...].astype(jnp.float32)
        probs = jnp.exp(scores - lse[pl.ds(head, 1), :])
        grad_scores = (probs * (dot_nt(values[...], grad) - delta)).astype(jnp.bfloat16)
        sums[0, :count] += dot_nn(grad_scores, query)
        sums[1, :count] += dot_nn(probs.astype(jnp.bfloat16), grad)
        turned[rows, :] = dot_nn(keys_turned[rows, :], grad_scores) * 0.125
        return 0

    lax.fori_loop(0, LANES // HDIM, one, 0)
    q_ref[...] = turned[...].T.astype(jnp.bfloat16)


def backward_layer(layer, refs, place, tick, key_sems, sems, tile_sems):
    (
        full_a,
        full_b,
        grad_in,
        x_in,
        q_in,
        kv_in,
        att_in,
        mid_in,
        hid_in,
        lse_in,
        gains,
        bias,
        cosine,
        sine_table,
        grads_a,
        grad_out,
        small_out,
        wa,
        wb,
        low,
        q,
        kv,
        att,
        mid,
        hid,
        grad,
        gathered,
        grad_low,
        grad_att,
        near_in,
        far_in,
        sums,
        keys_turned,
        turned_q,
        grad_turned,
        normed_turned,
        lse,
    ) = refs
    share = KeyReturn(place, kv, near_in, far_in, key_sems)
    pairs = [
        (grad_in, grad_low),
        (mid_in.at[layer], mid),
        (hid_in.at[layer], hid),
        (full_a.at[layer], wa),
        (att_in.at[layer], att),
        (q_in.at[layer], q),
        (kv_in.at[layer], kv),
        (x_in, low),
        (lse_in.at[layer], lse),
    ]
    loads = [pltpu.make_async_copy(a, b, sems.at[i]) for i, (a, b) in enumerate(pairs)]
    def tile_copy(pack, tile):
        return pltpu.make_async_copy(
            full_b.at[layer, pack, tile], wb.at[pack, tile], tile_sems.at[pack, tile]
        )

    for copy in loads[:3]:
        copy.start()
    for part in range(2):
        for rel in range(4):
            for pack in (1, 0):
                tile_copy(pack, rel * 2 + part).start()
    for copy in loads[3:]:
        copy.start()
    tick()
    gain_one, gain_two = gains[layer, 0:1], gains[layer, 1:2]
    for copy in loads[:3]:
        copy.wait()
    small_out[...] = jnp.zeros_like(small_out)

    def by_rows(step):
        def one(i, _):
            step(pl.ds(pl.multiple_of(i * 128, 128), 128))
            return 0

        lax.fori_loop(0, grad.shape[0] // 128, one, 0)

    def enter(rows):
        incoming = grad_low[rows, :].astype(jnp.float32)
        grad[rows, :] = incoming
        small_out[2:3] += jnp.sum(incoming, axis=0, keepdims=True)
        grad_turned[:, rows] = incoming.T.astype(jnp.bfloat16)
        unit, _ = normalize(mid[rows, :])
        normed_turned[:, rows] = (unit * gain_two).T.astype(jnp.bfloat16)
        gathered[rows, :] = jnp.zeros((128, grad.shape[1]), jnp.float32)

    by_rows(enter)
    tick()

    def feed(part, rel):
        start = pl.multiple_of(rel * 768 + part * 384, 128)
        units = pl.ds(start, 384)
        tile = rel * 2 + part
        pre = hid[:, units].astype(jnp.float32)
        squared = pre * pre
        bent = jnp.tanh(0.7978845608028654 * pre * (1.0 + 0.044715 * squared))
        raised = 0.5 * (1.0 + bent)
        active = (pre * raised).astype(jnp.bfloat16)
        slope = raised + 0.5 * pre * (1.0 - bent * bent) * (
            0.7978845608028654 * (1.0 + 3 * 0.044715 * squared)
        )
        tile_copy(1, tile).wait()
        grad_act = dot_nn(grad_low[...], wb[1, tile])
        grad_pre = (grad_act * slope).astype(jnp.bfloat16)
        total = jnp.sum(grad_pre.astype(jnp.float32), axis=0, keepdims=True)
        small_out[pl.ds(4 + rel, 1), pl.ds(part * 384, 384)] = total
        wb[1, tile] = dot_nn(grad_turned[...], active).astype(jnp.bfloat16)
        tile_copy(0, tile).wait()
        gathered[...] += dot_nt(grad_pre, wb[0, tile])
        wb[0, tile] = dot_nn(normed_turned[...], grad_pre).astype(jnp.bfloat16)

    for part in range(2):
        for pair in range(2):

            def one(i, _):
                feed(part, 2 * pair + i)
                return 0

            lax.fori_loop(0, 2, one, 0)
            tick()

    def between(rows):
        found = gathered[rows, :]
        unit, scale = normalize(mid[rows, :])
        small_out[1:2] += jnp.sum(found * unit, axis=0, keepdims=True)
        total = grad[rows, :] + normalize_back(found, unit, scale, gain_two)
        grad[rows, :] = total
        grad_low[rows, :] = total.astype(jnp.bfloat16)

    by_rows(between)
    for copy in loads[3:]:
        copy.wait()

    def project(part, _):
        lanes = pl.ds(pl.multiple_of(part * LANES, LANES), LANES)
        grad_att[:, lanes] = dot_nt(grad_low[...], wa[1, 1, lanes, :]).astype(jnp.bfloat16)
        wa[1, 1, lanes, :] = dot_tn(att[:, lanes], grad_low[...]).astype(jnp.bfloat16)
        return 0

    lax.fori_loop(0, 3, project, 0)
    tick()
    for part in range(3):
        lanes = pl.ds(part * LANES, LANES)
        sums[...] = jnp.zeros_like(sums)
        keys_turned[...] = kv[0, :, lanes].astype(jnp.float32).T.astype(jnp.bfloat16)
        for start, count in ((0, 4 * PIECE), (PIECE, 3 * PIECE)):
            rows = pl.ds(start, PIECE)
            attention_back(
                q.at[rows, lanes],
                grad_att.at[rows, lanes],
                att.at[rows, lanes],
                kv.at[0, :count, lanes],
                kv.at[1, :count, lanes],
                keys_turned.at[:, :count],
                bias.at[:count, rows],
                lse.at[pl.ds(8 * part, 8), rows],
                sums,
                turned_q,
                count,
            )
            if start == 0:
                tick()
        kv[:, :, lanes] = sums[...].astype(jnp.bfloat16)
        share.start(part)
        if part > 0:
            share.relay(part - 1)
        tick()
    normed = grad_att

    def again(rows):
        unit, _ = normalize(low[rows, :].astype(jnp.float32))
        normed[rows, :] = (unit * gain_one).astype(jnp.bfloat16)

    by_rows(again)

    def turned(part, _):
        lanes = pl.ds(pl.multiple_of(part * LANES, LANES), LANES)
        raw = turn(q[:, lanes].astype(jnp.float32), cosine[...], -sine_table[...])
        raw = raw.astype(jnp.bfloat16)
        found = dot_nn(raw, wa[0, 0, lanes, :])

        @pl.when(part == 0)
        def _():
            gathered[...] = found

        @pl.when(part > 0)
        def _():
            gathered[...] += found

        wa[0, 0, lanes, :] = dot_tn(raw, normed[...]).astype(jnp.bfloat16)
        return 0

    lax.fori_loop(0, 3, turned, 0)
    share.relay(2)
    tick()
    for part in range(3):
        share.collect(part)

    def keyed(part, _):
        lanes = pl.ds(pl.multiple_of(part * LANES, LANES), LANES)
        noisy, clean = pl.ds(3 * PIECE, PIECE), pl.ds(2 * PIECE, PIECE)
        raw = jnp.concatenate([kv[0, noisy, lanes], kv[0, clean, lanes]], axis=0)
        raw = turn(raw.astype(jnp.float32), cosine[...], -sine_table[...]).astype(jnp.bfloat16)
        gathered[...] += dot_nn(raw, wa[0, 1, lanes, :])
        wa[0, 1, lanes, :] = dot_tn(raw, normed[...]).astype(jnp.bfloat16)
        raw = jnp.concatenate([kv[1, noisy, lanes], kv[1, clean, lanes]], axis=0)
        gathered[...] += dot_nn(raw, wa[1, 0, lanes, :])
        wa[1, 0, lanes, :] = dot_tn(raw, normed[...]).astype(jnp.bfloat16)
        return 0

    lax.fori_loop(0, 3, keyed, 0)
    tick()
    save_a = pltpu.make_async_copy(wa, grads_a, sems.at[10])
    save_a.start()

    def leave(rows):
        found = gathered[rows, :]
        unit, scale = normalize(low[rows, :].astype(jnp.float32))
        small_out[0:1] += jnp.sum(found * unit, axis=0, keepdims=True)
        total = grad[rows, :] + normalize_back(found, unit, scale, gain_one)
        grad_low[rows, :] = total.astype(jnp.bfloat16)

    by_rows(leave)
    save_grad = pltpu.make_async_copy(grad_low, grad_out, sems.at[11])
    save_grad.start()
    tick()
    share.drain()
    save_a.wait()
    save_grad.wait()


class Ticks:
    def __init__(self, groups):
        self.groups = list(groups)

    def __call__(self):
        if self.groups:
            for step in self.groups.pop(0):
                step()

    def rest(self):
        while self.groups:
            self()


def backward_buffers(width, units):
    low, full, count = jnp.bfloat16, jnp.float32, 2 * PIECE
    return [
        pltpu.VMEM((2, 2, width, width), low),
        pltpu.VMEM((2, 8, width, units // 8), low),
        pltpu.VMEM((count, width), low),
        pltpu.VMEM((count, width), low),
        pltpu.VMEM((2, 4 * PIECE, width), low),
        pltpu.VMEM((count, width), low),
        pltpu.VMEM((count, width), full),
        pltpu.VMEM((count, units), low),
        pltpu.VMEM((count, width), full),
        pltpu.VMEM((count, width), full),
        pltpu.VMEM((count, width), low),
        pltpu.VMEM((count, width), low),
        pltpu.VMEM((2, PIECE, width), low),
        pltpu.VMEM((2, PIECE, width), low),
        pltpu.VMEM((2, 4 * PIECE, LANES), full),
        pltpu.VMEM((LANES, 4 * PIECE), low),
        pltpu.VMEM((LANES, PIECE), full),
        pltpu.VMEM((width, count), low),
        pltpu.VMEM((width, count), low),
        pltpu.VMEM((24, count), full),
    ]


def backward_sems():
    dma = pltpu.SemaphoreType.DMA
    return [dma((3,))] * 6 + [dma((12,)), dma((2, 8))]


BUFFERS = 20


def later(step, *args):
    return lambda: step(*args)


def second_kernel(*refs):
    ins, refs = refs[:15], refs[15:]
    (grads_a, grad_out, small_out, out, final_b, carry), refs = refs[:6], refs[6:]
    buffers, stages, feed, refs = refs[:BUFFERS], refs[BUFFERS : BUFFERS + 2], refs[22:25], refs[25:]
    sems, feed_sem, gate, carry_sem = refs[:24], refs[24:-2], refs[-2], refs[-1]
    low_both = ins[14]
    place = Place()
    place.meet(place.partners())
    zero, last = [
        Spread(place, low_both.at[i], stages[i], i, out, sems[8 + 8 * i : 16 + 8 * i])
        for i in range(2)
    ]
    one, two = feed_sums(place, buffers[1], feed, feed_sem, gate)
    carries = [
        pltpu.make_async_copy(two.total(rel), carry.at[rel], carry_sem.at[rel]) for rel in range(4)
    ]

    def hand_on():
        two.load(travels=False)
        for copy in carries:
            copy.start()

    tick = Ticks(
        [
            [zero.take, last.take, zero.swap, later(zero.hops, 0), later(last.hops, 0)],
            [],
            [later(zero.forward, 0)],
            [one.start, last.swap],
            [later(zero.hops, 1), later(last.forward, 0)],
            [later(zero.finish, 0)],
            [one.load],
            [later(zero.forward, 1), two.start],
            [later(last.finish, 0)],
            [one.middle],
            [later(last.hops, 1), later(zero.finish, 1)],
            [one.gather],
            [hand_on],
            [one.line_one, later(last.forward, 1)],
            [one.line_two],
            [later(last.finish, 1), later(one.finish, 1, final_b.at[place.s])],
        ]
    )
    body = ins[:3] + (low_both.at[0],) + ins[4:14] + (grads_a, grad_out, small_out) + buffers
    backward_layer(1, body, place, tick, sems[:6], sems[6], sems[7])
    tick.rest()
    zero.drain()
    last.drain()
    one.drain(1, final_b.at[place.s])
    two.drain_exchange()
    for copy in carries:
        copy.wait()


def first_kernel(*refs):
    ins, refs = refs[:16], refs[16:]
    (grads_a, grad_out, small_out, out, final_b), refs = refs[:5], refs[5:]
    buffers, stage, refs = refs[:BUFFERS], refs[BUFFERS], refs[BUFFERS + 1 :]
    feed, (total, hop_in, line_in), refs = refs[:3], refs[3:6], refs[6:]
    sems, feed_sem, kept_sem, gate = refs[:16], refs[16:36], refs[36:46], refs[46]
    carry, prior_grad = ins[14:]
    place = Place()
    place.meet(place.partners())
    back = Spread(place, prior_grad, stage, 1, out, sems[8:16])
    one, two = feed_sums(place, buffers[1], feed, feed_sem, gate)
    kept = Sum(
        place,
        lambda pack, rel: carry.at[rel],
        lambda rel: total.at[rel],
        (None, hop_in, line_in),
        kept_sem,
        loaded=True,
    )
    targets = [final_b.at[place.s, 0], final_b.at[place.s, 1]]
    tick = Ticks(
        [
            [back.take, back.swap, kept.start, later(back.hops, 0)],
            [kept.load],
            [later(back.forward, 0)],
            [one.start, kept.middle],
            [later(back.hops, 1)],
            [kept.gather, later(back.finish, 0)],
            [one.load],
            [kept.line_one, two.start],
            [later(back.forward, 1)],
            [one.middle, kept.line_two],
            [two.load],
            [later(back.finish, 1), one.gather],
            [two.middle, later(kept.finish, 1, targets[1])],
            [one.line_one],
            [two.gather, one.line_two],
            [later(one.finish, 0, targets[0]), two.line_one],
            [two.line_two, later(two.finish, 0, targets[1])],
        ]
    )
    body = ins[:14] + (grads_a, grad_out, small_out) + buffers
    backward_layer(0, body, place, tick, sems[:6], sems[6], sems[7])
    tick.rest()
    back.drain()
    kept.drain(1, targets[1])
    one.drain(0, targets[0])
    two.drain(0, targets[1])


def last_kernel(*refs):
    priors, (grad_zero, small_zero, small_one, out, final_a, small) = refs[:2], refs[2:8]
    held, stage, (small_in, extra), sems = refs[8:24], refs[24], refs[25:27], refs[27:]
    held_sem, spread_sem, (tiny_send, tiny_recv) = sems[:40], sems[40:48], sems[48:]
    place = Place()
    place.meet(place.partners())
    sums = []
    for i in range(2):
        sums += attention_sums(
            place, priors[i], held[8 * i : 8 * i + 8], held_sem[20 * i : 20 * i + 20]
        )
    back = Spread(place, grad_zero, stage, 0, out, spread_sem)
    targets = [final_a.at[place.s, 0], final_a.at[place.s, 1]] * 2
    layers = (1, 1, 0, 0)
    small[0], small[1] = small_zero[...], small_one[...]
    rows_beside = ((4, 5, 6, 7), (5, 4, 7, 6), (6, 7, 4, 5), (4, 5, 6, 7), (4, 5, 6, 7))
    partners = (
        place.on(section=place.core),
        place.on(tp=place.beside_x),
        place.on(tp=place.beside_y),
        place.on(seq=place.twin),
        place.on(seq=place.far),
    )

    def tiny(i):
        return remote(extra.at[i], small_in.at[i], tiny_send.at[i], tiny_recv.at[i], partners[i])

    def tiny_start(i):
        extra[i] = small[...]
        tiny(i).start()

    def tiny_end(i):
        tiny(i).wait_recv()
        for layer in range(2):
            small[layer, 0:4] = extra[i, layer, 0:4] + small_in[i, layer, 0:4]
            for row, other in enumerate(rows_beside[i]):
                at = row + 4
                small[layer, at : at + 1] = (
                    extra[i, layer, at : at + 1] + small_in[i, layer, other : other + 1]
                )

    tiny_start(0)
    back.take()
    back.swap()
    sums[0].start()
    back.hops(0)
    for item in sums[1:]:
        item.start()
    sums[0].load()
    sums[1].load()
    tiny_end(0)
    tiny_start(1)
    back.forward(0)
    sums[2].load()
    sums[0].middle()
    sums[3].load()
    sums[1].middle()
    tiny_end(1)
    tiny_start(2)
    sums[0].gather()
    sums[2].middle()
    sums[1].gather()
    sums[0].line_one()
    sums[3].middle()
    back.hops(1)
    sums[1].line_one()
    tiny_end(2)
    tiny_start(3)
    sums[2].gather()
    sums[0].line_two()
    sums[2].line_one()
    sums[3].gather()
    sums[1].line_two()
    sums[3].line_one()
    back.forward(1)
    tiny_end(3)
    tiny_start(4)
    sums[2].line_two()
    sums[0].finish(1, targets[0])
    sums[1].finish(1, targets[1])
    sums[3].line_two()
    back.finish(0)
    sums[2].finish(0, targets[2])
    back.finish(1)
    sums[3].finish(0, targets[3])
    tiny_end(4)
    for item, layer, target in zip(sums, layers, targets):
        item.drain(layer, target)
    back.drain()
    for i in range(5):
        tiny(i).wait_send()


def call(kernel, name, number, ins, spaces, shapes, out_spaces, scratch, flops, moved):
    return pl.pallas_call(
        kernel,
        name=name,
        out_shape=[jax.ShapeDtypeStruct(shape, kind) for shape, kind in shapes],
        in_specs=spaces,
        out_specs=out_spaces,
        scratch_shapes=scratch,
        compiler_params=pltpu.CompilerParams(
            collective_id=number, has_side_effects=True, vmem_limit_bytes=62 * 1024 * 1024
        ),
        cost_estimate=pl.CostEstimate(
            flops=flops, bytes_accessed=moved, transcendentals=20_000_000
        ),
    )(*ins)


def run_backward(full_a, full_b, seeded, tokens, low_both, kept, gains, bias, tables):
    low, full, count = jnp.bfloat16, jnp.float32, 2 * PIECE
    width, units = full_a.shape[-1], 8 * full_b.shape[-1]
    grads = [
        ((2, 2, width, width), low),
        ((count, width), low),
        ((8, width), full),
    ]
    out = ((2, 4, count, width), low)
    row_piece, tile_piece = (192, width), (width, units // 8)
    final_a, final_b = ((2, 2) + row_piece, low), ((2, 2) + tile_piece, low)
    half_b, carry = ((2,) + tile_piece, low), ((4,) + tile_piece, low)
    stage = pltpu.VMEM((4, 2, PIECE, width), low)
    dma, gate = pltpu.SemaphoreType.DMA, pltpu.SemaphoreType.REGULAR
    common = (*kept, gains, bias, *tables)
    common_spaces = [HBM] * 10 + [VMEM] * 4
    held = sum_buffers(row_piece, (4, 4, 3, 2) * 2)
    second = call(
        second_kernel,
        "backward_second",
        2,
        (full_a, full_b, seeded, tokens) + common + (low_both,),
        common_spaces + [HBM],
        grads + [out, half_b, carry],
        [HBM] * 2 + [VMEM] + [HBM] * 3,
        backward_buffers(width, units)
        + [stage, stage]
        + feed_buffers(tile_piece, 1)
        + backward_sems()
        + spread_sems()
        + spread_sems()
        + sum_sems()
        + sum_sems()
        + [gate, dma((4,))],
        40_000_000_000,
        80_000_000,
    )
    prior_a, grad_one, small_one, layer_out, feed_one, carried = second
    first = call(
        first_kernel,
        "backward_first",
        3,
        (full_a, full_b, grad_one, tokens) + common + (carried, grad_one),
        common_spaces + [HBM] * 2,
        grads + [out, final_b],
        [HBM] * 2 + [VMEM] + [HBM] * 2,
        backward_buffers(width, units)
        + [stage]
        + feed_buffers(tile_piece, 2)
        + sum_buffers(tile_piece, (4, 3, 2))
        + backward_sems()
        + spread_sems()
        + sum_sems()
        + sum_sems()
        + sum_sems()
        + [gate],
        40_000_000_000,
        80_000_000,
    )
    grads_a, grad_zero, small_zero, out_one, feed_zero = first
    by_shard = (2, 2, 4, 192, width)
    last = call(
        last_kernel,
        "sum_and_spread",
        4,
        (prior_a.reshape(by_shard), grads_a.reshape(by_shard), grad_zero, small_zero, small_one),
        [HBM] * 3 + [VMEM] * 2,
        [out, final_a, ((2, 8, width), full)],
        [HBM] * 2 + [VMEM],
        held
        + held
        + [stage]
        + [pltpu.VMEM((5, 2, 8, width), full), pltpu.VMEM((5, 2, 8, width), full)]
        + sum_sems()
        + sum_sems()
        + sum_sems()
        + sum_sems()
        + spread_sems()
        + [dma((5,)), dma((5,))],
        100_000_000,
        40_000_000,
    )
    out_zero, rows, small = last
    return layer_out, (out_zero, out_one), rows, (feed_zero, feed_one), small


def spread(
    layer_input,
    cotangent,
    doc_lengths,
    ln1_gain,
    w_qkv,
    w_out,
    ln2_gain,
    w_up,
    b_up,
    w_down,
    b_down,
):
    s, t, z = (lax.axis_index(name) for name in ("section", "tp", "seq"))
    micros, rows, width_pos, width = layer_input.shape
    half, group = z % 2, z // 2

    own_a = jnp.stack(
        [
            jnp.stack([w_qkv[0, :, 0].T, w_qkv[0, :, 1].T]),
            jnp.stack([w_qkv[0, :, 2].T, w_out[0]]),
        ]
    )
    shard = w_up.shape[-1]
    own_b = jnp.stack([w_up[0], w_down[0].T]).reshape(2, width, 2, shard // 2).transpose(0, 2, 1, 3)
    gains = jnp.concatenate([ln1_gain, ln2_gain, b_down, jnp.zeros((5, width), jnp.float32)])
    own_c = jnp.stack([gains, jnp.concatenate([b_up, jnp.zeros((7, width), jnp.float32)])])

    block = 2 * half + s
    lengths = doc_lengths.reshape(micros * rows, -1)
    lengths = lax.dynamic_index_in_dim(lengths, 4 * group + t, 0, keepdims=False)
    ends = jnp.cumsum(lengths)
    piece_pos = jnp.arange(PIECE)
    query_base = jnp.tile(block * PIECE + piece_pos, 2)
    key_base = jnp.concatenate([(block - 2 + i) * PIECE + piece_pos for i in (0, 1, 2, 2)])
    query_noisy = jnp.arange(2 * PIECE) < PIECE
    key_noisy = jnp.arange(4 * PIECE) >= 3 * PIECE

    def docs_of(base):
        return jnp.sum((base[:, None] >= ends[None, :]).astype(jnp.int32), axis=-1)

    query_block, key_block = query_base[None, :] // BLOCK, key_base[:, None] // BLOCK
    query_kind, key_kind = query_noisy[None, :], key_noisy[:, None]
    mask = (
        (query_kind & key_kind & (query_block == key_block))
        | (query_kind & ~key_kind & (key_block < query_block))
        | (~query_kind & ~key_kind & (key_block <= query_block))
    )
    mask = mask & (docs_of(query_base)[None, :] == docs_of(key_base)[:, None])
    mask = mask & (key_base >= 0)[:, None]
    bias = jnp.where(mask, 0.0, -1e30).astype(jnp.bfloat16)
    frequency = 10000.0 ** (-jnp.arange(HDIM // 2).astype(jnp.float32) * 2.0 / HDIM)
    angles = query_base.astype(jnp.float32)[:, None] * frequency[None, :]
    cosine, sine_table = jnp.cos(angles), jnp.sin(angles)
    turn_cos = jnp.tile(cosine, (1, 4))
    turn_sin = jnp.tile(jnp.concatenate([-sine_table, sine_table], axis=1), (1, 2))

    flat = (micros * rows, width_pos, width)
    forward = run_forward(
        layer_input.reshape(flat), cotangent.reshape(flat), own_a, own_b, own_c, bias, turn_cos, turn_sin
    )
    full_a, full_b, gains, seeded, tokens, low_both, *kept = forward
    tables = (turn_cos, turn_sin)
    layer_out, input_grads, final_a, feeds, small = run_backward(
        full_a, full_b, seeded, tokens, low_both, kept, gains, bias, tables
    )
    input_grad = jnp.where(s == 0, *input_grads)
    final_b = jnp.stack([jnp.where(s == 0, feeds[0][:, 0], feeds[1]), feeds[0][:, 1]], axis=1)
    small = lax.dynamic_index_in_dim(small, s, 0, keepdims=False)
    final_a, final_b = final_a.astype(jnp.float32), final_b.astype(jnp.float32)
    grad_qkv = jnp.stack([final_a[0, 0].T, final_a[0, 1].T, final_a[1, 0].T], axis=1)
    grad_up, grad_down = final_b.transpose(0, 2, 1, 3).reshape(2, width, shard)
    out_shape = (1,) + layer_input.shape
    return (
        layer_out.reshape(out_shape),
        input_grad.reshape(out_shape),
        small[0:1],
        grad_qkv[None],
        final_a[1, 1][None],
        small[1:2],
        grad_up[None],
        small[4:5],
        grad_down.T[None],
        small[2:3],
    )


def solution(mesh):
    sizes = tuple(mesh.shape[name] for name in ("section", "tp", "seq"))
    local = spread if sizes == (2, 4, 4) else pipelined
    return jax.shard_map(
        local,
        mesh=mesh,
        in_specs=(
            P(None, None, "seq", None),
            P(None, None, "seq", None),
            P(),
            P("section", None),
            P("section", None, None, "tp"),
            P("section", "tp", None),
            P("section", None),
            P("section", None, "tp"),
            P("section", "tp"),
            P("section", "tp", None),
            P("section", None),
        ),
        out_specs=(
            P("section", None, None, "seq", None),
            P("section", None, None, "seq", None),
            P("section", None),
            P("section", None, None, "tp"),
            P("section", "tp", None),
            P("section", None),
            P("section", None, "tp"),
            P("section", "tp"),
            P("section", "tp", None),
            P("section", None),
        ),
        check_vma=False,
    )
```

profile of v0, /device:TPU:0, one launch (start us, length us, event | category | flops | bytes accessed | tf_op | source)
XLA Modules:
  0.0 553.3 jit_solution(4418888297688205906)
XLA Ops:
  0.8 0.6 copy-done
  1.3 0.2 reduce-window.8
  1.7 0.1 convert_reduce_fusion.1
  1.8 2.8 select_convert_fusion.bias.refs_11_
  4.6 0.3 fusion.2
  5.0 0.8 copy.39.sine_table.refs_13_
  5.8 0.8 copy.38.cosine.refs_12_
  6.8 0.1 maximum_bitcast_fusion.2
  6.9 1.1 pad_maximum_fusion.own_a
  8.2 0.6 pad_maximum_fusion.2.own_c
  8.8 0.6 copy.35
  9.5 0.7 copy.36
  10.2 0.7 copy.37
  11.0 1.7 maximum_bitcast_fusion.own_b
  12.6 157.3 %forward_layers.1 = (bf16[2,2,2,768,768]{4,3,2,1,0:T(8,128)(2,1)}, bf16[2,2,8,768,384]{4,3,2,1,0:T(8,128)(2,1)}, f32[2,8,768]{2,1,0:T(8,128)}, bf16[512,768]{1,0...) custom-call(bf16[8,512,768]{2,1,0:T(8,128)(2,1)} %bitcast.111, ...), custom_call_target="tpu_custom_call" | custom-call | flops 30000001024 | bytes 80000000 | tf_op jit(solution)/shard_map/forward_layers/pallas_call | solution.py:904
  169.9 118.4 %backward_second.1 = (bf16[2,2,768,768]{3,2,1,0:T(8,128)(2,1)}, bf16[512,768]{1,0:T(8,128)(2,1)}, f32[8,768]{1,0:T(8,128)}, bf16[2,4,512,768]{3,2,1,0:T(8,128)(2...) custom-call(bf16[2,2,2,768,768]{4,3,2,1,0:T(8,128)(2,1)} %get-tuple-element.36.refs_0_, ...), custom_call_target="tpu_custom_call" | custom-call | flops 40000000000 | bytes 80000000 | tf_op jit(solution)/shard_map/backward_second/pallas_call | solution.py:1961
  288.4 148.2 %backward_first.1 = (bf16[2,2,768,768]{3,2,1,0:T(8,128)(2,1)}, bf16[512,768]{1,0:T(8,128)(2,1)}, f32[8,768]{1,0:T(8,128)}, bf16[2,4,512,768]{3,2,1,0:T(8,128)(2,1)}, bf16[2,2,768,384]{3,2,1,0:T(8,128)(2,1)}) custom-call(bf16[2,2,2,768,768]{4,3,2,1,0:T(8,128)(2,1)} %get-tuple-element.36.refs_0_, bf16[2,2,8,768,384]{4,3,2,1,0:T(8,128)(2,1)} %get-tuple-element.37.refs_1_, ...), custom_call_target="tpu_custom_call" | custom-call | flops 40000000000 | bytes 80000000 | tf_op jit(solution)/shard_map/backward_first/pallas_call | solution.py:1961
  436.6 1.8 fusion.1
  438.5 0.2 copy-done.2
  438.6 0.1 slice.65
  438.8 0.3 convert_bitcast_fusion
  439.1 2.5 fusion.10
  441.6 2.0 copy.45
  443.6 2.0 copy.47
  445.6 3.0 copy.46
  448.6 87.1 %sum_and_spread.1 = (bf16[2,4,512,768]{3,2,1,0:T(8,128)(2,1)}, bf16[2,2,192,768]{3,2,1,0:T(8,128)(2,1)}, f32[2,8,768]{2,1,0:T(8,128)}) custom-call(bf16[2,2,4,192,768]{4,3,2,1,0:T(8,128)(2,1)} %bitcast.113, bf16[2,2,4,192,768]{4,3,2,1,0:T(8,128)(2,1)} %bitcast.114, bf16[512,768]{1,0:T(8,128)(2,1)} %get-tuple-element.53.refs_2_, ...), custom_call_target="tpu_custom_call" | custom-call | flops 100000000 | bytes 40000000 | tf_op jit(solution)/shard_map/sum_and_spread/pallas_call | solution.py:1961
  535.7 1.6 convert_element_type.32
  537.3 1.0 slice_bitcast_fusion.1
  538.3 1.3 maximum_bitcast_fusion.1
  539.6 6.1 %broadcast_select_fusion = bf16[2,4,512,768]{3,2,1,0:T(8,128)(2,1)} fusion(bf16[2,4,512,768]{3,2,1,0:T(8,128)(2,1)} %get-tuple-element.56, bf16[2,4,512,768]{3,2,1,0:T(8,128)(2,1)S(1)} %bitcast.99, pred[]{:T(512)S(6)} %eq.38), kind=kLoop, calls=%fused_computation | loop fusion | flops 3145728 | bytes 18874368 | tf_op jit(solution)/shard_map/jit(_where)/select_n | solution.py:2129
  545.7 1.5 dynamic-slice_bitcast_fusion
  547.2 5.9 %copy.52 = bf16[1,4,2,512,768]{4,3,2,1,0:T(8,128)(2,1)} copy(bf16[1,4,2,512,768]{4,3,2,1,0:T(8,128)(2,1)} %bitcast.97) | data formatting | bytes 12582912
  (47 shorter events, 0.5 us)
Async XLA Ops:
  0.6 0.7 copy-start
  0.7 6.0 %copy-start.6 = (bf16[1,768,3,192]{1,3,2,0:T(8,128)(2,1)S(1)}, bf16[1,768,3,192]{1,3,2,0:T(8,128)(2,1)}, u32[]{:S(2)}) copy-start(bf16[1,768,3,192]{1,3,2,0:T(8,128)(2,1)} %param.15) | copy-start | bytes 2654212
  1.8 5.0 copy-start.7
  6.7 1.4 copy-start.8
  6.7 1.4 copy-start.9
  6.8 1.4 copy-start.10
  6.8 1.3 copy-start.11
  6.8 2.0 copy-start.3
  8.8 1.4 copy-start.4
  288.3 148.3 %copy-start.5 = (bf16[2,768,384]{2,1,0:T(8,128)(2,1)S(1)}, bf16[2,768,384]{2,1,0:T(8,128)(2,1)}, u32[]{:S(2)}) copy-start(bf16[2,768,384]{2,1,0:T(8,128)(2,1)} %get-tuple-element.61) | copy-start | bytes 3538948
  436.6 2.0 copy-start.2
  535.7 3.9 slice-start
  537.3 2.3 slice-start.1
  547.2 5.9 %copy-start.1 = (s32[4,2,4]{2,1,0:T(2,128)S(1)}, s32[4,2,4]{2,1,0:T(2,128)}, u32[]{:S(2)}) copy-start(s32[4,2,4]{2,1,0:T(2,128)} %param.13) | copy-start | bytes 388
where the time goes:
time: 563 us; the launch traced here: 553 us
  Pallas kernels  511 us (91%)
  local copies, waits for them, and re-layouts  22.8 us (4%)
  other arithmetic  18.3 us (3%)
    pallas_call x3, Pallas kernels, call(): pl.pallas_call(kernel, name=name, out_shape=[jax.ShapeDtypeStruct(shape,...  354 us
    pallas_call x1, Pallas kernels, run_forward(): pl.pallas_call(forward_kernel, name='forward_layers', out_shape=[shape((2...  157 us

commit v1 on v0

--- a/solution.py
+++ b/solution.py
@@ -523,21 +523,20 @@
         return here, there
 
     def start_own(self, chunk):
-        for pack in range(2):
-            for copy in self.own_copies(chunk, pack):
+        for pack in (self.place.core, self.place.s):
+            for copy in self.own_copies(chunk, pack)[::-1]:
                 copy.start()
 
-    def wait_own(self, layer, chunk):
-        for pack in range(2):
-            here, there = self.own_copies(chunk, pack)
-
-            @pl.when(self.place.s == layer)
-            def _():
-                here.wait()
-
-            @pl.when(self.place.s != layer)
-            def _():
-                there.wait_recv()
+    def wait_own(self, layer, chunk, pack):
+        here, there = self.own_copies(chunk, pack)
+
+        @pl.when(self.place.s == layer)
+        def _():
+            here.wait()
+
+        @pl.when(self.place.s != layer)
+        def _():
+            there.wait_recv()
 
     def hops(self, layer, chunk):
         place = self.place
@@ -571,7 +570,7 @@
         ]
 
     def begin(self, layer, chunk):
-        self.wait_own(layer, chunk)
+        self.wait_own(layer, chunk, self.place.s)
         first, second, _ = self.hops(layer, chunk)
         first.start()
         second.start()
@@ -590,6 +589,8 @@
         self.chips(layer, chunk)[2].start()
 
     def need(self, layer, chunk):
+        if chunk < 3:
+            self.wait_own(layer, chunk, self.place.core)
         for copy in self.chips(layer, chunk):
             copy.wait_recv()
 
@@ -745,14 +746,16 @@
     own_seed, seed_swap = bring(cotangent, seeded_out, seed_sem, seed_send, seed_recv)
     own_tokens.start()
     swap.start()
-    for chunk in (3, 0, 1, 2):
-        weights.start_own(chunk)
+    weights.start_own(0)
     weights.begin(0, 0)
-    weights.begin(0, 1)
-    weights.begin(0, 3)
-    weights.begin(1, 3)
+    weights.start_own(3)
+    weights.start_own(1)
+    for layer in range(2):
+        weights.begin(layer, 3)
+        weights.wait_own(layer, 3, place.core)
     gains = full_c.at[:, 0, 0]
     gains_out[...] = full_c[:, 0, 0]
+    weights.forward(0, 0)
     own_tokens.wait()
     swap.wait()
     x_save = pltpu.make_async_copy(low, x_out, save_sem.at[16])
@@ -784,13 +787,12 @@
         unit, _ = normalize(x[...])
         normed[...] = (unit * gains[layer, 0:1]).astype(jnp.bfloat16)
         if layer == 0:
-            weights.forward(0, 0)
-            weights.begin(0, 2)
             weights.finish(0, 0)
+            weights.begin(0, 1)
+            weights.start_own(2)
         else:
-            weights.forward(1, 0)
+            weights.finish(1, 0)
             weights.begin(1, 2)
-            weights.finish(1, 0)
             for copy in saves(0)[1:]:
                 copy.wait()
         weights.need(layer, 0)
@@ -815,8 +817,7 @@
             weights.finish(0, 3)
             weights.finish(1, 3)
             own_seed.start()
-            weights.forward(0, 1)
-            weights.begin(1, 0)
+            weights.begin(0, 2)
         else:
             weights.forward(1, 1)
         for part in range(3):
@@ -835,14 +836,19 @@
                 )
             if part == 2 and layer == 0:
                 seed_swap.start()
-            if part == 0:
-                weights.finish(layer, 1)
-            elif part == 1:
-                weights.forward(layer, 2)
-                if layer == 0:
-                    weights.begin(1, 1)
+            if layer == 0:
+                if part == 0:
+                    weights.forward(0, 1)
+                elif part == 1:
+                    weights.finish(0, 1)
+                    weights.begin(1, 0)
+                else:
+                    weights.forward(0, 2)
             else:
-                weights.finish(layer, 2)
+                if part == 1:
+                    weights.finish(1, 1)
+                elif part == 2:
+                    weights.forward(1, 2)
         for copy in saves(layer)[1:4] + saves(layer)[6:]:
             copy.start()
 
@@ -858,6 +864,10 @@
         saves(layer)[4].start()
         weights.need(layer, 3)
         for part in range(2):
+            if part == 1:
+                weights.finish(layer, 2)
+                if layer == 0:
+                    weights.begin(1, 1)
             weights.need(layer, part + 1)
             if part == 1:
                 for copy in weight_saves(layer)[2:]:
@@ -883,6 +893,8 @@
         low[...] = x[...].astype(jnp.bfloat16)
         saves(layer)[0].start()
         x[...] = low[...].astype(jnp.float32)
+        if layer == 0:
+            weights.forward(1, 0)
     for copy in saves(1):
         copy.wait()
     for layer in range(2):
@@ -1199,7 +1211,7 @@
             for i, (source, target, plane) in enumerate(listed)
         ]
 
-    def gather(self):
+    def gather(self, save=None):
         _, second, third = self.moves()
         second.wait_recv()
         third.wait_recv()
@@ -1207,7 +1219,16 @@
         total[...] = low_sum(total[...], self.hop_in[1], self.hop_in[2])
         second.wait_send()
         third.wait_send()
-
+        if save is not None:
+            save.start()
+        else:
+            self.enter_line()
+
+    def resume(self, saved):
+        saved.wait()
+        self.enter_line()
+
+    def enter_line(self):
         @pl.when(self.outer)
         def _():
             self.lines()[0].start()
@@ -1243,6 +1264,10 @@
         )
         return here, there
 
+    def store(self, save):
+        self.line_three()
+        save.start()
+
     def finish(self, layer, target):
         self.line_three()
         here, there = self.ends(target)
@@ -1260,7 +1285,7 @@
             for rel in range(4):
                 self.other(rel).wait_send()
 
-    def drain(self, layer, target):
+    def drain_end(self, layer, target):
         here, there = self.ends(target)
 
         @pl.when(self.place.s == layer)
@@ -1272,9 +1297,11 @@
         def _():
             there.wait_send()
 
+    def drain_plane(self):
         self.drain_exchange()
         self.moves()[0].wait_send()
 
+    def drain_line(self):
         @pl.when(self.outer)
         def _():
             self.lines()[0].wait_send()
@@ -1326,18 +1353,17 @@
         own_sems = sems[SUM_SEMS * i : SUM_SEMS * (i + 1)]
         gates = {"opens": gate} if i == 0 else {"waits": gate}
         at = min(i, buffers[1].shape[0] - 1)
-        parts = (inbox, buffers[1].at[at], buffers[2].at[at])
-        sums.append(Sum(place, source, kept, parts, own_sems, **gates))
+        sums.append(Sum(place, source, kept, (inbox, buffers[1].at[at], None), own_sems, **gates))
     return sums
 
 
 def feed_buffers(piece, count):
     kind = jnp.bfloat16
-    return [
-        pltpu.VMEM((4,) + piece, kind),
-        pltpu.VMEM((count, 3) + piece, kind),
-        pltpu.VMEM((count, 2) + piece, kind),
-    ]
+    return [pltpu.VMEM((4,) + piece, kind), pltpu.VMEM((count, 3) + piece, kind)]
+
+
+def line_sum(place, total, line_in, sems):
+    return Sum(place, None, lambda rel: total.at[rel], (None, None, line_in), sems)
 
 
 class KeyReturn:
@@ -1763,8 +1789,8 @@
 
 def second_kernel(*refs):
     ins, refs = refs[:15], refs[15:]
-    (grads_a, grad_out, small_out, out, final_b, carry), refs = refs[:6], refs[6:]
-    buffers, stages, feed, refs = refs[:BUFFERS], refs[BUFFERS : BUFFERS + 2], refs[22:25], refs[25:]
+    (grads_a, grad_out, small_out, out, carry_one, carry), refs = refs[:6], refs[6:]
+    buffers, stages, feed, refs = refs[:BUFFERS], refs[BUFFERS : BUFFERS + 2], refs[22:24], refs[24:]
     sems, feed_sem, gate, carry_sem = refs[:24], refs[24:-2], refs[-2], refs[-1]
     low_both = ins[14]
     place = Place()
@@ -1777,6 +1803,7 @@
     carries = [
         pltpu.make_async_copy(two.total(rel), carry.at[rel], carry_sem.at[rel]) for rel in range(4)
     ]
+    save_one = pltpu.make_async_copy(one.total(0), carry_one, carry_sem.at[4])
 
     def hand_on():
         two.load(travels=False)
@@ -1796,11 +1823,11 @@
             [later(last.finish, 0)],
             [one.middle],
             [later(last.hops, 1), later(zero.finish, 1)],
-            [one.gather],
+            [],
             [hand_on],
-            [one.line_one, later(last.forward, 1)],
-            [one.line_two],
-            [later(last.finish, 1), later(one.finish, 1, final_b.at[place.s])],
+            [later(one.gather, save_one), later(last.forward, 1)],
+            [],
+            [later(last.finish, 1)],
         ]
     )
     body = ins[:3] + (low_both.at[0],) + ins[4:14] + (grads_a, grad_out, small_out) + buffers
@@ -1808,19 +1835,21 @@
     tick.rest()
     zero.drain()
     last.drain()
-    one.drain(1, final_b.at[place.s])
+    one.drain_plane()
+    save_one.wait()
     two.drain_exchange()
     for copy in carries:
         copy.wait()
 
 
 def first_kernel(*refs):
-    ins, refs = refs[:16], refs[16:]
-    (grads_a, grad_out, small_out, out, final_b), refs = refs[:5], refs[5:]
+    ins, refs = refs[:17], refs[17:]
+    (grads_a, grad_out, small_out, out, done, carry_out), refs = refs[:6], refs[6:]
     buffers, stage, refs = refs[:BUFFERS], refs[BUFFERS], refs[BUFFERS + 1 :]
-    feed, (total, hop_in, line_in), refs = refs[:3], refs[3:6], refs[6:]
-    sems, feed_sem, kept_sem, gate = refs[:16], refs[16:36], refs[36:46], refs[46]
-    carry, prior_grad = ins[14:]
+    feed, (total, hop_in, line_in, line_total, line_in_one), refs = refs[:2], refs[2:7], refs[7:]
+    sems, feed_sem, kept_sem, line_sem = refs[:16], refs[16:36], refs[36:46], refs[46:56]
+    gate, carry_sem = refs[56:]
+    carry_one, carry, prior_grad = ins[14:]
     place = Place()
     place.meet(place.partners())
     back = Spread(place, prior_grad, stage, 1, out, sems[8:16])
@@ -1833,41 +1862,54 @@
         kept_sem,
         loaded=True,
     )
-    targets = [final_b.at[place.s, 0], final_b.at[place.s, 1]]
+    line = line_sum(place, line_total, line_in_one, line_sem)
+    line_load = pltpu.make_async_copy(carry_one, line_total.at[0], carry_sem.at[0])
+    saves = [
+        pltpu.make_async_copy(line.total(1), done.at[0], carry_sem.at[1]),
+        pltpu.make_async_copy(kept.total(1), done.at[1], carry_sem.at[2]),
+        pltpu.make_async_copy(one.total(0), carry_out.at[0], carry_sem.at[3]),
+        pltpu.make_async_copy(two.total(0), carry_out.at[1], carry_sem.at[4]),
+    ]
     tick = Ticks(
         [
-            [back.take, back.swap, kept.start, later(back.hops, 0)],
-            [kept.load],
+            [back.take, back.swap, line_load.start, kept.start, later(back.hops, 0)],
+            [later(line.resume, line_load), kept.load],
             [later(back.forward, 0)],
-            [one.start, kept.middle],
-            [later(back.hops, 1)],
-            [kept.gather, later(back.finish, 0)],
+            [one.start, line.line_one],
+            [kept.middle, later(back.hops, 1)],
+            [line.line_two, later(back.finish, 0)],
             [one.load],
-            [kept.line_one, two.start],
-            [later(back.forward, 1)],
-            [one.middle, kept.line_two],
-            [two.load],
-            [later(back.finish, 1), one.gather],
-            [two.middle, later(kept.finish, 1, targets[1])],
-            [one.line_one],
-            [two.gather, one.line_two],
-            [later(one.finish, 0, targets[0]), two.line_one],
-            [two.line_two, later(two.finish, 0, targets[1])],
+            [kept.gather, two.start],
+            [later(back.forward, 1), later(line.store, saves[0])],
+            [kept.line_one],
+            [one.middle, two.load],
+            [kept.line_two, later(back.finish, 1)],
+            [],
+            [later(one.gather, saves[2]), later(kept.store, saves[1])],
+            [two.middle],
+            [],
+            [later(two.gather, saves[3])],
         ]
     )
     body = ins[:14] + (grads_a, grad_out, small_out) + buffers
     backward_layer(0, body, place, tick, sems[:6], sems[6], sems[7])
     tick.rest()
     back.drain()
-    kept.drain(1, targets[1])
-    one.drain(0, targets[0])
-    two.drain(0, targets[1])
+    for item in (kept, one, two):
+        item.drain_plane()
+    line.drain_line()
+    kept.drain_line()
+    for copy in saves:
+        copy.wait()
 
 
 def last_kernel(*refs):
-    priors, (grad_zero, small_zero, small_one, out, final_a, small) = refs[:2], refs[2:8]
-    held, stage, (small_in, extra), sems = refs[8:24], refs[24], refs[25:27], refs[27:]
-    held_sem, spread_sem, (tiny_send, tiny_recv) = sems[:40], sems[40:48], sems[48:]
+    priors, (done, carry, grad_zero, small_zero, small_one), refs = refs[:2], refs[2:7], refs[7:]
+    (out, final_a, final_b, small), refs = refs[:4], refs[4:]
+    held, stage, (small_in, extra), refs = refs[:16], refs[16], refs[17:19], refs[19:]
+    (line_total, line_in), sems = refs[:2], refs[2:]
+    held_sem, spread_sem, line_sem, sems = sems[:40], sems[40:48], sems[48:68], sems[68:]
+    tiny_send, tiny_recv, carry_sem, end_local, end_send, end_recv = sems
     place = Place()
     place.meet(place.partners())
     sums = []
@@ -1875,8 +1917,13 @@
         sums += attention_sums(
             place, priors[i], held[8 * i : 8 * i + 8], held_sem[20 * i : 20 * i + 20]
         )
+    lines, loads = [], []
+    for i in range(2):
+        lines.append(line_sum(place, line_total.at[i], line_in.at[i], line_sem[10 * i : 10 * i + 10]))
+        loads.append(pltpu.make_async_copy(carry.at[i], line_total.at[i, 0], carry_sem.at[i]))
     back = Spread(place, grad_zero, stage, 0, out, spread_sem)
     targets = [final_a.at[place.s, 0], final_a.at[place.s, 1]] * 2
+    halves = [final_b.at[place.s, :, pl.ds(384 * i, 384)] for i in range(2)]
     layers = (1, 1, 0, 0)
     small[0], small[1] = small_zero[...], small_one[...]
     rows_beside = ((4, 5, 6, 7), (5, 4, 7, 6), (6, 7, 4, 5), (4, 5, 6, 7), (4, 5, 6, 7))
@@ -1888,6 +1935,37 @@
         place.on(seq=place.far),
     )
 
+    def done_ends(i):
+        here = pltpu.make_async_copy(done.at[i], halves[i], end_local.at[i])
+        there = remote(
+            done.at[i], halves[i], end_send.at[i], end_recv.at[i], place.on(section=place.core)
+        )
+        return here, there
+
+    def done_start():
+        @pl.when(place.s == 1)
+        def _():
+            for i in range(2):
+                done_ends(i)[0].start()
+
+        @pl.when(place.s == 0)
+        def _():
+            for i in range(2):
+                done_ends(i)[1].start()
+
+    def done_wait():
+        @pl.when(place.s == 1)
+        def _():
+            for i in range(2):
+                here, there = done_ends(i)
+                here.wait()
+                there.wait_recv()
+
+        @pl.when(place.s == 0)
+        def _():
+            for i in range(2):
+                done_ends(i)[1].wait_send()
+
     def tiny(i):
         return remote(extra.at[i], small_in.at[i], tiny_send.at[i], tiny_recv.at[i], partners[i])
 
@@ -1905,53 +1983,71 @@
                     extra[i, layer, at : at + 1] + small_in[i, layer, other : other + 1]
                 )
 
+    back.take()
+    sums[0].start()
+    for load in loads:
+        load.start()
+    back.swap()
     tiny_start(0)
-    back.take()
-    back.swap()
-    sums[0].start()
+    sums[1].start()
     back.hops(0)
-    for item in sums[1:]:
-        item.start()
+    for line, load in zip(lines, loads):
+        line.resume(load)
     sums[0].load()
+    sums[2].start()
     sums[1].load()
+    sums[3].start()
     tiny_end(0)
     tiny_start(1)
     back.forward(0)
     sums[2].load()
+    done_start()
+    lines[0].line_one()
     sums[0].middle()
     sums[3].load()
+    lines[1].line_one()
     sums[1].middle()
+    lines[0].line_two()
     tiny_end(1)
     tiny_start(2)
     sums[0].gather()
     sums[2].middle()
+    lines[1].line_two()
     sums[1].gather()
-    sums[0].line_one()
     sums[3].middle()
     back.hops(1)
+    lines[0].finish(0, halves[0])
+    sums[0].line_one()
+    sums[2].gather()
     sums[1].line_one()
     tiny_end(2)
     tiny_start(3)
-    sums[2].gather()
+    lines[1].finish(0, halves[1])
+    back.finish(0)
+    sums[3].gather()
     sums[0].line_two()
     sums[2].line_one()
-    sums[3].gather()
     sums[1].line_two()
+    back.forward(1)
     sums[3].line_one()
-    back.forward(1)
     tiny_end(3)
     tiny_start(4)
+    sums[0].finish(1, targets[0])
     sums[2].line_two()
-    sums[0].finish(1, targets[0])
     sums[1].finish(1, targets[1])
     sums[3].line_two()
-    back.finish(0)
+    back.finish(1)
     sums[2].finish(0, targets[2])
-    back.finish(1)
     sums[3].finish(0, targets[3])
     tiny_end(4)
     for item, layer, target in zip(sums, layers, targets):
-        item.drain(layer, target)
+        item.drain_plane()
+        item.drain_line()
+        item.drain_end(layer, target)
+    for item, target in zip(lines, halves):
+        item.drain_line()
+        item.drain_end(0, target)
+    done_wait()
     back.drain()
     for i in range(5):
         tiny(i).wait_send()
@@ -1984,8 +2080,8 @@
     ]
     out = ((2, 4, count, width), low)
     row_piece, tile_piece = (192, width), (width, units // 8)
-    final_a, final_b = ((2, 2) + row_piece, low), ((2, 2) + tile_piece, low)
-    half_b, carry = ((2,) + tile_piece, low), ((4,) + tile_piece, low)
+    final_a, final_b = ((2, 2) + row_piece, low), ((2, width, 2 * tile_piece[1]), low)
+    carry_one, carry, two_tiles = (tile_piece, low), ((4,) + tile_piece, low), ((2,) + tile_piece, low)
     stage = pltpu.VMEM((4, 2, PIECE, width), low)
     dma, gate = pltpu.SemaphoreType.DMA, pltpu.SemaphoreType.REGULAR
     common = (*kept, gains, bias, *tables)
@@ -1997,7 +2093,7 @@
         2,
         (full_a, full_b, seeded, tokens) + common + (low_both,),
         common_spaces + [HBM],
-        grads + [out, half_b, carry],
+        grads + [out, carry_one, carry],
         [HBM] * 2 + [VMEM] + [HBM] * 3,
         backward_buffers(width, units)
         + [stage, stage]
@@ -2007,57 +2103,63 @@
         + spread_sems()
         + sum_sems()
         + sum_sems()
-        + [gate, dma((4,))],
+        + [gate, dma((5,))],
         40_000_000_000,
         80_000_000,
     )
-    prior_a, grad_one, small_one, layer_out, feed_one, carried = second
+    prior_a, grad_one, small_one, layer_out, carried_one, carried = second
     first = call(
         first_kernel,
         "backward_first",
         3,
-        (full_a, full_b, grad_one, tokens) + common + (carried, grad_one),
-        common_spaces + [HBM] * 2,
-        grads + [out, final_b],
-        [HBM] * 2 + [VMEM] + [HBM] * 2,
+        (full_a, full_b, grad_one, tokens) + common + (carried_one, carried, grad_one),
+        common_spaces + [HBM] * 3,
+        grads + [out, two_tiles, two_tiles],
+        [HBM] * 2 + [VMEM] + [HBM] * 3,
         backward_buffers(width, units)
         + [stage]
         + feed_buffers(tile_piece, 2)
-        + sum_buffers(tile_piece, (4, 3, 2))
+        + sum_buffers(tile_piece, (4, 3, 2, 2, 2))
         + backward_sems()
         + spread_sems()
         + sum_sems()
         + sum_sems()
         + sum_sems()
-        + [gate],
+        + sum_sems()
+        + [gate, dma((5,))],
         40_000_000_000,
         80_000_000,
     )
-    grads_a, grad_zero, small_zero, out_one, feed_zero = first
+    grads_a, grad_zero, small_zero, out_one, done, carried = first
     by_shard = (2, 2, 4, 192, width)
     last = call(
         last_kernel,
         "sum_and_spread",
         4,
-        (prior_a.reshape(by_shard), grads_a.reshape(by_shard), grad_zero, small_zero, small_one),
-        [HBM] * 3 + [VMEM] * 2,
-        [out, final_a, ((2, 8, width), full)],
-        [HBM] * 2 + [VMEM],
+        (prior_a.reshape(by_shard), grads_a.reshape(by_shard), done, carried, grad_zero)
+        + (small_zero, small_one),
+        [HBM] * 5 + [VMEM] * 2,
+        [out, final_a, final_b, ((2, 8, width), full)],
+        [HBM] * 3 + [VMEM],
         held
         + held
         + [stage]
         + [pltpu.VMEM((5, 2, 8, width), full), pltpu.VMEM((5, 2, 8, width), full)]
+        + [pltpu.VMEM((2, 2) + tile_piece, low), pltpu.VMEM((2, 2) + tile_piece, low)]
         + sum_sems()
         + sum_sems()
         + sum_sems()
         + sum_sems()
         + spread_sems()
-        + [dma((5,)), dma((5,))],
+        + sum_sems()
+        + sum_sems()
+        + [dma((5,)), dma((5,))]
+        + [dma((2,))] * 4,
         100_000_000,
         40_000_000,
     )
-    out_zero, rows, small = last
-    return layer_out, (out_zero, out_one), rows, (feed_zero, feed_one), small
+    out_zero, final_a, final_b, small = last
+    return layer_out, (out_zero, out_one), final_a, final_b, small
 
 
 def spread(
@@ -2123,15 +2225,13 @@
     )
     full_a, full_b, gains, seeded, tokens, low_both, *kept = forward
     tables = (turn_cos, turn_sin)
-    layer_out, input_grads, final_a, feeds, small = run_backward(
+    layer_out, input_grads, final_a, final_b, small = run_backward(
         full_a, full_b, seeded, tokens, low_both, kept, gains, bias, tables
     )
     input_grad = jnp.where(s == 0, *input_grads)
-    final_b = jnp.stack([jnp.where(s == 0, feeds[0][:, 0], feeds[1]), feeds[0][:, 1]], axis=1)
     small = lax.dynamic_index_in_dim(small, s, 0, keepdims=False)
     final_a, final_b = final_a.astype(jnp.float32), final_b.astype(jnp.float32)
     grad_qkv = jnp.stack([final_a[0, 0].T, final_a[0, 1].T, final_a[1, 0].T], axis=1)
-    grad_up, grad_down = final_b.transpose(0, 2, 1, 3).reshape(2, width, shard)
     out_shape = (1,) + layer_input.shape
     return (
         layer_out.reshape(out_shape),
@@ -2140,9 +2240,9 @@
         grad_qkv[None],
         final_a[1, 1][None],
         small[1:2],
-        grad_up[None],
+        final_b[0][None],
         small[4:5],
-        grad_down.T[None],
+        final_b[1].T[None],
         small[2:3],
     )
 

time: 563 us -> 513 us (0.911)
  Pallas kernels: 511 us -> 466 us
    pallas_call x3, Pallas kernels: 354 us -> 311 us  [call(): pl.pallas_call(kernel, name=name, out_shape=[jax.ShapeDtypeStruct(shape,...]
    another operation x4 -> x1, local copies, waits for them, and re-layouts: 7.57 us -> 0.01 us  [the longest x3 7.56 us: spread(): grad_up, grad_down = final_b.transpose(0, 2, 1, 3).reshape(2, width, shard)]
where the time goes in v1:
time: 513 us; the launch traced here: 504 us
  Pallas kernels  466 us (91%)
  local copies, waits for them, and re-layouts  20.1 us (4%)
  other arithmetic  16.4 us (3%)
    pallas_call x3, Pallas kernels, call(): pl.pallas_call(kernel, name=name, out_shape=[jax.ShapeDtypeStruct(shape,...  311 us
    pallas_call x1, Pallas kernels, run_forward(): pl.pallas_call(forward_kernel, name='forward_layers', out_shape=[shape((2...  155 us
    unnamed x27, local copies, waits for them, and re-layouts  11.2 us

profile of v1, /device:TPU:0, one launch (start us, length us, event | category | flops | bytes accessed | tf_op | source)
XLA Modules:
  0.0 503.5 jit_solution(3509041544572493940)
XLA Ops:
  0.8 0.6 copy-done
  1.3 0.2 reduce-window.8
  1.5 0.1 convert_reduce_fusion
  1.7 0.1 convert_reduce_fusion.1
  1.8 2.8 select_convert_fusion.bias.refs_11_
  4.6 0.3 fusion
  5.0 0.8 copy.36.sine_table.refs_13_
  5.8 0.8 copy.35.cosine.refs_12_
  6.8 0.1 maximum_bitcast_fusion.2
  6.9 1.1 pad_maximum_fusion.own_a
  8.0 0.1 pad.15.clone
  8.1 0.1 maximum_bitcast_fusion.4
  8.2 0.6 pad_maximum_fusion.2.own_c
  8.8 0.6 copy.32
  9.5 0.7 copy.33
  10.2 0.7 copy.34
  11.0 1.7 maximum_bitcast_fusion.own_b
  12.6 154.7 %forward_layers.1 = (bf16[2,2,2,768,768]{4,3,2,1,0:T(8,128)(2,1)}, bf16[2,2,8,768,384]{4,3,2,1,0:T(8,128)(2,1)}, f32[2,8,768]{2,1,0:T(8,128)}, bf16[512,768]{1,0...) custom-call(bf16[8,512,768]{2,1,0:T(8,128)(2,1)} %bitcast.97, ...), custom_call_target="tpu_custom_call" | custom-call | flops 30000001024 | bytes 80000000 | tf_op jit(solution)/shard_map/forward_layers/pallas_call | solution.py:916
  167.4 99.6 %backward_second.1 = (bf16[2,2,768,768]{3,2,1,0:T(8,128)(2,1)}, bf16[512,768]{1,0:T(8,128)(2,1)}, f32[8,768]{1,0:T(8,128)}, bf16[2,4,512,768]{3,2,1,0:T(8,128)(2...) custom-call(bf16[2,2,2,768,768]{4,3,2,1,0:T(8,128)(2,1)} %get-tuple-element.38.refs_0_, ...), custom_call_target="tpu_custom_call" | custom-call | flops 40000000000 | bytes 80000000 | tf_op jit(solution)/shard_map/backward_second/pallas_call | solution.py:2057
  267.0 112.7 %backward_first.1 = (bf16[2,2,768,768]{3,2,1,0:T(8,128)(2,1)}, bf16[512,768]{1,0:T(8,128)(2,1)}, f32[8,768]{1,0:T(8,128)}, bf16[2,4,512,768]{3,2,1,0:T(8,128)(2,...) custom-call(bf16[2,2,2,768,768]{4,3,2,1,0:T(8,128)(2,1)} %get-tuple-element.38.refs_0_, ...), custom_call_target="tpu_custom_call" | custom-call | flops 40000000000 | bytes 80000000 | tf_op jit(solution)/shard_map/backward_first/pallas_call | solution.py:2057
  379.6 98.6 %sum_and_spread.1 = (bf16[2,4,512,768]{3,2,1,0:T(8,128)(2,1)}, bf16[2,2,192,768]{3,2,1,0:T(8,128)(2,1)}, bf16[2,768,768]{2,1,0:T(8,128)(2,1)}, f32[2,8,768]{2,1,0:T(8,128)}) custom-call(bf16[2,2,4,192,768]{4,3,2,1,0:T(8,128)(2,1)} %bitcast.99, bf16[2,2,4,192,768]{4,3,2,1,0:T(8,128)(2,1)} %bitcast.100, bf16[2,768,384]{2,1,0:T(8,128)(2,1)} %get-tuple-element.56.refs_2_, ...), custom_call_target="tpu_custom_call" | custom-call | flops 100000000 | bytes 40000000 | tf_op jit(solution)/shard_map/sum_and_spread/pallas_call | solution.py:2057
  478.3 1.5 convert_element_type.34
  479.7 1.0 slice_bitcast_fusion.1
  480.7 1.3 maximum_bitcast_fusion.1
  482.0 1.0 copy-done.2
  483.0 0.4 convert_element_type.35
  483.4 1.6 slice_bitcast_fusion
  484.9 3.0 copy.41
  488.0 6.1 %broadcast_select_fusion = bf16[2,4,512,768]{3,2,1,0:T(8,128)(2,1)} fusion(bf16[2,4,512,768]{3,2,1,0:T(8,128)(2,1)} %get-tuple-element.61, bf16[2,4,512,768]{3,2,1,0:T(8,128)(2,1)} %get-tuple-element.62, pred[]{:T(512)S(6)} %eq.37), kind=kLoop, calls=%fused_computation | loop fusion | flops 3145728 | bytes 18874368 | tf_op jit(solution)/shard_map/jit(_where)/select_n | solution.py:2231
  494.1 1.6 slice.72
  495.7 1.5 dynamic-slice_bitcast_fusion
  497.2 5.9 %copy.44 = bf16[1,4,2,512,768]{4,3,2,1,0:T(8,128)(2,1)} copy(bf16[1,4,2,512,768]{4,3,2,1,0:T(8,128)(2,1)} %bitcast.86) | data formatting | bytes 12582912
  (37 shorter events, 0.2 us)
Async XLA Ops:
  0.6 0.7 copy-start
  0.7 6.0 %copy-start.5 = (bf16[1,768,3,192]{1,3,2,0:T(8,128)(2,1)S(1)}, bf16[1,768,3,192]{1,3,2,0:T(8,128)(2,1)}, u32[]{:S(2)}) copy-start(bf16[1,768,3,192]{1,3,2,0:T(8,128)(2,1)} %param.15) | copy-start | bytes 2654212
  1.8 5.0 copy-start.6
  6.7 1.4 copy-start.7
  6.7 1.4 copy-start.8
  6.8 1.4 copy-start.9
  6.8 1.3 copy-start.10
  6.8 2.0 copy-start.3
  8.8 1.4 copy-start.4
  480.7 2.3 copy-start.2
  497.2 5.9 %copy-start.1 = (s32[4,2,4]{2,1,0:T(2,128)S(1)}, s32[4,2,4]{2,1,0:T(2,128)}, u32[]{:S(2)}) copy-start(s32[4,2,4]{2,1,0:T(2,128)} %param.13) | copy-start | bytes 388

commit v2 on v1

--- a/solution.py
+++ b/solution.py
@@ -469,7 +469,7 @@
     def one(head, _):
         rows = pl.ds(pl.multiple_of(head * HDIM, HDIM), HDIM)
         query = q_ref[...] * head_mask(head, 0.125).astype(jnp.bfloat16)
-        scores = dot_nt(keys[...], query) + bias[...].astype(jnp.float32)
+        scores = dot_nt(keys[...], query) + bias[...]
         top = jnp.max(scores, axis=0, keepdims=True)
         raised = jnp.exp(scores - top)
         total = jnp.sum(raised, axis=0, keepdims=True)
@@ -479,6 +479,33 @@
 
     lax.fori_loop(0, LANES // HDIM, one, 0)
     return turned[...].T.astype(jnp.bfloat16)
+
+
+def fill_bias(bias, lengths, row, block):
+    ends, total = [], 0
+    for i in range(lengths.shape[1]):
+        total = total + lengths[row, i]
+        ends.append(total)
+
+    def docs_of(base):
+        return sum((base >= end).astype(jnp.int32) for end in ends)
+
+    shape = (PIECE, bias.shape[1])
+    lane = lax.broadcasted_iota(jnp.int32, shape, 1)
+    query_noisy = lane < PIECE
+    query_base = block * PIECE + lane - jnp.where(query_noisy, 0, PIECE)
+    query_doc, query_block = docs_of(query_base), query_base >> 4
+    for i in range(4):
+        start = (block - 2 + min(i, 2)) * PIECE
+        key_base = start + lax.broadcasted_iota(jnp.int32, shape, 0)
+        key_block = key_base >> 4
+        if i == 3:
+            allow = query_noisy & (key_block == query_block)
+        else:
+            later = jnp.where(query_noisy, key_block + 1, key_block)
+            allow = (later <= query_block) & (key_base >= 0)
+        allow = allow & (docs_of(key_base) == query_doc)
+        bias[i * PIECE : (i + 1) * PIECE, :] = jnp.where(allow, 0.0, -1e30)
 
 
 class Weights:
@@ -692,7 +719,7 @@
     own_a,
     own_b,
     own_c,
-    bias,
+    lengths,
     cosine,
     sine_table,
     full_a_out,
@@ -707,6 +734,7 @@
     mid_out,
     hid_out,
     lse_out,
+    bias_out,
     full_a,
     full_b,
     full_c,
@@ -721,6 +749,7 @@
     lse,
     values_turned,
     turned_att,
+    bias,
     *sems,
 ):
     weight_sems, key_sems = sems[:7], sems[7:11]
@@ -755,6 +784,9 @@
         weights.wait_own(layer, 3, place.core)
     gains = full_c.at[:, 0, 0]
     gains_out[...] = full_c[:, 0, 0]
+    fill_bias(bias, lengths, 4 * place.group + place.t, 2 * place.half + place.s)
+    bias_save = pltpu.make_async_copy(bias, bias_out, save_sem.at[17])
+    bias_save.start()
     weights.forward(0, 0)
     own_tokens.wait()
     swap.wait()
@@ -902,11 +934,12 @@
             copy.wait()
         KeyShare(place, kv, layer, key_sems).drain()
     weights.drain()
+    bias_save.wait()
     own_seed.wait()
     seed_swap.wait()
 
 
-def run_forward(tokens, cotangent, own_a, own_b, own_c, bias, cosine, sine_table):
+def run_forward(tokens, cotangent, own_a, own_b, own_c, lengths, cosine, sine_table):
     shape = jax.ShapeDtypeStruct
     low_type, full_type = jnp.bfloat16, jnp.float32
     count = 2 * PIECE
@@ -929,9 +962,10 @@
             shape((2, count, width), full_type),
             shape((2, count, units), low_type),
             shape((2, 24, count), full_type),
+            shape((4 * PIECE, count), full_type),
         ],
-        in_specs=[HBM] * 5 + [VMEM] * 3,
-        out_specs=[HBM] * 2 + [VMEM] + [HBM] * 9,
+        in_specs=[HBM] * 5 + [pl.BlockSpec(memory_space=pltpu.SMEM)] + [VMEM] * 2,
+        out_specs=[HBM] * 2 + [VMEM] + [HBM] * 10,
         scratch_shapes=[
             pltpu.VMEM((2, 2, 2, width, width), low_type),
             pltpu.VMEM((2, 2, 8, width, units // 8), low_type),
@@ -947,6 +981,7 @@
             pltpu.VMEM((24, count), full_type),
             pltpu.VMEM((LANES, 4 * PIECE), low_type),
             pltpu.VMEM((LANES, PIECE), full_type),
+            pltpu.VMEM((4 * PIECE, count), full_type),
             dma((4, 2)),
             dma((4, 2)),
             dma((4, 2)),
@@ -964,7 +999,7 @@
             dma,
             dma,
             dma,
-            dma((17,)),
+            dma((18,)),
         ],
         compiler_params=pltpu.CompilerParams(
             collective_id=1, has_side_effects=True, vmem_limit_bytes=62 * 1024 * 1024
@@ -972,7 +1007,7 @@
         cost_estimate=pl.CostEstimate(
             flops=30_000_000_000, bytes_accessed=80_000_000, transcendentals=20_000_000
         ),
-    )(tokens, cotangent, own_a, own_b, own_c, bias, cosine, sine_table)
+    )(tokens, cotangent, own_a, own_b, own_c, lengths, cosine, sine_table)
 
 
 def low_sum(*parts):
@@ -1485,20 +1520,26 @@
 def attention_back(q_ref, grad_ref, att_ref, keys, values, keys_turned, bias, lse, sums, turned, count):
     turned[...] = (grad_ref[...].astype(jnp.float32) * att_ref[...].astype(jnp.float32)).T
 
-    def one(head, _):
+    def head_terms(head):
         rows = pl.ds(pl.multiple_of(head * HDIM, HDIM), HDIM)
         query = q_ref[...] * head_mask(head, 0.125).astype(jnp.bfloat16)
         grad = grad_ref[...] * head_mask(head, 1.0).astype(jnp.bfloat16)
         delta = jnp.sum(turned[rows, :], axis=0, keepdims=True)
-        scores = dot_nt(keys[...], query) + bias[...].astype(jnp.float32)
+        scores = dot_nt(keys[...], query) + bias[...]
         probs = jnp.exp(scores - lse[pl.ds(head, 1), :])
         grad_scores = (probs * (dot_nt(values[...], grad) - delta)).astype(jnp.bfloat16)
+        turned[rows, :] = dot_nn(keys_turned[rows, :], grad_scores) * 0.125
+        return query, grad, grad_scores, probs.astype(jnp.bfloat16)
+
+    def one(pair, _):
+        left, right = head_terms(2 * pair), head_terms(2 * pair + 1)
+        query, grad = (jnp.concatenate([left[i], right[i]], axis=0) for i in (0, 1))
+        grad_scores, probs = (jnp.concatenate([left[i], right[i]], axis=1) for i in (2, 3))
         sums[0, :count] += dot_nn(grad_scores, query)
-        sums[1, :count] += dot_nn(probs.astype(jnp.bfloat16), grad)
-        turned[rows, :] = dot_nn(keys_turned[rows, :], grad_scores) * 0.125
+        sums[1, :count] += dot_nn(probs, grad)
         return 0
 
-    lax.fori_loop(0, LANES // HDIM, one, 0)
+    lax.fori_loop(0, LANES // HDIM // 2, one, 0)
     q_ref[...] = turned[...].T.astype(jnp.bfloat16)
 
 
@@ -1514,8 +1555,8 @@
         mid_in,
         hid_in,
         lse_in,
+        bias_in,
         gains,
-        bias,
         cosine,
         sine_table,
         grads_a,
@@ -1541,6 +1582,7 @@
         grad_turned,
         normed_turned,
         lse,
+        bias,
     ) = refs
     share = KeyReturn(place, kv, near_in, far_in, key_sems)
     pairs = [
@@ -1553,6 +1595,7 @@
         (kv_in.at[layer], kv),
         (x_in, low),
         (lse_in.at[layer], lse),
+        (bias_in, bias),
     ]
     loads = [pltpu.make_async_copy(a, b, sems.at[i]) for i, (a, b) in enumerate(pairs)]
     def tile_copy(pack, tile):
@@ -1772,6 +1815,7 @@
         pltpu.VMEM((width, count), low),
         pltpu.VMEM((width, count), low),
         pltpu.VMEM((24, count), full),
+        pltpu.VMEM((4 * PIECE, count), full),
     ]
 
 
@@ -1780,7 +1824,7 @@
     return [dma((3,))] * 6 + [dma((12,)), dma((2, 8))]
 
 
-BUFFERS = 20
+BUFFERS = 21
 
 
 def later(step, *args):
@@ -1790,7 +1834,7 @@
 def second_kernel(*refs):
     ins, refs = refs[:15], refs[15:]
     (grads_a, grad_out, small_out, out, carry_one, carry), refs = refs[:6], refs[6:]
-    buffers, stages, feed, refs = refs[:BUFFERS], refs[BUFFERS : BUFFERS + 2], refs[22:24], refs[24:]
+    buffers, stages, feed, refs = refs[:BUFFERS], refs[BUFFERS : BUFFERS + 2], refs[23:25], refs[25:]
     sems, feed_sem, gate, carry_sem = refs[:24], refs[24:-2], refs[-2], refs[-1]
     low_both = ins[14]
     place = Place()
@@ -1985,61 +2029,61 @@
 
     back.take()
     sums[0].start()
+    back.swap()
+    sums[1].start()
     for load in loads:
         load.start()
-    back.swap()
     tiny_start(0)
-    sums[1].start()
     back.hops(0)
-    for line, load in zip(lines, loads):
-        line.resume(load)
+    lines[0].resume(loads[0])
     sums[0].load()
     sums[2].start()
+    back.forward(0)
+    tiny_end(0)
+    tiny_start(1)
+    lines[1].resume(loads[1])
     sums[1].load()
     sums[3].start()
-    tiny_end(0)
-    tiny_start(1)
-    back.forward(0)
-    sums[2].load()
-    done_start()
+    sums[0].middle()
     lines[0].line_one()
-    sums[0].middle()
-    sums[3].load()
-    lines[1].line_one()
-    sums[1].middle()
-    lines[0].line_two()
     tiny_end(1)
     tiny_start(2)
+    sums[2].load()
     sums[0].gather()
-    sums[2].middle()
-    lines[1].line_two()
+    back.finish(0)
+    sums[1].middle()
+    back.hops(1)
     sums[1].gather()
-    sums[3].middle()
-    back.hops(1)
-    lines[0].finish(0, halves[0])
-    sums[0].line_one()
-    sums[2].gather()
-    sums[1].line_one()
     tiny_end(2)
     tiny_start(3)
-    lines[1].finish(0, halves[1])
-    back.finish(0)
-    sums[3].gather()
-    sums[0].line_two()
-    sums[2].line_one()
-    sums[1].line_two()
+    sums[3].load()
+    sums[2].middle()
+    lines[1].line_one()
+    done_start()
+    lines[0].line_two()
+    sums[2].gather()
     back.forward(1)
-    sums[3].line_one()
+    sums[3].middle()
+    sums[0].line_one()
     tiny_end(3)
     tiny_start(4)
+    sums[3].gather()
+    sums[1].line_one()
+    back.finish(1)
+    lines[1].line_two()
+    lines[0].finish(0, halves[0])
+    sums[2].line_one()
+    sums[0].line_two()
+    tiny_end(4)
+    sums[3].line_one()
+    sums[1].line_two()
     sums[0].finish(1, targets[0])
     sums[2].line_two()
+    lines[1].finish(0, halves[1])
     sums[1].finish(1, targets[1])
     sums[3].line_two()
-    back.finish(1)
     sums[2].finish(0, targets[2])
     sums[3].finish(0, targets[3])
-    tiny_end(4)
     for item, layer, target in zip(sums, layers, targets):
         item.drain_plane()
         item.drain_line()
@@ -2070,7 +2114,93 @@
     )(*ins)
 
 
-def run_backward(full_a, full_b, seeded, tokens, low_both, kept, gains, bias, tables):
+def results_kernel(*refs):
+    layer_raw, zero_raw, one_raw, final_a, final_b = refs[:5]
+    layer_out, input_grad, grad_out, grad_up, grad_down = refs[5:10]
+    rows, turned, part, tiles, converted, row_sem, tile_sem = refs[10:]
+    s = lax.axis_index("section")
+    count = rows.shape[0] // 2
+
+    def load(i):
+        sem = row_sem.at[0, i]
+        if i < count:
+            return [pltpu.make_async_copy(layer_raw.at[i // 4, i % 4], rows.at[i], sem)] * 2
+        at = i - count
+        return [
+            pltpu.make_async_copy(raw.at[at // 4, at % 4], rows.at[i], sem) for raw in (zero_raw, one_raw)
+        ]
+
+    def store(i):
+        target, at = (layer_out, i) if i < count else (input_grad, i - count)
+        return pltpu.make_async_copy(rows.at[i], target.at[at // 4, at % 4], row_sem.at[1, i])
+
+    loads = [
+        pltpu.make_async_copy(final_b.at[0], tiles.at[0], tile_sem.at[0]),
+        pltpu.make_async_copy(final_b.at[1], tiles.at[1], tile_sem.at[1]),
+        pltpu.make_async_copy(final_a.at[1, 1], part, tile_sem.at[2]),
+    ]
+    stores = [
+        pltpu.make_async_copy(converted, grad_up, tile_sem.at[3]),
+        pltpu.make_async_copy(turned, grad_down, tile_sem.at[4]),
+    ]
+    for copy in loads:
+        copy.start()
+    for i in range(count):
+        load(i)[0].start()
+
+    @pl.when(s == 0)
+    def _():
+        for i in range(count, 2 * count):
+            load(i)[0].start()
+
+    @pl.when(s != 0)
+    def _():
+        for i in range(count, 2 * count):
+            load(i)[1].start()
+
+    for copy in loads:
+        copy.wait()
+    converted[...] = tiles[0].astype(jnp.float32)
+    stores[0].start()
+    grad_out[...] = part[...].astype(jnp.float32)
+    turned[...] = tiles[1].astype(jnp.float32).T
+    stores[1].start()
+    for i in range(2 * count):
+        load(i)[0].wait()
+        store(i).start()
+    for i in range(2 * count):
+        store(i).wait()
+    for copy in stores:
+        copy.wait()
+
+
+def run_results(layer_raw, zero_raw, one_raw, final_a, final_b):
+    full = jnp.float32
+    width = final_b.shape[-1]
+    big = jax.ShapeDtypeStruct(layer_raw.shape, layer_raw.dtype)
+    square = jax.ShapeDtypeStruct((width, width), full)
+    dma = pltpu.SemaphoreType.DMA
+    return pl.pallas_call(
+        results_kernel,
+        name="place_results",
+        out_shape=[big, big, jax.ShapeDtypeStruct((192, width), full), square, square],
+        in_specs=[HBM] * 5,
+        out_specs=[HBM] * 2 + [VMEM] + [HBM] * 2,
+        scratch_shapes=[
+            pltpu.VMEM((16,) + layer_raw.shape[2:], jnp.bfloat16),
+            pltpu.VMEM((width, width), full),
+            pltpu.VMEM((192, width), jnp.bfloat16),
+            pltpu.VMEM((2, width, width), jnp.bfloat16),
+            pltpu.VMEM((width, width), full),
+            dma((2, 16)),
+            dma((5,)),
+        ],
+        compiler_params=pltpu.CompilerParams(vmem_limit_bytes=48 * 1024 * 1024),
+        cost_estimate=pl.CostEstimate(flops=1_000_000, bytes_accessed=35_000_000, transcendentals=0),
+    )(layer_raw, zero_raw, one_raw, final_a, final_b)
+
+
+def run_backward(full_a, full_b, seeded, tokens, low_both, kept, gains, tables):
     low, full, count = jnp.bfloat16, jnp.float32, 2 * PIECE
     width, units = full_a.shape[-1], 8 * full_b.shape[-1]
     grads = [
@@ -2084,8 +2214,8 @@
     carry_one, carry, two_tiles = (tile_piece, low), ((4,) + tile_piece, low), ((2,) + tile_piece, low)
     stage = pltpu.VMEM((4, 2, PIECE, width), low)
     dma, gate = pltpu.SemaphoreType.DMA, pltpu.SemaphoreType.REGULAR
-    common = (*kept, gains, bias, *tables)
-    common_spaces = [HBM] * 10 + [VMEM] * 4
+    common = (*kept, gains, *tables)
+    common_spaces = [HBM] * 11 + [VMEM] * 3
     held = sum_buffers(row_piece, (4, 4, 3, 2) * 2)
     second = call(
         second_kernel,
@@ -2190,47 +2320,29 @@
     gains = jnp.concatenate([ln1_gain, ln2_gain, b_down, jnp.zeros((5, width), jnp.float32)])
     own_c = jnp.stack([gains, jnp.concatenate([b_up, jnp.zeros((7, width), jnp.float32)])])
 
-    block = 2 * half + s
+    lane = jnp.arange(128)
+    block_base = (2 * half + s) * PIECE
+    query_base = block_base + jnp.arange(2 * PIECE) % PIECE
+    frequency = 10000.0 ** (-(lane % (HDIM // 2)).astype(jnp.float32) * 2.0 / HDIM)
+    angles = query_base.astype(jnp.float32)[:, None] * frequency[None, :]
+    sign = jnp.where(lane % HDIM < HDIM // 2, -1.0, 1.0)
+    turn_cos, turn_sin = jnp.cos(angles), jnp.sin(angles) * sign
+
     lengths = doc_lengths.reshape(micros * rows, -1)
-    lengths = lax.dynamic_index_in_dim(lengths, 4 * group + t, 0, keepdims=False)
-    ends = jnp.cumsum(lengths)
-    piece_pos = jnp.arange(PIECE)
-    query_base = jnp.tile(block * PIECE + piece_pos, 2)
-    key_base = jnp.concatenate([(block - 2 + i) * PIECE + piece_pos for i in (0, 1, 2, 2)])
-    query_noisy = jnp.arange(2 * PIECE) < PIECE
-    key_noisy = jnp.arange(4 * PIECE) >= 3 * PIECE
-
-    def docs_of(base):
-        return jnp.sum((base[:, None] >= ends[None, :]).astype(jnp.int32), axis=-1)
-
-    query_block, key_block = query_base[None, :] // BLOCK, key_base[:, None] // BLOCK
-    query_kind, key_kind = query_noisy[None, :], key_noisy[:, None]
-    mask = (
-        (query_kind & key_kind & (query_block == key_block))
-        | (query_kind & ~key_kind & (key_block < query_block))
-        | (~query_kind & ~key_kind & (key_block <= query_block))
-    )
-    mask = mask & (docs_of(query_base)[None, :] == docs_of(key_base)[:, None])
-    mask = mask & (key_base >= 0)[:, None]
-    bias = jnp.where(mask, 0.0, -1e30).astype(jnp.bfloat16)
-    frequency = 10000.0 ** (-jnp.arange(HDIM // 2).astype(jnp.float32) * 2.0 / HDIM)
-    angles = query_base.astype(jnp.float32)[:, None] * frequency[None, :]
-    cosine, sine_table = jnp.cos(angles), jnp.sin(angles)
-    turn_cos = jnp.tile(cosine, (1, 4))
-    turn_sin = jnp.tile(jnp.concatenate([-sine_table, sine_table], axis=1), (1, 2))
-
     flat = (micros * rows, width_pos, width)
     forward = run_forward(
-        layer_input.reshape(flat), cotangent.reshape(flat), own_a, own_b, own_c, bias, turn_cos, turn_sin
+        layer_input.reshape(flat), cotangent.reshape(flat), own_a, own_b, own_c, lengths, turn_cos, turn_sin
     )
     full_a, full_b, gains, seeded, tokens, low_both, *kept = forward
     tables = (turn_cos, turn_sin)
-    layer_out, input_grads, final_a, final_b, small = run_backward(
-        full_a, full_b, seeded, tokens, low_both, kept, gains, bias, tables
-    )
-    input_grad = jnp.where(s == 0, *input_grads)
+    layer_raw, input_raws, final_a, final_b, small = run_backward(
+        full_a, full_b, seeded, tokens, low_both, kept, gains, tables
+    )
+    layer_out, input_grad, grad_out, grad_up, grad_down = run_results(
+        layer_raw, *input_raws, final_a, final_b
+    )
     small = lax.dynamic_index_in_dim(small, s, 0, keepdims=False)
-    final_a, final_b = final_a.astype(jnp.float32), final_b.astype(jnp.float32)
+    final_a = final_a.astype(jnp.float32)
     grad_qkv = jnp.stack([final_a[0, 0].T, final_a[0, 1].T, final_a[1, 0].T], axis=1)
     out_shape = (1,) + layer_input.shape
     return (
@@ -2238,11 +2350,11 @@
         input_grad.reshape(out_shape),
         small[0:1],
         grad_qkv[None],
-        final_a[1, 1][None],
+        grad_out[None],
         small[1:2],
-        final_b[0][None],
+        grad_up[None],
         small[4:5],
-        final_b[1].T[None],
+        grad_down[None],
         small[2:3],
     )
 

time: 513 us -> 518 us (level)
  Pallas kernels: 466 us -> 494 us
  local copies, waits for them, and re-layouts: 20.1 us -> 6.37 us
  other arithmetic: 16.4 us -> 8.22 us
    pallas_call x3, Pallas kernels: 311 us -> 327 us  [call(): pl.pallas_call(kernel, name=name, out_shape=[jax.ShapeDtypeStruct(shape,...]
    pallas_call x0 -> x1, Pallas kernels: none -> 12.2 us  [run_results(): pl.pallas_call(results_kernel, name='place_results', out_shape=[big, big,...]
    unnamed x27 -> x19, local copies, waits for them, and re-layouts: 11.2 us -> 2.01 us
    select_n x3 -> x1, other arithmetic: 6.17 us -> 0.01 us  [spread(): sign = jnp.where(lane % HDIM < HDIM // 2, -1.0, 1.0)]
where the time goes in v2:
time: 518 us; the launch traced here: 510 us
  Pallas kernels  494 us (95%)
  other arithmetic  8.22 us (2%)
  local copies, waits for them, and re-layouts  6.37 us (1%)
    pallas_call x3, Pallas kernels, call(): pl.pallas_call(kernel, name=name, out_shape=[jax.ShapeDtypeStruct(shape,...  327 us
    pallas_call x1, Pallas kernels, run_forward(): pl.pallas_call(forward_kernel, name='forward_layers', out_shape=[shape((2...  155 us
    pallas_call x1, Pallas kernels, run_results(): pl.pallas_call(results_kernel, name='place_results', out_shape=[big, big,...  12.2 us

profile of v2, /device:TPU:0, one launch (start us, length us, event | category | flops | bytes accessed | tf_op | source)
XLA Modules:
  0.0 509.9 jit_solution(12991346087555431384)
XLA Ops:
  0.6 0.0 copy-start.4
  0.7 1.8 fusion
  2.5 1.2 slice_bitcast_fusion.5
  3.7 0.0 copy-done.4
  3.7 0.0 copy-start.5
  3.7 0.0 copy-start.6
  3.8 0.0 copy-start.7
  3.8 0.0 copy-start.8
  3.8 0.0 copy-start.2
  3.8 0.1 maximum_bitcast_fusion.2
  3.9 1.1 pad_maximum_fusion.own_a
  5.0 0.1 pad.9.clone
  5.1 0.0 copy-done.5
  5.1 0.0 copy-done.6
  5.1 0.0 copy-done.7
  5.1 0.1 maximum_bitcast_fusion.4
  5.2 0.6 pad_maximum_fusion.1.own_c
  5.8 0.6 copy.21
  6.5 0.7 copy.22
  7.2 0.7 copy.23
  8.0 1.7 maximum_bitcast_fusion.own_b
  9.6 154.7 %forward_layers.1 = (bf16[2,2,2,768,768]{4,3,2,1,0:T(8,128)(2,1)}, bf16[2,2,8,768,384]{4,3,2,1,0:T(8,128)(2,1)}, f32[2,8,768]{2,1,0:T(8,128)}, bf16[512,768]{1,0...) custom-call(bf16[8,512,768]{2,1,0:T(8,128)(2,1)} %bitcast.74, ...), custom_call_target="tpu_custom_call" | custom-call | flops 30000001024 | bytes 80000000 | tf_op jit(solution)/shard_map/forward_layers/pallas_call | solution.py:949
  164.3 100.1 %backward_second.1 = (bf16[2,2,768,768]{3,2,1,0:T(8,128)(2,1)}, bf16[512,768]{1,0:T(8,128)(2,1)}, f32[8,768]{1,0:T(8,128)}, bf16[2,4,512,768]{3,2,1,0:T(8,128)(2...) custom-call(bf16[2,2,2,768,768]{4,3,2,1,0:T(8,128)(2,1)} %get-tuple-element.44.refs_0_, ...), custom_call_target="tpu_custom_call" | custom-call | flops 40000000000 | bytes 80000000 | tf_op jit(solution)/shard_map/backward_second/pallas_call | solution.py:2101
  264.4 110.4 %backward_first.1 = (bf16[2,2,768,768]{3,2,1,0:T(8,128)(2,1)}, bf16[512,768]{1,0:T(8,128)(2,1)}, f32[8,768]{1,0:T(8,128)}, bf16[2,4,512,768]{3,2,1,0:T(8,128)(2,...) custom-call(bf16[2,2,2,768,768]{4,3,2,1,0:T(8,128)(2,1)} %get-tuple-element.44.refs_0_, ...), custom_call_target="tpu_custom_call" | custom-call | flops 40000000000 | bytes 80000000 | tf_op jit(solution)/shard_map/backward_first/pallas_call | solution.py:2101
  374.8 116.9 %sum_and_spread.1 = (bf16[2,4,512,768]{3,2,1,0:T(8,128)(2,1)}, bf16[2,2,192,768]{3,2,1,0:T(8,128)(2,1)}, bf16[2,768,768]{2,1,0:T(8,128)(2,1)}, f32[2,8,768]{2,1,0:T(8,128)}) custom-call(bf16[2,2,4,192,768]{4,3,2,1,0:T(8,128)(2,1)} %bitcast.82, bf16[2,2,4,192,768]{4,3,2,1,0:T(8,128)(2,1)} %bitcast.83, bf16[2,768,384]{2,1,0:T(8,128)(2,1)} %get-tuple-element.63.refs_2_, ...), custom_call_target="tpu_custom_call" | custom-call | flops 100000000 | bytes 40000000 | tf_op jit(solution)/shard_map/sum_and_spread/pallas_call | solution.py:2101
  491.7 1.5 convert_element_type.19
  493.2 0.1 slice_bitcast_fusion.2
  493.3 1.3 maximum_bitcast_fusion.1
  494.6 0.4 copy-done
  495.1 0.9 copy-done.1
  496.0 12.2 %place_results.1 = (bf16[2,4,512,768]{3,2,1,0:T(8,128)(2,1)}, bf16[2,4,512,768]{3,2,1,0:T(8,128)(2,1)}, f32[192,768]{1,0:T(8,128)}, f32[768,768]{1,0:T(8,128)}, f32[768,768]{1,0:T(8,128)}) custom-call(bf16[2,4,512,768]{3,2,1,0:T(8,128)(2,1)} %get-tuple-element.57.refs_0_, bf16[2,4,512,768]{3,2,1,0:T(8,128)(2,1)} %get-tuple-element.68.refs_1_, ...), custom_call_target="tpu_custom_call" | custom-call | flops 1000000 | bytes 35000000 | tf_op jit(solution)/shard_map/place_results/pallas_call | solution.py:2183
  508.2 1.5 dynamic-slice_bitcast_fusion
  (9 shorter events, 0.0 us)
Async XLA Ops:
  0.6 3.1 copy-start.4
  3.7 1.4 copy-start.5
  3.7 1.4 copy-start.6
  3.8 1.4 copy-start.7
  3.8 1.3 copy-start.8
  3.8 2.0 copy-start.2
  5.8 1.4 copy-start.3
  493.3 1.8 copy-start
  493.3 2.7 copy-start.1

commit v3 on v2

--- a/solution.py
+++ b/solution.py
@@ -508,6 +508,9 @@
         bias[i * PIECE : (i + 1) * PIECE, :] = jnp.where(allow, 0.0, -1e30)
 
 
+SHARED = ((0, 2), (1, 1))
+
+
 class Weights:
     def __init__(self, place, own, full, sems):
         self.place, self.own, self.full = place, own, full
@@ -519,6 +522,10 @@
             self.hop_recv,
             self.chip_send,
             self.chip_recv,
+            self.twin_send,
+            self.twin_recv,
+            self.late_send,
+            self.late_recv,
         ) = sems
 
     def source(self, chunk, pack):
@@ -565,12 +572,17 @@
         def _():
             there.wait_recv()
 
+    def half_of(self, layer, chunk, rel, half):
+        piece = self.piece(layer, chunk, self.place.s, rel)
+        if (layer, chunk) not in SHARED:
+            return piece
+        return piece.at[pl.ds(pl.multiple_of(half * 384, 128), 384)]
+
     def hops(self, layer, chunk):
         place = self.place
-        own = self.piece(layer, chunk, place.s, 0)
-        first = self.piece(layer, chunk, place.s, place.rel_one)
-        second = self.piece(layer, chunk, place.s, place.rel_two)
-        third = self.piece(layer, chunk, place.s, 3)
+        own, first, second, third = (
+            self.half_of(layer, chunk, rel, place.half) for rel in (0, place.rel_one, place.rel_two, 3)
+        )
         moves = ((own, first, place.hop_one), (own, second, place.hop_two), (first, third, place.hop_two))
         return [
             remote(
@@ -583,18 +595,39 @@
             for i, (source, target, column) in enumerate(moves)
         ]
 
+    def passes(self, layer, chunk, half, device, send, receive):
+        place = self.place
+        found = []
+        for i, rel in enumerate((place.rel_one, place.rel_two, 3)):
+            piece = self.half_of(layer, chunk, rel, half)
+            sems = send.at[layer, chunk, i], receive.at[layer, chunk, i]
+            found.append(remote(piece, piece, *sems, device))
+        return found
+
     def chips(self, layer, chunk):
         place = self.place
-        return [
-            remote(
-                self.piece(layer, chunk, place.s, rel),
-                self.piece(layer, chunk, place.s, rel),
-                self.chip_send.at[layer, chunk, i],
-                self.chip_recv.at[layer, chunk, i],
-                place.on(section=place.core),
-            )
-            for i, rel in enumerate((place.rel_one, place.rel_two, 3))
-        ]
+        device = place.on(section=place.core)
+        return self.passes(layer, chunk, place.half, device, self.chip_send, self.chip_recv)
+
+    def twins(self, layer, chunk):
+        place = self.place
+        device = place.on(seq=place.twin)
+        return self.passes(layer, chunk, place.half, device, self.twin_send, self.twin_recv)
+
+    def twins_in(self, layer, chunk):
+        place = self.place
+        device = place.on(seq=place.twin)
+        return self.passes(layer, chunk, 1 - place.half, device, self.twin_send, self.twin_recv)
+
+    def lates(self, layer, chunk):
+        place = self.place
+        device = place.on(section=place.core)
+        return self.passes(layer, chunk, 1 - place.half, device, self.late_send, self.late_recv)
+
+    def onward(self, layer, chunk, i):
+        self.chips(layer, chunk)[i].start()
+        if (layer, chunk) in SHARED:
+            self.twins(layer, chunk)[i].start()
 
     def begin(self, layer, chunk):
         self.wait_own(layer, chunk, self.place.s)
@@ -604,29 +637,39 @@
 
     def forward(self, layer, chunk):
         first, second, third = self.hops(layer, chunk)
-        chips = self.chips(layer, chunk)
         first.wait_recv()
         third.start()
-        chips[0].start()
+        self.onward(layer, chunk, 0)
         second.wait_recv()
-        chips[1].start()
+        self.onward(layer, chunk, 1)
 
     def finish(self, layer, chunk):
         self.hops(layer, chunk)[2].wait_recv()
-        self.chips(layer, chunk)[2].start()
+        self.onward(layer, chunk, 2)
+
+    def complete(self, layer, chunk):
+        for arrived, late in zip(self.twins_in(layer, chunk), self.lates(layer, chunk)):
+            arrived.wait_recv()
+            late.start()
 
     def need(self, layer, chunk):
         if chunk < 3:
             self.wait_own(layer, chunk, self.place.core)
         for copy in self.chips(layer, chunk):
             copy.wait_recv()
+        if (layer, chunk) in SHARED:
+            for copy in self.lates(layer, chunk):
+                copy.wait_recv()
 
     def drain(self):
         for chunk in range(4):
             for pack in range(2):
                 self.own_copies(chunk, pack)[1].wait_send()
             for layer in range(2):
-                for copy in self.hops(layer, chunk) + self.chips(layer, chunk):
+                sent = self.hops(layer, chunk) + self.chips(layer, chunk)
+                if (layer, chunk) in SHARED:
+                    sent += self.twins(layer, chunk) + self.lates(layer, chunk)
+                for copy in sent:
                     copy.wait_send()
 
 
@@ -752,8 +795,8 @@
     bias,
     *sems,
 ):
-    weight_sems, key_sems = sems[:7], sems[7:11]
-    token_sem, swap_send, swap_recv, seed_sem, seed_send, seed_recv, save_sem = sems[11:]
+    weight_sems, key_sems = sems[:11], sems[11:15]
+    token_sem, swap_send, swap_recv, seed_sem, seed_send, seed_recv, save_sem = sems[15:]
     place = Place()
     weights = Weights(place, (own_a, own_b, own_c), (full_a, full_b, full_c), weight_sems)
     lse[...] = jnp.zeros_like(lse)
@@ -881,6 +924,7 @@
                     weights.finish(1, 1)
                 elif part == 2:
                     weights.forward(1, 2)
+                    weights.complete(1, 1)
         for copy in saves(layer)[1:4] + saves(layer)[6:]:
             copy.start()
 
@@ -896,10 +940,13 @@
         saves(layer)[4].start()
         weights.need(layer, 3)
         for part in range(2):
-            if part == 1:
-                weights.finish(layer, 2)
-                if layer == 0:
-                    weights.begin(1, 1)
+            if part == 0 and layer == 0:
+                weights.finish(0, 2)
+                weights.begin(1, 1)
+            elif part == 1 and layer == 0:
+                weights.complete(0, 2)
+            elif part == 1:
+                weights.finish(1, 2)
             weights.need(layer, part + 1)
             if part == 1:
                 for copy in weight_saves(layer)[2:]:
@@ -985,6 +1032,10 @@
             dma((4, 2)),
             dma((4, 2)),
             dma((4, 2)),
+            dma((2, 4, 3)),
+            dma((2, 4, 3)),
+            dma((2, 4, 3)),
+            dma((2, 4, 3)),
             dma((2, 4, 3)),
             dma((2, 4, 3)),
             dma((2, 4, 3)),
@@ -2029,61 +2080,61 @@
 
     back.take()
     sums[0].start()
-    back.swap()
-    sums[1].start()
     for load in loads:
         load.start()
+    back.swap()
     tiny_start(0)
+    sums[1].start()
     back.hops(0)
-    lines[0].resume(loads[0])
+    for line, load in zip(lines, loads):
+        line.resume(load)
     sums[0].load()
     sums[2].start()
-    back.forward(0)
+    sums[1].load()
+    sums[3].start()
     tiny_end(0)
     tiny_start(1)
-    lines[1].resume(loads[1])
-    sums[1].load()
-    sums[3].start()
+    back.forward(0)
+    sums[2].load()
+    done_start()
+    lines[0].line_one()
     sums[0].middle()
-    lines[0].line_one()
+    sums[3].load()
+    lines[1].line_one()
+    sums[1].middle()
+    lines[0].line_two()
     tiny_end(1)
     tiny_start(2)
-    sums[2].load()
     sums[0].gather()
-    back.finish(0)
-    sums[1].middle()
+    sums[2].middle()
+    lines[1].line_two()
+    sums[1].gather()
+    sums[3].middle()
     back.hops(1)
-    sums[1].gather()
+    lines[0].finish(0, halves[0])
+    sums[0].line_one()
+    sums[2].gather()
+    sums[1].line_one()
     tiny_end(2)
     tiny_start(3)
-    sums[3].load()
-    sums[2].middle()
-    lines[1].line_one()
-    done_start()
-    lines[0].line_two()
-    sums[2].gather()
+    lines[1].finish(0, halves[1])
+    back.finish(0)
+    sums[3].gather()
+    sums[0].line_two()
+    sums[2].line_one()
+    sums[1].line_two()
     back.forward(1)
-    sums[3].middle()
-    sums[0].line_one()
+    sums[3].line_one()
     tiny_end(3)
     tiny_start(4)
-    sums[3].gather()
-    sums[1].line_one()
-    back.finish(1)
-    lines[1].line_two()
-    lines[0].finish(0, halves[0])
-    sums[2].line_one()
-    sums[0].line_two()
-    tiny_end(4)
-    sums[3].line_one()
-    sums[1].line_two()
     sums[0].finish(1, targets[0])
     sums[2].line_two()
-    lines[1].finish(0, halves[1])
     sums[1].finish(1, targets[1])
     sums[3].line_two()
+    back.finish(1)
     sums[2].finish(0, targets[2])
     sums[3].finish(0, targets[3])
+    tiny_end(4)
     for item, layer, target in zip(sums, layers, targets):
         item.drain_plane()
         item.drain_line()

time: 518 us -> 515 us (level)
    pallas_call x3, Pallas kernels: 327 us -> 319 us  [call(): pl.pallas_call(kernel, name=name, out_shape=[jax.ShapeDtypeStruct(shape,...]
    pallas_call x1, Pallas kernels: 155 us -> 160 us  [run_forward(): pl.pallas_call(forward_kernel, name='forward_layers', out_shape=[shape((2...]
where the time goes in v3:
time: 515 us; the launch traced here: 507 us
  Pallas kernels  492 us (96%)
  other arithmetic  8.22 us (2%)
  local copies, waits for them, and re-layouts  6.37 us (1%)
    pallas_call x3, Pallas kernels, call(): pl.pallas_call(kernel, name=name, out_shape=[jax.ShapeDtypeStruct(shape,...  319 us
    pallas_call x1, Pallas kernels, run_forward(): pl.pallas_call(forward_kernel, name='forward_layers', out_shape=[shape((2...  160 us
    pallas_call x1, Pallas kernels, run_results(): pl.pallas_call(results_kernel, name='place_results', out_shape=[big, big,...  12.2 us

profile of v3, /device:TPU:0, one launch (start us, length us, event | category | flops | bytes accessed | tf_op | source)
XLA Modules:
  0.0 507.2 jit_solution(11148424088081337746)
XLA Ops:
  0.6 0.0 copy-start.4
  0.7 1.8 fusion
  2.5 1.2 slice_bitcast_fusion.5
  3.7 0.0 copy-done.4
  3.7 0.0 copy-start.5
  3.7 0.0 copy-start.6
  3.8 0.0 copy-start.7
  3.8 0.0 copy-start.8
  3.8 0.0 copy-start.2
  3.8 0.1 maximum_bitcast_fusion.2
  3.9 1.1 pad_maximum_fusion.own_a
  5.0 0.1 pad.9.clone
  5.1 0.0 copy-done.7
  5.1 0.1 maximum_bitcast_fusion.4
  5.2 0.6 pad_maximum_fusion.1.own_c
  5.8 0.6 copy.21
  6.5 0.7 copy.22
  7.2 0.7 copy.23
  8.0 1.7 maximum_bitcast_fusion.own_b
  9.6 160.3 %forward_layers.1 = (bf16[2,2,2,768,768]{4,3,2,1,0:T(8,128)(2,1)}, bf16[2,2,8,768,384]{4,3,2,1,0:T(8,128)(2,1)}, f32[2,8,768]{2,1,0:T(8,128)}, bf16[512,768]{1,0...) custom-call(bf16[8,512,768]{2,1,0:T(8,128)(2,1)} %bitcast.74, ...), custom_call_target="tpu_custom_call" | custom-call | flops 30000001024 | bytes 80000000 | tf_op jit(solution)/shard_map/forward_layers/pallas_call | solution.py:996
  169.9 103.9 %backward_second.1 = (bf16[2,2,768,768]{3,2,1,0:T(8,128)(2,1)}, bf16[512,768]{1,0:T(8,128)(2,1)}, f32[8,768]{1,0:T(8,128)}, bf16[2,4,512,768]{3,2,1,0:T(8,128)(2...) custom-call(bf16[2,2,2,768,768]{4,3,2,1,0:T(8,128)(2,1)} %get-tuple-element.44.refs_0_, ...), custom_call_target="tpu_custom_call" | custom-call | flops 40000000000 | bytes 80000000 | tf_op jit(solution)/shard_map/backward_second/pallas_call | solution.py:2152
  273.8 115.7 %backward_first.1 = (bf16[2,2,768,768]{3,2,1,0:T(8,128)(2,1)}, bf16[512,768]{1,0:T(8,128)(2,1)}, f32[8,768]{1,0:T(8,128)}, bf16[2,4,512,768]{3,2,1,0:T(8,128)(2,...) custom-call(bf16[2,2,2,768,768]{4,3,2,1,0:T(8,128)(2,1)} %get-tuple-element.44.refs_0_, ...), custom_call_target="tpu_custom_call" | custom-call | flops 40000000000 | bytes 80000000 | tf_op jit(solution)/shard_map/backward_first/pallas_call | solution.py:2152
  389.6 99.4 %sum_and_spread.1 = (bf16[2,4,512,768]{3,2,1,0:T(8,128)(2,1)}, bf16[2,2,192,768]{3,2,1,0:T(8,128)(2,1)}, bf16[2,768,768]{2,1,0:T(8,128)(2,1)}, f32[2,8,768]{2,1,0:T(8,128)}) custom-call(bf16[2,2,4,192,768]{4,3,2,1,0:T(8,128)(2,1)} %bitcast.82, bf16[2,2,4,192,768]{4,3,2,1,0:T(8,128)(2,1)} %bitcast.83, bf16[2,768,384]{2,1,0:T(8,128)(2,1)} %get-tuple-element.63.refs_2_, ...), custom_call_target="tpu_custom_call" | custom-call | flops 100000000 | bytes 40000000 | tf_op jit(solution)/shard_map/sum_and_spread/pallas_call | solution.py:2152
  489.0 1.5 convert_element_type.19
  490.5 0.1 slice_bitcast_fusion.2
  490.6 0.0 copy-start
  490.6 0.0 copy-start.1
  490.6 1.3 maximum_bitcast_fusion.1
  491.9 0.4 copy-done
  492.4 0.9 copy-done.1
  493.3 12.2 %place_results.1 = (bf16[2,4,512,768]{3,2,1,0:T(8,128)(2,1)}, bf16[2,4,512,768]{3,2,1,0:T(8,128)(2,1)}, f32[192,768]{1,0:T(8,128)}, f32[768,768]{1,0:T(8,128)}, f32[768,768]{1,0:T(8,128)}) custom-call(bf16[2,4,512,768]{3,2,1,0:T(8,128)(2,1)} %get-tuple-element.57.refs_0_, bf16[2,4,512,768]{3,2,1,0:T(8,128)(2,1)} %get-tuple-element.68.refs_1_, ...), custom_call_target="tpu_custom_call" | custom-call | flops 1000000 | bytes 35000000 | tf_op jit(solution)/shard_map/place_results/pallas_call | solution.py:2234
  505.5 1.5 dynamic-slice_bitcast_fusion
  (9 shorter events, 0.0 us)
Async XLA Ops:
  0.6 3.1 copy-start.4
  3.7 1.4 copy-start.5
  3.7 1.4 copy-start.6
  3.8 1.4 copy-start.7
  3.8 1.3 copy-start.8
  3.8 2.0 copy-start.2
  5.8 1.4 copy-start.3
  490.6 1.8 copy-start
  490.6 2.7 copy-start.1

commit v4 on v2

--- a/solution.py
+++ b/solution.py
@@ -466,18 +466,25 @@
 
 
 def attention_block(q_ref, keys, values_turned, bias, lse, turned):
-    def one(head, _):
+    def head_scores(head):
+        query = q_ref[...] * head_mask(head, 0.125).astype(jnp.bfloat16)
+        return dot_nt(keys[...], query) + bias[...]
+
+    def head_rest(head, scores):
         rows = pl.ds(pl.multiple_of(head * HDIM, HDIM), HDIM)
-        query = q_ref[...] * head_mask(head, 0.125).astype(jnp.bfloat16)
-        scores = dot_nt(keys[...], query) + bias[...]
         top = jnp.max(scores, axis=0, keepdims=True)
         raised = jnp.exp(scores - top)
         total = jnp.sum(raised, axis=0, keepdims=True)
         lse[pl.ds(head, 1), :] = top + jnp.log(total)
         turned[rows, :] = dot_nn(values_turned[rows, :], raised.astype(jnp.bfloat16)) * (1.0 / total)
+
+    def one(pair, _):
+        left, right = head_scores(2 * pair), head_scores(2 * pair + 1)
+        head_rest(2 * pair, left)
+        head_rest(2 * pair + 1, right)
         return 0
 
-    lax.fori_loop(0, LANES // HDIM, one, 0)
+    lax.fori_loop(0, LANES // HDIM // 2, one, 0)
     return turned[...].T.astype(jnp.bfloat16)
 
 
@@ -506,6 +513,126 @@
             allow = (later <= query_block) & (key_base >= 0)
         allow = allow & (docs_of(key_base) == query_doc)
         bias[i * PIECE : (i + 1) * PIECE, :] = jnp.where(allow, 0.0, -1e30)
+
+
+class Spread:
+    def __init__(self, place, source, stage, layer, out, sems):
+        self.place, self.source, self.stage = place, source, stage
+        self.layer, self.out = layer, out
+        self.local, self.swap_send, self.swap_recv, self.hop_send, self.hop_recv = sems[:5]
+        self.end_local, self.end_send, self.end_recv = sems[5:]
+        self.groups = (place.group, 1 - place.group)
+
+    def entry(self):
+        place = self.place
+        kept = self.source.at[pl.ds(pl.multiple_of(place.group * PIECE, PIECE), PIECE)]
+        sent = self.source.at[pl.ds(pl.multiple_of((1 - place.group) * PIECE, PIECE), PIECE)]
+        target = self.stage.at[0, place.group]
+        here = pltpu.make_async_copy(kept, target, self.local)
+        there = remote(sent, target, self.swap_send, self.swap_recv, place.on(seq=place.far))
+        return here, there
+
+    def take(self):
+        self.entry()[0].start()
+
+    def swap(self):
+        self.entry()[1].start()
+
+    def moves(self, half):
+        place, group = self.place, self.groups[half]
+        own = self.stage.at[0, group]
+        first = self.stage.at[place.rel_one, group]
+        second = self.stage.at[place.rel_two, group]
+        third = self.stage.at[3, group]
+        listed = (
+            (own, first, place.hop_one),
+            (own, second, place.hop_two),
+            (first, third, place.hop_two),
+        )
+        return [
+            remote(
+                source,
+                target,
+                self.hop_send.at[half, i],
+                self.hop_recv.at[half, i],
+                place.on(tp=column),
+            )
+            for i, (source, target, column) in enumerate(listed)
+        ]
+
+    def hops(self, half):
+        here, there = self.entry()
+        if half == 0:
+            here.wait()
+        else:
+            there.wait_recv()
+        first, second, _ = self.moves(half)
+        first.start()
+        second.start()
+        self.put(half, 0)
+
+    def forward(self, half):
+        first, _, third = self.moves(half)
+        first.wait_recv()
+        third.start()
+        self.put(half, 1)
+
+    def finish(self, half):
+        _, second, third = self.moves(half)
+        second.wait_recv()
+        self.put(half, 2)
+        third.wait_recv()
+        self.put(half, 3)
+
+    def ends(self, half, step):
+        place, group = self.place, self.groups[half]
+        rows = pl.ds(pl.multiple_of(place.s * PIECE, PIECE), PIECE)
+        rel = (0, place.rel_one, place.rel_two, 3)[step]
+        column = (place.t, place.hop_one, place.hop_two, 3 - place.t)[step]
+        source, target = self.stage.at[rel, group], self.out.at[group, column, rows]
+        here = pltpu.make_async_copy(source, target, self.end_local.at[half, step])
+        there = remote(
+            source,
+            target,
+            self.end_send.at[half, step],
+            self.end_recv.at[half, step],
+            place.on(section=place.core),
+        )
+        return here, there
+
+    def put(self, half, step):
+        @pl.when(self.place.s == self.layer)
+        def _():
+            self.ends(half, step)[0].start()
+
+        @pl.when(self.place.s != self.layer)
+        def _():
+            self.ends(half, step)[1].start()
+
+    def drain(self):
+        self.entry()[1].wait_send()
+        for half in range(2):
+            for copy in self.moves(half):
+                copy.wait_send()
+
+        @pl.when(self.place.s == self.layer)
+        def _():
+            for half in range(2):
+                for step in range(4):
+                    here, there = self.ends(half, step)
+                    here.wait()
+                    there.wait_recv()
+
+        @pl.when(self.place.s != self.layer)
+        def _():
+            for half in range(2):
+                for step in range(4):
+                    self.ends(half, step)[1].wait_send()
+
+
+def spread_sems():
+    dma = pltpu.SemaphoreType.DMA
+    return [dma, dma, dma, dma((2, 3)), dma((2, 3)), dma((2, 4)), dma((2, 4)), dma((2, 4))]
 
 
 class Weights:
@@ -735,6 +862,7 @@
     hid_out,
     lse_out,
     bias_out,
+    out,
     full_a,
     full_b,
     full_c,
@@ -750,11 +878,14 @@
     values_turned,
     turned_att,
     bias,
+    bias_low,
+    stage,
     *sems,
 ):
     weight_sems, key_sems = sems[:7], sems[7:11]
-    token_sem, swap_send, swap_recv, seed_sem, seed_send, seed_recv, save_sem = sems[11:]
+    token_sem, swap_send, swap_recv, seed_sem, seed_send, seed_recv, save_sem = sems[11:18]
     place = Place()
+    zero = Spread(place, low_out.at[0], stage, 0, out, sems[18:])
     weights = Weights(place, (own_a, own_b, own_c), (full_a, full_b, full_c), weight_sems)
     lse[...] = jnp.zeros_like(lse)
     kv[:, :, : 2 * PIECE, :] = jnp.zeros((2, 2, 2 * PIECE, kv.shape[-1]), jnp.bfloat16)
@@ -785,7 +916,8 @@
     gains = full_c.at[:, 0, 0]
     gains_out[...] = full_c[:, 0, 0]
     fill_bias(bias, lengths, 4 * place.group + place.t, 2 * place.half + place.s)
-    bias_save = pltpu.make_async_copy(bias, bias_out, save_sem.at[17])
+    bias_low[...] = bias[...].astype(jnp.bfloat16)
+    bias_save = pltpu.make_async_copy(bias_low, bias_out, save_sem.at[17])
     bias_save.start()
     weights.forward(0, 0)
     own_tokens.wait()
@@ -825,6 +957,7 @@
         else:
             weights.finish(1, 0)
             weights.begin(1, 2)
+            zero.hops(0)
             for copy in saves(0)[1:]:
                 copy.wait()
         weights.need(layer, 0)
@@ -852,6 +985,7 @@
             weights.begin(0, 2)
         else:
             weights.forward(1, 1)
+            zero.hops(1)
         for part in range(3):
             lanes = pl.ds(part * LANES, LANES)
             share.arrive(part)
@@ -877,10 +1011,14 @@
                 else:
                     weights.forward(0, 2)
             else:
-                if part == 1:
+                if part == 0:
+                    zero.forward(0)
+                elif part == 1:
                     weights.finish(1, 1)
-                elif part == 2:
+                    zero.forward(1)
+                else:
                     weights.forward(1, 2)
+                    zero.finish(0)
         for copy in saves(layer)[1:4] + saves(layer)[6:]:
             copy.start()
 
@@ -900,6 +1038,8 @@
                 weights.finish(layer, 2)
                 if layer == 0:
                     weights.begin(1, 1)
+                else:
+                    zero.finish(1)
             weights.need(layer, part + 1)
             if part == 1:
                 for copy in weight_saves(layer)[2:]:
@@ -920,12 +1060,13 @@
         saves(layer)[5].start()
         if layer == 0:
             x_save.wait()
-        else:
-            saves(0)[0].wait()
         low[...] = x[...].astype(jnp.bfloat16)
         saves(layer)[0].start()
         x[...] = low[...].astype(jnp.float32)
         if layer == 0:
+            saves(0)[0].wait()
+            zero.take()
+            zero.swap()
             weights.forward(1, 0)
     for copy in saves(1):
         copy.wait()
@@ -934,6 +1075,7 @@
             copy.wait()
         KeyShare(place, kv, layer, key_sems).drain()
     weights.drain()
+    zero.drain()
     bias_save.wait()
     own_seed.wait()
     seed_swap.wait()
@@ -962,10 +1104,11 @@
             shape((2, count, width), full_type),
             shape((2, count, units), low_type),
             shape((2, 24, count), full_type),
-            shape((4 * PIECE, count), full_type),
+            shape((4 * PIECE, count), low_type),
+            shape((2, 4, count, width), low_type),
         ],
         in_specs=[HBM] * 5 + [pl.BlockSpec(memory_space=pltpu.SMEM)] + [VMEM] * 2,
-        out_specs=[HBM] * 2 + [VMEM] + [HBM] * 10,
+        out_specs=[HBM] * 2 + [VMEM] + [HBM] * 11,
         scratch_shapes=[
             pltpu.VMEM((2, 2, 2, width, width), low_type),
             pltpu.VMEM((2, 2, 8, width, units // 8), low_type),
@@ -982,6 +1125,8 @@
             pltpu.VMEM((LANES, 4 * PIECE), low_type),
             pltpu.VMEM((LANES, PIECE), full_type),
             pltpu.VMEM((4 * PIECE, count), full_type),
+            pltpu.VMEM((4 * PIECE, count), low_type),
+            pltpu.VMEM((4, 2, PIECE, width), low_type),
             dma((4, 2)),
             dma((4, 2)),
             dma((4, 2)),
@@ -1000,6 +1145,7 @@
             dma,
             dma,
             dma((18,)),
+            *spread_sems(),
         ],
         compiler_params=pltpu.CompilerParams(
             collective_id=1, has_side_effects=True, vmem_limit_bytes=62 * 1024 * 1024
@@ -1017,131 +1163,12 @@
     return total.astype(jnp.bfloat16)
 
 
-class Spread:
-    def __init__(self, place, source, stage, layer, out, sems):
-        self.place, self.source, self.stage = place, source, stage
-        self.layer, self.out = layer, out
-        self.local, self.swap_send, self.swap_recv, self.hop_send, self.hop_recv = sems[:5]
-        self.end_local, self.end_send, self.end_recv = sems[5:]
-        self.groups = (place.group, 1 - place.group)
-
-    def entry(self):
-        place = self.place
-        kept = self.source.at[pl.ds(pl.multiple_of(place.group * PIECE, PIECE), PIECE)]
-        sent = self.source.at[pl.ds(pl.multiple_of((1 - place.group) * PIECE, PIECE), PIECE)]
-        target = self.stage.at[0, place.group]
-        here = pltpu.make_async_copy(kept, target, self.local)
-        there = remote(sent, target, self.swap_send, self.swap_recv, place.on(seq=place.far))
-        return here, there
-
-    def take(self):
-        self.entry()[0].start()
-
-    def swap(self):
-        self.entry()[1].start()
-
-    def moves(self, half):
-        place, group = self.place, self.groups[half]
-        own = self.stage.at[0, group]
-        first = self.stage.at[place.rel_one, group]
-        second = self.stage.at[place.rel_two, group]
-        third = self.stage.at[3, group]
-        listed = (
-            (own, first, place.hop_one),
-            (own, second, place.hop_two),
-            (first, third, place.hop_two),
-        )
-        return [
-            remote(
-                source,
-                target,
-                self.hop_send.at[half, i],
-                self.hop_recv.at[half, i],
-                place.on(tp=column),
-            )
-            for i, (source, target, column) in enumerate(listed)
-        ]
-
-    def hops(self, half):
-        here, there = self.entry()
-        if half == 0:
-            here.wait()
-        else:
-            there.wait_recv()
-        first, second, _ = self.moves(half)
-        first.start()
-        second.start()
-        self.put(half, 0)
-
-    def forward(self, half):
-        first, _, third = self.moves(half)
-        first.wait_recv()
-        third.start()
-        self.put(half, 1)
-
-    def finish(self, half):
-        _, second, third = self.moves(half)
-        second.wait_recv()
-        self.put(half, 2)
-        third.wait_recv()
-        self.put(half, 3)
-
-    def ends(self, half, step):
-        place, group = self.place, self.groups[half]
-        rows = pl.ds(pl.multiple_of(place.s * PIECE, PIECE), PIECE)
-        rel = (0, place.rel_one, place.rel_two, 3)[step]
-        column = (place.t, place.hop_one, place.hop_two, 3 - place.t)[step]
-        source, target = self.stage.at[rel, group], self.out.at[group, column, rows]
-        here = pltpu.make_async_copy(source, target, self.end_local.at[half, step])
-        there = remote(
-            source,
-            target,
-            self.end_send.at[half, step],
-            self.end_recv.at[half, step],
-            place.on(section=place.core),
-        )
-        return here, there
-
-    def put(self, half, step):
-        @pl.when(self.place.s == self.layer)
-        def _():
-            self.ends(half, step)[0].start()
-
-        @pl.when(self.place.s != self.layer)
-        def _():
-            self.ends(half, step)[1].start()
-
-    def drain(self):
-        self.entry()[1].wait_send()
-        for half in range(2):
-            for copy in self.moves(half):
-                copy.wait_send()
-
-        @pl.when(self.place.s == self.layer)
-        def _():
-            for half in range(2):
-                for step in range(4):
-                    here, there = self.ends(half, step)
-                    here.wait()
-                    there.wait_recv()
-
-        @pl.when(self.place.s != self.layer)
-        def _():
-            for half in range(2):
-                for step in range(4):
-                    self.ends(half, step)[1].wait_send()
-
-
-def spread_sems():
-    dma = pltpu.SemaphoreType.DMA
-    return [dma, dma, dma, dma((2, 3)), dma((2, 3)), dma((2, 4)), dma((2, 4)), dma((2, 4))]
-
-
 class Sum:
-    def __init__(self, place, source, total, buffers, sems, loaded=False, opens=None, waits=None):
+    def __init__(self, place, source, total, buffers, sems, loaded=False, opens=None, waits=None, slim=False):
         self.place, self.source, self.total = place, source, total
         self.inbox, self.hop_in, self.line_in = buffers
         self.loaded, self.opens, self.waits = loaded, opens, waits
+        self.slim = slim
         (
             self.mine_sem,
             self.chip_send,
@@ -1227,12 +1254,18 @@
         total[...] = low_sum(total[...], self.hop_in[0])
         third.start()
 
+    def line_slots(self):
+        if self.slim:
+            return self.total(1), self.line_in.at[0]
+        return self.line_in.at[0], self.line_in.at[1]
+
     def lines(self):
         place = self.place
         own, line_sum = self.total(0), self.total(1)
+        first, second = self.line_slots()
         listed = (
-            (own, self.line_in.at[0], place.twin),
-            (own, self.line_in.at[1], 3 - place.z),
+            (own, first, place.twin),
+            (own, second, 3 - place.z),
             (line_sum, line_sum, place.twin),
         )
         return [
@@ -1273,14 +1306,14 @@
         def _():
             self.lines()[0].wait_recv()
             total = self.total(0)
-            total[...] = low_sum(total[...], self.line_in[0])
+            total[...] = low_sum(total[...], self.line_slots()[0][...])
             self.lines()[1].start()
 
     def line_two(self):
         @pl.when(self.inner)
         def _():
             self.lines()[1].wait_recv()
-            self.total(1)[...] = low_sum(self.total(0)[...], self.line_in[1])
+            self.total(1)[...] = low_sum(self.total(0)[...], self.line_slots()[1][...])
             self.lines()[2].start()
 
     def line_three(self):
@@ -1359,10 +1392,14 @@
     return [pltpu.VMEM((count,) + piece, jnp.bfloat16) for count in counts]
 
 
-def attention_sums(place, grads, buffers, sems):
+def attention_sums(place, grads, buffers, sems, gate=None):
     sums = []
     for i in range(2):
         total, inbox, hop_in, line_in = buffers[4 * i : 4 * i + 4]
+        gates = {}
+        if gate is not None:
+            inbox = buffers[1]
+            gates = {"opens": gate} if i == 0 else {"waits": gate}
 
         def source(pack, rel, i=i):
             return grads.at[pack, i, rel]
@@ -1371,7 +1408,7 @@
             return total.at[rel]
 
         own_sems = sems[SUM_SEMS * i : SUM_SEMS * (i + 1)]
-        sums.append(Sum(place, source, kept, (inbox, hop_in, line_in), own_sems, loaded=True))
+        sums.append(Sum(place, source, kept, (inbox, hop_in, line_in), own_sems, loaded=True, **gates))
     return sums
 
 
@@ -1398,7 +1435,7 @@
 
 
 def line_sum(place, total, line_in, sems):
-    return Sum(place, None, lambda rel: total.at[rel], (None, None, line_in), sems)
+    return Sum(place, None, lambda rel: total.at[rel], (None, None, line_in), sems, slim=True)
 
 
 class KeyReturn:
@@ -1520,26 +1557,20 @@
 def attention_back(q_ref, grad_ref, att_ref, keys, values, keys_turned, bias, lse, sums, turned, count):
     turned[...] = (grad_ref[...].astype(jnp.float32) * att_ref[...].astype(jnp.float32)).T
 
-    def head_terms(head):
+    def one(head, _):
         rows = pl.ds(pl.multiple_of(head * HDIM, HDIM), HDIM)
         query = q_ref[...] * head_mask(head, 0.125).astype(jnp.bfloat16)
         grad = grad_ref[...] * head_mask(head, 1.0).astype(jnp.bfloat16)
         delta = jnp.sum(turned[rows, :], axis=0, keepdims=True)
-        scores = dot_nt(keys[...], query) + bias[...]
+        scores = dot_nt(keys[...], query) + bias[...].astype(jnp.float32)
         probs = jnp.exp(scores - lse[pl.ds(head, 1), :])
         grad_scores = (probs * (dot_nt(values[...], grad) - delta)).astype(jnp.bfloat16)
+        sums[0, :count] += dot_nn(grad_scores, query)
+        sums[1, :count] += dot_nn(probs.astype(jnp.bfloat16), grad)
         turned[rows, :] = dot_nn(keys_turned[rows, :], grad_scores) * 0.125
-        return query, grad, grad_scores, probs.astype(jnp.bfloat16)
-
-    def one(pair, _):
-        left, right = head_terms(2 * pair), head_terms(2 * pair + 1)
-        query, grad = (jnp.concatenate([left[i], right[i]], axis=0) for i in (0, 1))
-        grad_scores, probs = (jnp.concatenate([left[i], right[i]], axis=1) for i in (2, 3))
-        sums[0, :count] += dot_nn(grad_scores, query)
-        sums[1, :count] += dot_nn(probs, grad)
         return 0
 
-    lax.fori_loop(0, LANES // HDIM // 2, one, 0)
+    lax.fori_loop(0, LANES // HDIM, one, 0)
     q_ref[...] = turned[...].T.astype(jnp.bfloat16)
 
 
@@ -1564,7 +1595,6 @@
         small_out,
         wa,
         wb,
-        low,
         q,
         kv,
         att,
@@ -1593,7 +1623,6 @@
         (att_in.at[layer], att),
         (q_in.at[layer], q),
         (kv_in.at[layer], kv),
-        (x_in, low),
         (lse_in.at[layer], lse),
         (bias_in, bias),
     ]
@@ -1714,6 +1743,10 @@
         if part > 0:
             share.relay(part - 1)
         tick()
+    low_load = pltpu.make_async_copy(x_in, att, sems.at[9])
+    low_load.start()
+    low_load.wait()
+    low = att
     normed = grad_att
 
     def again(rows):
@@ -1797,7 +1830,6 @@
     return [
         pltpu.VMEM((2, 2, width, width), low),
         pltpu.VMEM((2, 8, width, units // 8), low),
-        pltpu.VMEM((count, width), low),
         pltpu.VMEM((count, width), low),
         pltpu.VMEM((2, 4 * PIECE, width), low),
         pltpu.VMEM((count, width), low),
@@ -1815,7 +1847,7 @@
         pltpu.VMEM((width, count), low),
         pltpu.VMEM((width, count), low),
         pltpu.VMEM((24, count), full),
-        pltpu.VMEM((4 * PIECE, count), full),
+        pltpu.VMEM((4 * PIECE, count), low),
     ]
 
 
@@ -1824,7 +1856,7 @@
     return [dma((3,))] * 6 + [dma((12,)), dma((2, 8))]
 
 
-BUFFERS = 21
+BUFFERS = 20
 
 
 def later(step, *args):
@@ -1833,142 +1865,123 @@
 
 def second_kernel(*refs):
     ins, refs = refs[:15], refs[15:]
-    (grads_a, grad_out, small_out, out, carry_one, carry), refs = refs[:6], refs[6:]
-    buffers, stages, feed, refs = refs[:BUFFERS], refs[BUFFERS : BUFFERS + 2], refs[23:25], refs[25:]
-    sems, feed_sem, gate, carry_sem = refs[:24], refs[24:-2], refs[-2], refs[-1]
+    (grads_a, grad_out, small_out, out, carry), refs = refs[:5], refs[5:]
+    buffers, stage, feed, refs = refs[:BUFFERS], refs[BUFFERS], refs[21:23], refs[23:]
+    sems, feed_sem, gate, carry_sem = refs[:16], refs[16:-2], refs[-2], refs[-1]
     low_both = ins[14]
     place = Place()
     place.meet(place.partners())
-    zero, last = [
-        Spread(place, low_both.at[i], stages[i], i, out, sems[8 + 8 * i : 16 + 8 * i])
-        for i in range(2)
+    back = Spread(place, low_both.at[1], stage, 1, out, sems[8:16])
+    one, two = feed_sums(place, buffers[1], feed, feed_sem, gate)
+    saves = [
+        pltpu.make_async_copy(item.total(0), carry.at[i], carry_sem.at[i])
+        for i, item in enumerate((one, two))
     ]
-    one, two = feed_sums(place, buffers[1], feed, feed_sem, gate)
-    carries = [
-        pltpu.make_async_copy(two.total(rel), carry.at[rel], carry_sem.at[rel]) for rel in range(4)
-    ]
-    save_one = pltpu.make_async_copy(one.total(0), carry_one, carry_sem.at[4])
-
-    def hand_on():
-        two.load(travels=False)
-        for copy in carries:
-            copy.start()
-
     tick = Ticks(
         [
-            [zero.take, last.take, zero.swap, later(zero.hops, 0), later(last.hops, 0)],
+            [back.take, back.swap, later(back.hops, 0)],
             [],
-            [later(zero.forward, 0)],
-            [one.start, last.swap],
-            [later(zero.hops, 1), later(last.forward, 0)],
-            [later(zero.finish, 0)],
+            [later(back.forward, 0)],
+            [one.start],
+            [later(back.hops, 1), later(back.finish, 0)],
+            [],
             [one.load],
-            [later(zero.forward, 1), two.start],
-            [later(last.finish, 0)],
+            [two.start, later(back.forward, 1)],
+            [],
             [one.middle],
-            [later(last.hops, 1), later(zero.finish, 1)],
+            [two.load, later(back.finish, 1)],
             [],
-            [hand_on],
-            [later(one.gather, save_one), later(last.forward, 1)],
+            [later(one.gather, saves[0])],
+            [two.middle],
             [],
-            [later(last.finish, 1)],
+            [later(two.gather, saves[1])],
         ]
     )
     body = ins[:3] + (low_both.at[0],) + ins[4:14] + (grads_a, grad_out, small_out) + buffers
     backward_layer(1, body, place, tick, sems[:6], sems[6], sems[7])
     tick.rest()
-    zero.drain()
-    last.drain()
+    back.drain()
     one.drain_plane()
-    save_one.wait()
-    two.drain_exchange()
-    for copy in carries:
+    two.drain_plane()
+    for copy in saves:
         copy.wait()
 
 
 def first_kernel(*refs):
     ins, refs = refs[:17], refs[17:]
-    (grads_a, grad_out, small_out, out, done, carry_out), refs = refs[:6], refs[6:]
+    (grads_a, grad_out, small_out, out, done, done_a, carry_out), refs = refs[:7], refs[7:]
     buffers, stage, refs = refs[:BUFFERS], refs[BUFFERS], refs[BUFFERS + 1 :]
-    feed, (total, hop_in, line_in, line_total, line_in_one), refs = refs[:2], refs[2:7], refs[7:]
-    sems, feed_sem, kept_sem, line_sem = refs[:16], refs[16:36], refs[36:46], refs[46:56]
-    gate, carry_sem = refs[56:]
-    carry_one, carry, prior_grad = ins[14:]
+    feed, held, (line_total, line_in), refs = refs[:2], refs[2:10], refs[10:12], refs[12:]
+    sems, feed_sem, held_sem, line_sem = refs[:16], refs[16:36], refs[36:56], refs[56:76]
+    gate, gate_rows, carry_sem = refs[76:]
+    carry, prior, prior_grad = ins[14:]
     place = Place()
     place.meet(place.partners())
     back = Spread(place, prior_grad, stage, 1, out, sems[8:16])
     one, two = feed_sums(place, buffers[1], feed, feed_sem, gate)
-    kept = Sum(
-        place,
-        lambda pack, rel: carry.at[rel],
-        lambda rel: total.at[rel],
-        (None, hop_in, line_in),
-        kept_sem,
-        loaded=True,
-    )
-    line = line_sum(place, line_total, line_in_one, line_sem)
-    line_load = pltpu.make_async_copy(carry_one, line_total.at[0], carry_sem.at[0])
-    saves = [
-        pltpu.make_async_copy(line.total(1), done.at[0], carry_sem.at[1]),
-        pltpu.make_async_copy(kept.total(1), done.at[1], carry_sem.at[2]),
-        pltpu.make_async_copy(one.total(0), carry_out.at[0], carry_sem.at[3]),
-        pltpu.make_async_copy(two.total(0), carry_out.at[1], carry_sem.at[4]),
+    first, second = attention_sums(place, prior, held, held_sem, gate_rows)
+    lines, loads, saves = [], [], []
+    for i in range(2):
+        line = line_sum(place, line_total.at[i], line_in.at[i], line_sem[10 * i : 10 * i + 10])
+        lines.append(line)
+        loads.append(pltpu.make_async_copy(carry.at[i], line_total.at[i, 0], carry_sem.at[i]))
+        saves.append(pltpu.make_async_copy(line.total(1), done.at[i], carry_sem.at[2 + i]))
+    saves += [
+        pltpu.make_async_copy(first.total(1), done_a.at[0], carry_sem.at[4]),
+        pltpu.make_async_copy(second.total(1), done_a.at[1], carry_sem.at[5]),
+        pltpu.make_async_copy(one.total(0), carry_out.at[0], carry_sem.at[6]),
+        pltpu.make_async_copy(two.total(0), carry_out.at[1], carry_sem.at[7]),
     ]
     tick = Ticks(
         [
-            [back.take, back.swap, line_load.start, kept.start, later(back.hops, 0)],
-            [later(line.resume, line_load), kept.load],
-            [later(back.forward, 0)],
-            [one.start, line.line_one],
-            [kept.middle, later(back.hops, 1)],
-            [line.line_two, later(back.finish, 0)],
-            [one.load],
-            [kept.gather, two.start],
-            [later(back.forward, 1), later(line.store, saves[0])],
-            [kept.line_one],
-            [one.middle, two.load],
-            [kept.line_two, later(back.finish, 1)],
-            [],
-            [later(one.gather, saves[2]), later(kept.store, saves[1])],
-            [two.middle],
-            [],
-            [later(two.gather, saves[3])],
+            [back.take, back.swap, loads[0].start, loads[1].start, first.start, later(back.hops, 0)],
+            [later(lines[0].resume, loads[0]), first.load, second.start],
+            [later(lines[1].resume, loads[1]), later(back.forward, 0)],
+            [second.load, one.start, first.middle],
+            [second.middle, later(back.hops, 1), lines[0].line_one],
+            [first.gather, later(back.finish, 0)],
+            [one.load, second.gather],
+            [two.start, lines[1].line_one, lines[0].line_two],
+            [later(back.forward, 1), first.line_one],
+            [one.middle, second.line_one],
+            [two.load, lines[1].line_two],
+            [later(back.finish, 1), first.line_two, later(lines[0].store, saves[0])],
+            [second.line_two],
+            [later(one.gather, saves[4]), later(lines[1].store, saves[1])],
+            [two.middle, later(first.store, saves[2])],
+            [later(second.store, saves[3])],
+            [later(two.gather, saves[5])],
         ]
     )
     body = ins[:14] + (grads_a, grad_out, small_out) + buffers
     backward_layer(0, body, place, tick, sems[:6], sems[6], sems[7])
     tick.rest()
     back.drain()
-    for item in (kept, one, two):
+    for item in (first, second, one, two):
         item.drain_plane()
-    line.drain_line()
-    kept.drain_line()
+    for item in (first, second, *lines):
+        item.drain_line()
     for copy in saves:
         copy.wait()
 
 
 def last_kernel(*refs):
-    priors, (done, carry, grad_zero, small_zero, small_one), refs = refs[:2], refs[2:7], refs[7:]
+    (prior, done, done_a, carry, grad_zero, small_zero, small_one), refs = refs[:7], refs[7:]
     (out, final_a, final_b, small), refs = refs[:4], refs[4:]
-    held, stage, (small_in, extra), refs = refs[:16], refs[16], refs[17:19], refs[19:]
+    held, stage, (small_in, extra), refs = refs[:8], refs[8], refs[9:11], refs[11:]
     (line_total, line_in), sems = refs[:2], refs[2:]
-    held_sem, spread_sem, line_sem, sems = sems[:40], sems[40:48], sems[48:68], sems[68:]
+    held_sem, spread_sem, line_sem, sems = sems[:20], sems[20:28], sems[28:48], sems[48:]
     tiny_send, tiny_recv, carry_sem, end_local, end_send, end_recv = sems
     place = Place()
     place.meet(place.partners())
-    sums = []
-    for i in range(2):
-        sums += attention_sums(
-            place, priors[i], held[8 * i : 8 * i + 8], held_sem[20 * i : 20 * i + 20]
-        )
+    first, second = attention_sums(place, prior, held, held_sem)
     lines, loads = [], []
     for i in range(2):
         lines.append(line_sum(place, line_total.at[i], line_in.at[i], line_sem[10 * i : 10 * i + 10]))
         loads.append(pltpu.make_async_copy(carry.at[i], line_total.at[i, 0], carry_sem.at[i]))
     back = Spread(place, grad_zero, stage, 0, out, spread_sem)
-    targets = [final_a.at[place.s, 0], final_a.at[place.s, 1]] * 2
+    parts = [final_a.at[place.s, i] for i in range(2)]
     halves = [final_b.at[place.s, :, pl.ds(384 * i, 384)] for i in range(2)]
-    layers = (1, 1, 0, 0)
     small[0], small[1] = small_zero[...], small_one[...]
     rows_beside = ((4, 5, 6, 7), (5, 4, 7, 6), (6, 7, 4, 5), (4, 5, 6, 7), (4, 5, 6, 7))
     partners = (
@@ -1978,36 +1991,38 @@
         place.on(seq=place.twin),
         place.on(seq=place.far),
     )
+    sources = [done.at[0], done.at[1], done_a.at[0], done_a.at[1]]
 
     def done_ends(i):
-        here = pltpu.make_async_copy(done.at[i], halves[i], end_local.at[i])
+        source, target = sources[i], (halves + parts)[i]
+        here = pltpu.make_async_copy(source, target, end_local.at[i])
         there = remote(
-            done.at[i], halves[i], end_send.at[i], end_recv.at[i], place.on(section=place.core)
+            source, target, end_send.at[i], end_recv.at[i], place.on(section=place.core)
         )
         return here, there
 
     def done_start():
         @pl.when(place.s == 1)
         def _():
-            for i in range(2):
+            for i in range(4):
                 done_ends(i)[0].start()
 
         @pl.when(place.s == 0)
         def _():
-            for i in range(2):
+            for i in range(4):
                 done_ends(i)[1].start()
 
     def done_wait():
         @pl.when(place.s == 1)
         def _():
-            for i in range(2):
+            for i in range(4):
                 here, there = done_ends(i)
                 here.wait()
                 there.wait_recv()
 
         @pl.when(place.s == 0)
         def _():
-            for i in range(2):
+            for i in range(4):
                 done_ends(i)[1].wait_send()
 
     def tiny(i):
@@ -2027,67 +2042,53 @@
                     extra[i, layer, at : at + 1] + small_in[i, layer, other : other + 1]
                 )
 
+    first.start()
     back.take()
-    sums[0].start()
-    back.swap()
-    sums[1].start()
     for load in loads:
         load.start()
+    second.start()
+    back.swap()
     tiny_start(0)
     back.hops(0)
     lines[0].resume(loads[0])
-    sums[0].load()
-    sums[2].start()
-    back.forward(0)
+    lines[1].resume(loads[1])
+    first.load()
+    second.load()
     tiny_end(0)
     tiny_start(1)
-    lines[1].resume(loads[1])
-    sums[1].load()
-    sums[3].start()
-    sums[0].middle()
+    back.forward(0)
+    done_start()
+    first.middle()
+    second.middle()
     lines[0].line_one()
     tiny_end(1)
     tiny_start(2)
-    sums[2].load()
-    sums[0].gather()
-    back.finish(0)
-    sums[1].middle()
+    first.gather()
     back.hops(1)
-    sums[1].gather()
+    second.gather()
+    lines[1].line_one()
+    first.line_one()
+    second.line_one()
     tiny_end(2)
     tiny_start(3)
-    sums[3].load()
-    sums[2].middle()
-    lines[1].line_one()
-    done_start()
+    back.finish(0)
     lines[0].line_two()
-    sums[2].gather()
+    lines[1].line_two()
     back.forward(1)
-    sums[3].middle()
-    sums[0].line_one()
+    first.line_two()
+    second.line_two()
     tiny_end(3)
     tiny_start(4)
-    sums[3].gather()
-    sums[1].line_one()
+    lines[0].finish(0, halves[0])
+    lines[1].finish(0, halves[1])
     back.finish(1)
-    lines[1].line_two()
-    lines[0].finish(0, halves[0])
-    sums[2].line_one()
-    sums[0].line_two()
+    first.finish(0, parts[0])
+    second.finish(0, parts[1])
     tiny_end(4)
-    sums[3].line_one()
-    sums[1].line_two()
-    sums[0].finish(1, targets[0])
-    sums[2].line_two()
-    lines[1].finish(0, halves[1])
-    sums[1].finish(1, targets[1])
-    sums[3].line_two()
-    sums[2].finish(0, targets[2])
-    sums[3].finish(0, targets[3])
-    for item, layer, target in zip(sums, layers, targets):
+    for item, target in ((first, parts[0]), (second, parts[1])):
         item.drain_plane()
         item.drain_line()
-        item.drain_end(layer, target)
+        item.drain_end(0, target)
     for item, target in zip(lines, halves):
         item.drain_line()
         item.drain_end(0, target)
@@ -2115,20 +2116,16 @@
 
 
 def results_kernel(*refs):
-    layer_raw, zero_raw, one_raw, final_a, final_b = refs[:5]
-    layer_out, input_grad, grad_out, grad_up, grad_down = refs[5:10]
-    rows, turned, part, tiles, converted, row_sem, tile_sem = refs[10:]
+    (out_zero, out_one, zero_raw, one_raw, final_a, final_b), refs = refs[:6], refs[6:]
+    layer_out, input_grad, grad_out, grad_up, grad_down = refs[:5]
+    rows, turned, part, tiles, converted, row_sem, tile_sem = refs[5:]
     s = lax.axis_index("section")
     count = rows.shape[0] // 2
 
     def load(i):
         sem = row_sem.at[0, i]
-        if i < count:
-            return [pltpu.make_async_copy(layer_raw.at[i // 4, i % 4], rows.at[i], sem)] * 2
-        at = i - count
-        return [
-            pltpu.make_async_copy(raw.at[at // 4, at % 4], rows.at[i], sem) for raw in (zero_raw, one_raw)
-        ]
+        pair, at = ((out_zero, out_one), i) if i < count else ((zero_raw, one_raw), i - count)
+        return [pltpu.make_async_copy(raw.at[at // 4, at % 4], rows.at[i], sem) for raw in pair]
 
     def store(i):
         target, at = (layer_out, i) if i < count else (input_grad, i - count)
@@ -2145,17 +2142,15 @@
     ]
     for copy in loads:
         copy.start()
-    for i in range(count):
-        load(i)[0].start()
 
     @pl.when(s == 0)
     def _():
-        for i in range(count, 2 * count):
+        for i in range(2 * count):
             load(i)[0].start()
 
     @pl.when(s != 0)
     def _():
-        for i in range(count, 2 * count):
+        for i in range(2 * count):
             load(i)[1].start()
 
     for copy in loads:
@@ -2174,20 +2169,20 @@
         copy.wait()
 
 
-def run_results(layer_raw, zero_raw, one_raw, final_a, final_b):
+def run_results(out_zero, out_one, zero_raw, one_raw, final_a, final_b):
     full = jnp.float32
     width = final_b.shape[-1]
-    big = jax.ShapeDtypeStruct(layer_raw.shape, layer_raw.dtype)
+    big = jax.ShapeDtypeStruct(out_zero.shape, out_zero.dtype)
     square = jax.ShapeDtypeStruct((width, width), full)
     dma = pltpu.SemaphoreType.DMA
     return pl.pallas_call(
         results_kernel,
         name="place_results",
         out_shape=[big, big, jax.ShapeDtypeStruct((192, width), full), square, square],
-        in_specs=[HBM] * 5,
+        in_specs=[HBM] * 6,
         out_specs=[HBM] * 2 + [VMEM] + [HBM] * 2,
         scratch_shapes=[
-            pltpu.VMEM((16,) + layer_raw.shape[2:], jnp.bfloat16),
+            pltpu.VMEM((16,) + out_zero.shape[2:], jnp.bfloat16),
             pltpu.VMEM((width, width), full),
             pltpu.VMEM((192, width), jnp.bfloat16),
             pltpu.VMEM((2, width, width), jnp.bfloat16),
@@ -2197,7 +2192,7 @@
         ],
         compiler_params=pltpu.CompilerParams(vmem_limit_bytes=48 * 1024 * 1024),
         cost_estimate=pl.CostEstimate(flops=1_000_000, bytes_accessed=35_000_000, transcendentals=0),
-    )(layer_raw, zero_raw, one_raw, final_a, final_b)
+    )(out_zero, out_one, zero_raw, one_raw, final_a, final_b)
 
 
 def run_backward(full_a, full_b, seeded, tokens, low_both, kept, gains, tables):
@@ -2211,85 +2206,77 @@
     out = ((2, 4, count, width), low)
     row_piece, tile_piece = (192, width), (width, units // 8)
     final_a, final_b = ((2, 2) + row_piece, low), ((2, width, 2 * tile_piece[1]), low)
-    carry_one, carry, two_tiles = (tile_piece, low), ((4,) + tile_piece, low), ((2,) + tile_piece, low)
+    two_tiles, two_rows = ((2,) + tile_piece, low), ((2,) + row_piece, low)
     stage = pltpu.VMEM((4, 2, PIECE, width), low)
     dma, gate = pltpu.SemaphoreType.DMA, pltpu.SemaphoreType.REGULAR
     common = (*kept, gains, *tables)
     common_spaces = [HBM] * 11 + [VMEM] * 3
     held = sum_buffers(row_piece, (4, 4, 3, 2) * 2)
+    lines = [pltpu.VMEM((2, 2) + tile_piece, low), pltpu.VMEM((2, 1) + tile_piece, low)]
     second = call(
         second_kernel,
         "backward_second",
         2,
         (full_a, full_b, seeded, tokens) + common + (low_both,),
         common_spaces + [HBM],
-        grads + [out, carry_one, carry],
-        [HBM] * 2 + [VMEM] + [HBM] * 3,
+        grads + [out, two_tiles],
+        [HBM] * 2 + [VMEM] + [HBM] * 2,
         backward_buffers(width, units)
-        + [stage, stage]
-        + feed_buffers(tile_piece, 1)
+        + [stage]
+        + feed_buffers(tile_piece, 2)
         + backward_sems()
         + spread_sems()
-        + spread_sems()
-        + sum_sems()
-        + sum_sems()
-        + [gate, dma((5,))],
+        + sum_sems() * 2
+        + [gate, dma((2,))],
         40_000_000_000,
         80_000_000,
     )
-    prior_a, grad_one, small_one, layer_out, carried_one, carried = second
+    prior, grad_one, small_one, layer_one, carried = second
+    by_shard = (2, 2, 4, 192, width)
     first = call(
         first_kernel,
         "backward_first",
         3,
-        (full_a, full_b, grad_one, tokens) + common + (carried_one, carried, grad_one),
+        (full_a, full_b, grad_one, tokens) + common + (carried, prior.reshape(by_shard), grad_one),
         common_spaces + [HBM] * 3,
-        grads + [out, two_tiles, two_tiles],
-        [HBM] * 2 + [VMEM] + [HBM] * 3,
+        grads + [out, two_tiles, two_rows, two_tiles],
+        [HBM] * 2 + [VMEM] + [HBM] * 4,
         backward_buffers(width, units)
         + [stage]
         + feed_buffers(tile_piece, 2)
-        + sum_buffers(tile_piece, (4, 3, 2, 2, 2))
+        + sum_buffers(row_piece, (4, 4, 3, 2))
+        + [held[4], pltpu.VMEM((1, 8, 128), low), held[6], held[7]]
+        + lines
         + backward_sems()
         + spread_sems()
-        + sum_sems()
-        + sum_sems()
-        + sum_sems()
-        + sum_sems()
-        + [gate, dma((5,))],
+        + sum_sems() * 6
+        + [gate, gate, dma((8,))],
         40_000_000_000,
         80_000_000,
     )
-    grads_a, grad_zero, small_zero, out_one, done, carried = first
-    by_shard = (2, 2, 4, 192, width)
+    grads_a, grad_zero, small_zero, input_one, done, done_a, carried = first
     last = call(
         last_kernel,
         "sum_and_spread",
         4,
-        (prior_a.reshape(by_shard), grads_a.reshape(by_shard), done, carried, grad_zero)
-        + (small_zero, small_one),
+        (grads_a.reshape(by_shard), done, done_a, carried, grad_zero, small_zero, small_one),
         [HBM] * 5 + [VMEM] * 2,
         [out, final_a, final_b, ((2, 8, width), full)],
         [HBM] * 3 + [VMEM],
         held
-        + held
         + [stage]
         + [pltpu.VMEM((5, 2, 8, width), full), pltpu.VMEM((5, 2, 8, width), full)]
-        + [pltpu.VMEM((2, 2) + tile_piece, low), pltpu.VMEM((2, 2) + tile_piece, low)]
-        + sum_sems()
-        + sum_sems()
-        + sum_sems()
-        + sum_sems()
+        + lines
+        + sum_sems() * 2
         + spread_sems()
-        + sum_sems()
-        + sum_sems()
-        + [dma((5,)), dma((5,))]
-        + [dma((2,))] * 4,
+        + sum_sems() * 2
+        + [dma((5,)), dma((5,)), dma((2,))]
+        + [dma((4,))] * 3,
         100_000_000,
         40_000_000,
     )
-    out_zero, final_a, final_b, small = last
-    return layer_out, (out_zero, out_one), final_a, final_b, small
+    input_zero, final_a, final_b, small = last
+    return layer_one, (input_zero, input_one), final_a, final_b, small
 
 
 def spread(
@@ -2333,13 +2320,13 @@
     forward = run_forward(
         layer_input.reshape(flat), cotangent.reshape(flat), own_a, own_b, own_c, lengths, turn_cos, turn_sin
     )
-    full_a, full_b, gains, seeded, tokens, low_both, *kept = forward
+    full_a, full_b, gains, seeded, tokens, low_both, *kept, layer_zero = forward
     tables = (turn_cos, turn_sin)
-    layer_raw, input_raws, final_a, final_b, small = run_backward(
+    layer_one, input_raws, final_a, final_b, small = run_backward(
         full_a, full_b, seeded, tokens, low_both, kept, gains, tables
     )
     layer_out, input_grad, grad_out, grad_up, grad_down = run_results(
-        layer_raw, *input_raws, final_a, final_b
+        layer_zero, layer_one, *input_raws, final_a, final_b
     )
     small = lax.dynamic_index_in_dim(small, s, 0, keepdims=False)
     final_a = final_a.astype(jnp.float32)

time: 518 us -> 528 us (1.019)
  Pallas kernels: 494 us -> 502 us
    pallas_call x1, Pallas kernels: 155 us -> 173 us  [run_forward(): pl.pallas_call(forward_kernel, name='forward_layers', out_shape=[shape((2...]
    pallas_call x3, Pallas kernels: 327 us -> 316 us  [call(): pl.pallas_call(kernel, name=name, out_shape=[jax.ShapeDtypeStruct(shape,...]
where the time goes in v4:
time: 528 us; the launch traced here: 519 us
  Pallas kernels  502 us (95%)
  local copies, waits for them, and re-layouts  8.01 us (2%)
  other arithmetic  8 us (2%)
    pallas_call x3, Pallas kernels, call(): pl.pallas_call(kernel, name=name, out_shape=[jax.ShapeDtypeStruct(shape,...  316 us
    pallas_call x1, Pallas kernels, run_forward(): pl.pallas_call(forward_kernel, name='forward_layers', out_shape=[shape((2...  173 us
    pallas_call x1, Pallas kernels, run_results(): pl.pallas_call(results_kernel, name='place_results', out_shape=[big, big,...  12.2 us

profile of v4, /device:TPU:0, one launch (start us, length us, event | category | flops | bytes accessed | tf_op | source)
XLA Modules:
  0.0 519.0 jit_solution(18216245509487583472)
XLA Ops:
  0.6 1.2 slice_bitcast_fusion.5
  1.8 0.0 copy-start.3
  1.9 1.2 maximum_bitcast_fusion.2
  3.0 0.0 copy-start.4
  3.0 1.1 pad_maximum_fusion.own_a
  4.2 0.0 copy-done.3
  4.2 0.7 copy.23
  4.9 0.0 copy-done.4
  4.9 0.6 copy.21
  5.6 0.7 copy.22
  6.3 0.0 copy-start.5
  6.3 0.0 copy-start.6
  6.3 0.0 copy-start.7
  6.3 0.0 copy-start.8
  6.3 1.7 maximum_bitcast_fusion.own_b
  8.0 0.1 pad.9.clone
  8.1 0.0 copy-done.5
  8.1 0.0 copy-done.8
  8.1 0.1 maximum_bitcast_fusion.4
  8.2 0.6 pad_maximum_fusion.1.own_c
  8.8 1.8 fusion
  10.7 173.3 %forward_layers.1 = (bf16[2,2,2,768,768]{4,3,2,1,0:T(8,128)(2,1)}, bf16[2,2,8,768,384]{4,3,2,1,0:T(8,128)(2,1)}, f32[2,8,768]{2,1,0:T(8,128)}, bf16[512,768]{1,0...) custom-call(bf16[8,512,768]{2,1,0:T(8,128)(2,1)} %bitcast.74, ...), custom_call_target="tpu_custom_call" | custom-call | flops 30000001024 | bytes 80000000 | tf_op jit(solution)/shard_map/forward_layers/pallas_call | solution.py:1091
  183.9 93.8 %backward_second.1 = (bf16[2,2,768,768]{3,2,1,0:T(8,128)(2,1)}, bf16[512,768]{1,0:T(8,128)(2,1)}, f32[8,768]{1,0:T(8,128)}, bf16[2,4,512,768]{3,2,1,0:T(8,128)(2,1)}, bf16[2,768,384]{2,1,0:T(8,128)(2,1)}) custom-call(bf16[2,2,2,768,768]{4,3,2,1,0:T(8,128)(2,1)} %get-tuple-element.46.refs_0_, bf16[2,2,8,768,384]{4,3,2,1,0:T(8,128)(2,1)} %get-tuple-element.47.refs_1_, ...), custom_call_target="tpu_custom_call" | custom-call | flops 40000000000 | bytes 80000000 | tf_op jit(solution)/shard_map/backward_second/pallas_call | solution.py:2102
  277.8 120.0 %backward_first.1 = (bf16[2,2,768,768]{3,2,1,0:T(8,128)(2,1)}, bf16[512,768]{1,0:T(8,128)(2,1)}, f32[8,768]{1,0:T(8,128)}, bf16[2,4,512,768]{3,2,1,0:T(8,128)(2,...) custom-call(bf16[2,2,2,768,768]{4,3,2,1,0:T(8,128)(2,1)} %get-tuple-element.46.refs_0_,, ...), custom_call_target="tpu_custom_call" | custom-call | flops 40000000000 | bytes 80000000 | tf_op jit(solution)/shard_map/backward_first/pallas_call | solution.py:2102
  397.8 102.6 %sum_and_spread.1 = (bf16[2,4,512,768]{3,2,1,0:T(8,128)(2,1)}, bf16[2,2,192,768]{3,2,1,0:T(8,128)(2,1)}, bf16[2,768,768]{2,1,0:T(8,128)(2,1)}, f32[2,8,768]{2,1,0:T(8,128)}) custom-call(bf16[2,2,4,192,768]{4,3,2,1,0:T(8,128)(2,1)} %bitcast.82, bf16[2,768,384]{2,1,0:T(8,128)(2,1)} %get-tuple-element.64.refs_1_, ...), custom_call_target="tpu_custom_call" | custom-call | flops 100000000 | bytes 40000000 | tf_op jit(solution)/shard_map/sum_and_spread/pallas_call | solution.py:2102
  500.4 1.3 copy-done
  501.7 1.7 copy-done.2
  503.3 12.2 %place_results.1 = (bf16[2,4,512,768]{3,2,1,0:T(8,128)(2,1)}, bf16[2,4,512,768]{3,2,1,0:T(8,128)(2,1)}, f32[192,768]{1,0:T(8,128)}, f32[768,768]{1,0:T(8,128)}, f32[768,768]{1,0:T(8,128)}) custom-call(bf16[2,4,512,768]{3,2,1,0:T(8,128)(2,1)} %get-tuple-element.45.refs_0_, bf16[2,4,512,768]{3,2,1,0:T(8,128)(2,1)} %get-tuple-element.59.refs_1_, ...), custom_call_target="tpu_custom_call" | custom-call | flops 1000000 | bytes 35000000 | tf_op jit(solution)/shard_map/place_results/pallas_call | solution.py:2178
  515.6 1.5 dynamic-slice_bitcast_fusion
  517.1 0.2 convert_element_type.19
  517.3 0.1 slice_bitcast_fusion.2
  517.5 1.3 maximum_bitcast_fusion.1
  (9 shorter events, 0.0 us)
Async XLA Ops:
  1.8 2.3 copy-start.3
  3.0 1.9 copy-start.4
  6.3 1.8 copy-start.5
  6.3 1.8 copy-start.6
  6.3 1.8 copy-start.7
  6.3 1.8 copy-start.8
  500.4 1.3 copy-start
  501.7 1.7 copy-start.2
  503.3 13.8 %copy-start.1 = (bf16[2,2,192,768]{3,2,1,0:T(8,128)(2,1)S(1)}, bf16[2,2,192,768]{3,2,1,0:T(8,128)(2,1)}, u32[]{:S(2)}) copy-start(bf16[2,2,192,768]{3,2,1,0:T(8,128)(2,1)} %get-tuple-element.72.refs_4_) | copy-start | bytes 3538948

commit v5 on v2

--- a/solution.py
+++ b/solution.py
@@ -2029,61 +2029,61 @@
 
     back.take()
     sums[0].start()
-    back.swap()
-    sums[1].start()
     for load in loads:
         load.start()
+    back.swap()
     tiny_start(0)
+    sums[1].start()
     back.hops(0)
-    lines[0].resume(loads[0])
+    for line, load in zip(lines, loads):
+        line.resume(load)
     sums[0].load()
     sums[2].start()
-    back.forward(0)
+    sums[1].load()
+    sums[3].start()
     tiny_end(0)
     tiny_start(1)
-    lines[1].resume(loads[1])
-    sums[1].load()
-    sums[3].start()
+    back.forward(0)
+    sums[2].load()
+    done_start()
+    lines[0].line_one()
     sums[0].middle()
-    lines[0].line_one()
+    sums[3].load()
+    lines[1].line_one()
+    sums[1].middle()
+    lines[0].line_two()
     tiny_end(1)
     tiny_start(2)
-    sums[2].load()
     sums[0].gather()
-    back.finish(0)
-    sums[1].middle()
+    sums[2].middle()
+    lines[1].line_two()
+    sums[1].gather()
+    sums[3].middle()
     back.hops(1)
-    sums[1].gather()
+    lines[0].finish(0, halves[0])
+    sums[0].line_one()
+    sums[2].gather()
+    sums[1].line_one()
     tiny_end(2)
     tiny_start(3)
-    sums[3].load()
-    sums[2].middle()
-    lines[1].line_one()
-    done_start()
-    lines[0].line_two()
-    sums[2].gather()
+    lines[1].finish(0, halves[1])
+    back.finish(0)
+    sums[3].gather()
+    sums[0].line_two()
+    sums[2].line_one()
+    sums[1].line_two()
     back.forward(1)
-    sums[3].middle()
-    sums[0].line_one()
+    sums[3].line_one()
     tiny_end(3)
     tiny_start(4)
-    sums[3].gather()
-    sums[1].line_one()
-    back.finish(1)
-    lines[1].line_two()
-    lines[0].finish(0, halves[0])
-    sums[2].line_one()
-    sums[0].line_two()
-    tiny_end(4)
-    sums[3].line_one()
-    sums[1].line_two()
     sums[0].finish(1, targets[0])
     sums[2].line_two()
-    lines[1].finish(0, halves[1])
     sums[1].finish(1, targets[1])
     sums[3].line_two()
+    back.finish(1)
     sums[2].finish(0, targets[2])
     sums[3].finish(0, targets[3])
+    tiny_end(4)
     for item, layer, target in zip(sums, layers, targets):
         item.drain_plane()
         item.drain_line()

time: 518 us -> 502 us (0.969)
  Pallas kernels: 494 us -> 478 us
    pallas_call x3, Pallas kernels: 327 us -> 311 us  [call(): pl.pallas_call(kernel, name=name, out_shape=[jax.ShapeDtypeStruct(shape,...]
where the time goes in v5:
time: 502 us; the launch traced here: 494 us
  Pallas kernels  478 us (95%)
  other arithmetic  8.22 us (2%)
  local copies, waits for them, and re-layouts  6.37 us (1%)
    pallas_call x3, Pallas kernels, call(): pl.pallas_call(kernel, name=name, out_shape=[jax.ShapeDtypeStruct(shape,...  311 us
    pallas_call x1, Pallas kernels, run_forward(): pl.pallas_call(forward_kernel, name='forward_layers', out_shape=[shape((2...  155 us
    pallas_call x1, Pallas kernels, run_results(): pl.pallas_call(results_kernel, name='place_results', out_shape=[big, big,...  12.2 us

profile of v5, /device:TPU:0, one launch (start us, length us, event | category | flops | bytes accessed | tf_op | source)
XLA Modules:
  0.0 493.9 jit_solution(10990913523642627203)
XLA Ops:
  0.6 0.0 copy-start.4
  0.7 1.8 fusion
  2.5 1.2 slice_bitcast_fusion.5
  3.7 0.0 copy-done.4
  3.7 0.0 copy-start.5
  3.7 0.0 copy-start.6
  3.8 0.0 copy-start.7
  3.8 0.0 copy-start.8
  3.8 0.0 copy-start.2
  3.8 0.1 maximum_bitcast_fusion.2
  3.9 1.1 pad_maximum_fusion.own_a
  5.0 0.1 pad.9.clone
  5.1 0.0 copy-done.5
  5.1 0.0 copy-done.8
  5.1 0.1 maximum_bitcast_fusion.4
  5.2 0.6 pad_maximum_fusion.1.own_c
  5.8 0.6 copy.21
  6.5 0.7 copy.22
  7.2 0.0 copy-done.3
  7.2 0.7 copy.23
  8.0 1.7 maximum_bitcast_fusion.own_b
  9.6 154.7 %forward_layers.1 = (bf16[2,2,2,768,768]{4,3,2,1,0:T(8,128)(2,1)}, bf16[2,2,8,768,384]{4,3,2,1,0:T(8,128)(2,1)}, f32[2,8,768]{2,1,0:T(8,128)}, bf16[512,768]{1,0...) custom-call(bf16[8,512,768]{2,1,0:T(8,128)(2,1)} %bitcast.74, ...), custom_call_target="tpu_custom_call" | custom-call | flops 30000001024 | bytes 80000000 | tf_op jit(solution)/shard_map/forward_layers/pallas_call | solution.py:949
  164.3 100.1 %backward_second.1 = (bf16[2,2,768,768]{3,2,1,0:T(8,128)(2,1)}, bf16[512,768]{1,0:T(8,128)(2,1)}, f32[8,768]{1,0:T(8,128)}, bf16[2,4,512,768]{3,2,1,0:T(8,128)(2...) custom-call(bf16[2,2,2,768,768]{4,3,2,1,0:T(8,128)(2,1)} %get-tuple-element.44.refs_0_, ...), custom_call_target="tpu_custom_call" | custom-call | flops 40000000000 | bytes 80000000 | tf_op jit(solution)/shard_map/backward_second/pallas_call | solution.py:2101
  264.4 110.4 %backward_first.1 = (bf16[2,2,768,768]{3,2,1,0:T(8,128)(2,1)}, bf16[512,768]{1,0:T(8,128)(2,1)}, f32[8,768]{1,0:T(8,128)}, bf16[2,4,512,768]{3,2,1,0:T(8,128)(2,...) custom-call(bf16[2,2,2,768,768]{4,3,2,1,0:T(8,128)(2,1)} %get-tuple-element.44.refs_0_, ...), custom_call_target="tpu_custom_call" | custom-call | flops 40000000000 | bytes 80000000 | tf_op jit(solution)/shard_map/backward_first/pallas_call | solution.py:2101
  374.8 100.8 %sum_and_spread.1 = (bf16[2,4,512,768]{3,2,1,0:T(8,128)(2,1)}, bf16[2,2,192,768]{3,2,1,0:T(8,128)(2,1)}, bf16[2,768,768]{2,1,0:T(8,128)(2,1)}, f32[2,8,768]{2,1,0:T(8,128)}) custom-call(bf16[2,2,4,192,768]{4,3,2,1,0:T(8,128)(2,1)} %bitcast.82, bf16[2,2,4,192,768]{4,3,2,1,0:T(8,128)(2,1)} %bitcast.83, bf16[2,768,384]{2,1,0:T(8,128)(2,1)} %get-tuple-element.63.refs_2_, ...), custom_call_target="tpu_custom_call" | custom-call | flops 100000000 | bytes 40000000 | tf_op jit(solution)/shard_map/sum_and_spread/pallas_call | solution.py:2101
  475.7 1.5 convert_element_type.19
  477.1 0.1 slice_bitcast_fusion.2
  477.3 1.3 maximum_bitcast_fusion.1
  478.6 0.4 copy-done
  479.0 0.9 copy-done.1
  479.9 12.2 %place_results.1 = (bf16[2,4,512,768]{3,2,1,0:T(8,128)(2,1)}, bf16[2,4,512,768]{3,2,1,0:T(8,128)(2,1)}, f32[192,768]{1,0:T(8,128)}, f32[768,768]{1,0:T(8,128)}, f32[768,768]{1,0:T(8,128)}) custom-call(bf16[2,4,512,768]{3,2,1,0:T(8,128)(2,1)} %get-tuple-element.57.refs_0_, bf16[2,4,512,768]{3,2,1,0:T(8,128)(2,1)} %get-tuple-element.68.refs_1_, ...), custom_call_target="tpu_custom_call" | custom-call | flops 1000000 | bytes 35000000 | tf_op jit(solution)/shard_map/place_results/pallas_call | solution.py:2183
  492.2 1.5 dynamic-slice_bitcast_fusion
  (9 shorter events, 0.0 us)
Async XLA Ops:
  0.6 3.1 copy-start.4
  3.7 1.4 copy-start.5
  3.7 1.4 copy-start.6
  3.8 1.4 copy-start.7
  3.8 1.3 copy-start.8
  3.8 2.0 copy-start.2
  5.8 1.4 copy-start.3
  477.2 1.8 copy-start
  477.3 2.7 copy-start.1
